TPU v7x, 128 devices: a whole 4x4x4 slice. The times are simulated.
128 devices in a mesh: erow: 8 (over z, core), ecol: 16 (over x, y).
Axes of the slice: x: 4, y: 4, z: 4, core: 2. Of those that a mesh axis runs over, the one named last changes fastest.
Arguments:
- hidden_in: bfloat16 [512, 4, 2304], P(('erow', 'ecol')), may hold values from -6 to 6
- kda_state: float32 [512, 16, 128, 128], P('erow', 'ecol'), may hold values from -0.6 to 0.6
- query_weight: bfloat16 [2304, 2048], P(None, 'ecol'), may hold values from -0.125 to 0.125
- key_weight: bfloat16 [2304, 2048], P(None, 'ecol'), may hold values from -0.125 to 0.125
- value_weight: bfloat16 [2304, 2048], P(None, 'ecol'), may hold values from -0.125 to 0.125
- beta_weight: bfloat16 [2304, 16], P(None, 'ecol'), may hold values from -0.125 to 0.125
- decay_down: bfloat16 [2304, 128], replicated, may hold values from -0.125 to 0.125
- decay_up: bfloat16 [128, 2048], P(None, 'ecol'), may hold values from -0.5 to 0.5
- decay_log: float32 [16], P('ecol'), may hold values from -2.5 to 1
- decay_bias: float32 [2048], P('ecol'), may hold values from -4 to 4
- gate_down: bfloat16 [2304, 128], replicated, may hold values from -0.125 to 0.125
- gate_lift: bfloat16 [128, 2048], P(None, 'ecol'), may hold values from -0.5 to 0.5
- norm_gain: float32 [128], replicated, may hold values from 0.1 to 1.9
- output_weight: bfloat16 [2048, 2304], P('ecol'), may hold values from -0.125 to 0.125
- ffn_gain: float32 [2304], replicated, may hold values from 0.1 to 1.9
- expert_ids: int32 [512, 4, 8], P(('erow', 'ecol')), may hold values from 0 to 127, as said below
- route_weight: float32 [512, 4, 8], P(('erow', 'ecol')), may hold values from 0.05 to 0.6
- expert_gate: bfloat16 [128, 2304, 1024], P(('erow', 'ecol')), may hold values from -0.125 to 0.125
- expert_up: bfloat16 [128, 2304, 1024], P(('erow', 'ecol')), may hold values from -0.125 to 0.125
- expert_down: bfloat16 [128, 1024, 2304], P(('erow', 'ecol')), may hold values from -0.1875 to 0.1875
Outputs:
- mixed: bfloat16 [512, 4, 2304], P(('erow', 'ecol'))
- new_state: float32 [512, 16, 128, 128], P('erow', 'ecol')
Inputs may be any that keep to these rules, and one draw needn't show every extreme that they name: `expert_ids`: each token names 8 different experts. Among the 16 tokens of one device no expert is named more than 2 times, and one and the same expert is named exactly 2 times on every device.
All inputs are finite; a program needn't handle non-finite values.
Results may differ from a plain program's by a relative error of at most 0.02.
Values may be sent and summed in bfloat16 or wider, within the bound.
No kernel may reach another device: no remote copies, remote signals or barrier semaphores. Data moves between devices by JAX's collectives and lax.ppermute only.
A program may use at most 128 MiB of HBM per device.

v0:
```python
import jax
import jax.numpy as jnp
from jax import lax
from jax.sharding import PartitionSpec as P

EPSILON = 1e-06
HIGHEST = lax.Precision.HIGHEST


def unit_rows(vectors):
    return vectors * lax.rsqrt(jnp.sum(vectors * vectors, -1, keepdims=True) + EPSILON)


def rms_scale(vectors):
    return vectors * lax.rsqrt(jnp.mean(vectors * vectors, -1, keepdims=True) + EPSILON)


def project(
    tokens,
    query_weight,
    key_weight,
    value_weight,
    beta_weight,
    decay_down,
    decay_up,
    decay_log,
    decay_bias,
    gate_down,
    gate_lift,
    head_size,
):
    row_total = tokens.shape[0]
    head_count = query_weight.shape[1] // head_size
    shape = (row_total, head_count, head_size)
    queries = unit_rows(
        jnp.dot(tokens, query_weight, preferred_element_type=jnp.float32).reshape(shape)
    ) * head_size ** (-0.5)
    key_rows = unit_rows(
        jnp.dot(tokens, key_weight, preferred_element_type=jnp.float32).reshape(shape)
    )
    values = jnp.dot(tokens, value_weight, preferred_element_type=jnp.float32).reshape(shape)
    write_rate = jax.nn.sigmoid(jnp.dot(tokens, beta_weight, preferred_element_type=jnp.float32))
    decay_low = jnp.dot(tokens, decay_down, preferred_element_type=jnp.float32).astype(jnp.bfloat16)
    decay_pre = jnp.dot(decay_low, decay_up, preferred_element_type=jnp.float32) + decay_bias
    log_decay = -jnp.exp(jnp.repeat(decay_log, head_size)) * jax.nn.softplus(decay_pre)
    factor = jnp.exp(log_decay).reshape(shape)
    gate_low = jnp.dot(tokens, gate_down, preferred_element_type=jnp.float32).astype(jnp.bfloat16)
    out_gate = jax.nn.sigmoid(
        jnp.dot(gate_low, gate_lift, preferred_element_type=jnp.float32)
    ).reshape(shape)
    return (queries, key_rows, values, factor, write_rate, out_gate)


def delta_head(memory, queries, key_rows, values, factor, write_rate):
    outputs = []
    for position in range(queries.shape[1]):
        memory = memory * factor[:, position, :, None]
        predicted = jnp.einsum("rkv,rk->rv", memory, key_rows[:, position], precision=HIGHEST)
        update = (
            write_rate[:, position, None, None]
            * key_rows[:, position, :, None]
            * (values[:, position] - predicted)[:, None, :]
        )
        memory = memory + update
        outputs.append(jnp.einsum("rkv,rk->rv", memory, queries[:, position], precision=HIGHEST))
    return (memory, jnp.stack(outputs, 1))


def local(
    hidden_in,
    kda_state,
    query_weight,
    key_weight,
    value_weight,
    beta_weight,
    decay_down,
    decay_up,
    decay_log,
    decay_bias,
    gate_down,
    gate_lift,
    norm_gain,
    output_weight,
    ffn_gain,
    expert_ids,
    route_weight,
    expert_gate,
    expert_up,
    expert_down,
):
    local_req, step_count, model_width = hidden_in.shape
    head_size = kda_state.shape[-1]
    gathered = lax.all_gather(hidden_in, "ecol", axis=0, tiled=True)
    group_req = gathered.shape[0]
    parts = project(
        gathered.reshape(group_req * step_count, model_width),
        query_weight,
        key_weight,
        value_weight,
        beta_weight,
        decay_down,
        decay_up,
        decay_log,
        decay_bias,
        gate_down,
        gate_lift,
        head_size,
    )
    queries, key_rows, values, factor, write_rate, out_gate = [
        piece.reshape((group_req, step_count) + piece.shape[1:]) for piece in parts
    ]
    new_state, head_out = jax.vmap(delta_head, in_axes=(1, 2, 2, 2, 2, 2), out_axes=(1, 2))(
        kda_state, queries, key_rows, values, factor, write_rate
    )
    mixed_heads = (
        (rms_scale(head_out) * norm_gain * out_gate)
        .astype(jnp.bfloat16)
        .reshape(group_req * step_count, -1)
    )
    own_rows = local_req * step_count
    attended = lax.psum_scatter(
        jnp.dot(mixed_heads, output_weight, preferred_element_type=jnp.float32).astype(
            jnp.bfloat16
        ),
        "ecol",
        scatter_dimension=0,
        tiled=True,
    ).astype(jnp.float32)
    residual = (hidden_in.reshape(own_rows, model_width).astype(jnp.float32) + attended).astype(
        jnp.bfloat16
    )
    normed = (rms_scale(residual.astype(jnp.float32)) * ffn_gain).astype(jnp.bfloat16)
    grid_rows = lax.axis_size("erow")
    grid_cols = lax.axis_size("ecol")
    device_count = grid_rows * grid_cols
    pick_count = expert_ids.shape[-1]
    capacity = max(2, 2 * own_rows * pick_count // device_count)
    slots_total = device_count * capacity
    flat_ids = expert_ids.reshape(-1)
    flat_weights = route_weight.reshape(-1)
    serial = jnp.arange(flat_ids.shape[0], dtype=jnp.int32)
    earlier = (flat_ids[:, None] == flat_ids[None, :]) & (serial[None, :] < serial[:, None])
    slot_of = flat_ids * capacity + jnp.sum(earlier.astype(jnp.int32), 1)
    matches = (slot_of[:, None] == jnp.arange(slots_total, dtype=jnp.int32)[None, :]).reshape(
        own_rows, pick_count, slots_total
    )
    placing = jnp.any(matches, 1).astype(jnp.bfloat16)
    combine = jnp.sum(jnp.where(matches, flat_weights.reshape(own_rows, pick_count, 1), 0.0), 1)
    outgoing = lax.dot_general(
        placing, normed, (((0,), (0,)), ((), ())), preferred_element_type=jnp.float32
    ).astype(jnp.bfloat16)
    received = lax.all_to_all(
        outgoing.reshape(device_count, capacity, model_width),
        ("erow", "ecol"),
        split_axis=0,
        concat_axis=0,
        tiled=True,
    )
    flat_rows = received.reshape(-1, model_width)
    gate_act = jnp.dot(flat_rows, expert_gate[0], preferred_element_type=jnp.float32)
    up_act = jnp.dot(flat_rows, expert_up[0], preferred_element_type=jnp.float32)
    hidden = (jax.nn.silu(gate_act) * up_act).astype(jnp.bfloat16)
    produced = jnp.dot(hidden, expert_down[0], preferred_element_type=jnp.float32).astype(
        jnp.bfloat16
    )
    returned = lax.all_to_all(
        produced.reshape(received.shape), ("erow", "ecol"), split_axis=0, concat_axis=0, tiled=True
    )
    returned = returned.reshape(slots_total, model_width)
    routed = jnp.dot(combine, returned.astype(jnp.float32), precision=HIGHEST)
    mixed = (
        (residual.astype(jnp.float32) + routed)
        .astype(jnp.bfloat16)
        .reshape(local_req, step_count, model_width)
    )
    return (mixed, new_state)


def solution(mesh):
    return jax.shard_map(
        local,
        mesh=mesh,
        in_specs=(
            P(("erow", "ecol"), None, None),
            P("erow", "ecol", None, None),
            P(None, "ecol"),
            P(None, "ecol"),
            P(None, "ecol"),
            P(None, "ecol"),
            P(),
            P(None, "ecol"),
            P("ecol"),
            P("ecol"),
            P(),
            P(None, "ecol"),
            P(),
            P("ecol", None),
            P(),
            P(("erow", "ecol"), None, None),
            P(("erow", "ecol"), None, None),
            P(("erow", "ecol"), None, None),
            P(("erow", "ecol"), None, None),
            P(("erow", "ecol"), None, None),
        ),
        out_specs=(P(("erow", "ecol"), None, None), P("erow", "ecol", None, None)),
        check_vma=False,
    )
```

profile of v0, /device:TPU:0, one launch (start us, length us, event | category | flops | bytes accessed | tf_op | source)
XLA Modules:
  0.0 294.2 jit_solution(13587256624977357636)
XLA Ops:
  7.2 0.0 copy-start
  7.2 0.0 all-gather.2.cloned.1.call-start
  7.2 0.7 all-gather.2.cloned.1.call-update
  7.9 0.0 reduce-scatter.2.cloned.1.call-start
  8.7 47.0 %all-gather.2.cloned.1.call-done = bf16[64,4,2304]{2,1,0:T(4,128)(2,1)} async-done(((bf16[4,4,2304]{2,1,0:T(4,128)(2,1)}), bf16[64,4,2304]{2,1,0:T(4,128)(2,1)}) %all-gather.2.cloned.1.call-update) | async-done | bytes 1179664 | tf_op jit(solution)/shard_map/all_gather | solution.py:93
  55.7 2.4 reshape.398
  58.1 1.1 fusion.95
  59.1 0.2 reshape.400
  59.3 0.2 slice_reduce_fusion
  59.6 1.7 fusion.74
  61.3 0.0 copy-start.1
  61.3 0.1 fusion.94
  61.4 0.0 copy-done.3
  61.4 0.0 copy-start.2
  61.4 0.0 copy-start.9
  61.4 0.5 multiply_reduce_fusion.1
  62.0 0.5 multiply_reduce_fusion.2
  62.5 0.1 broadcast_multiply_fusion
  62.7 0.1 fusion.93
  62.8 0.7 copy-done.1
  63.5 4.0 %fusion.9 = f32[64,1,128]{2,1,0:T(1,128)S(1)} fusion(f32[64,1,128,128]{3,2,1,0:T(8,128)S(1)} %copy-done.1, f32[64,128]{1,0:T(8,128)S(1)} %bitcast.184, f32[64,4,1,128]{3,1,0,2:T(4,128)S(1)} %bitcast.180), kind=kOutput, calls=%fused_computation.14 | convolution fusion | flops 13631488 | bytes 4292608 | tf_op jit(solution)/shard_map/vmap(rkv,rk->rv)/dot_general | solution.py:58
  67.5 0.5 fusion.53
  68.0 0.1 broadcast_multiply_fusion.3
  68.0 7.5 %fusion.15 = f32[64,1,128]{2,1,0:T(1,128)S(1)} fusion(f32[64,1,128,128]{3,2,1,0:T(8,128)S(1)} %copy-done.1, f32[64,128]{1,0:T(8,128)S(1)} %bitcast.206, f32[64,128]{1,0:T(8,128)S(1)} %fusion.83, f32[64,128]{1,0:T(8,128)S(1)} %get-tuple-element.25, f32[64,128]{1,0:T(8,128)S(1)} %bitcast.185, f32[64,4,1,128]{3,1,0,2:T(4,128)S(1)} %bitcast.181), kind=kOutput, calls=%fused_computation.20 | convolution fusion | flops 16777216 | bytes 4390912 | tf_op jit(solution)/shard_map/vmap(rkv,rk->rv)/dot_general | solution.py:58
  75.5 0.1 multiply_multiply_fusion
  75.6 5.6 %fusion.62 = f32[1,64,1,128]{3,2,1,0:T(1,128)S(1)} fusion(f32[64,1,128,128]{3,2,1,0:T(8,128)S(1)} %copy-done.1, f32[64,128]{1,0:T(8,128)S(1)} %fusion.83, f32[64,128]{1,0:T(8,128)S(1)} %get-tuple-element.25, f32[64,128]{1,0:T(8,128)S(1)} %bitcast.186, f32[64,4,1,128]{3,1,0,2:T(4,128)S(1)} %bitcast.193), kind=kOutput, calls=%fused_computation.66 | convolution fusion | flops 15728640 | bytes 4358144 | tf_op jit(solution)/shard_map/vmap(rkv,rk->rv)/dot_general | solution.py:65
  81.3 8.5 %convolution_bitcast_fusion = f32[1,64,1,128]{3,2,1,0:T(1,128)S(1)} fusion(f32[64,4,1,128]{3,1,0,2:T(4,128)S(1)} %bitcast.194, f32[64,1,128,128]{3,2,1,0:T(8,128)S(1)} %copy-done.1, f32[64,128]{1,0:T(8,128)S(1)} %fusion.82, f32[64,128]{1,0:T(8,128)S(1)} %get-tuple-element.24, f32[64,128]{1,0:T(8,128)S(1)} %bitcast.207, f32[64,128]{1,0:T(8,128)S(1)} %fusion.83, ...), kind=kOutput, calls=%fused_computation.68 | convolution fusion | flops 18874368 | bytes 4456448 | tf_op jit(solution)/shard_map/vmap(rkv,rk->rv)/dot_general | solution.py:65
  89.8 11.3 %fusion.13 = f32[64,1,128]{2,1,0:T(1,128)S(1)} fusion(f32[64,128]{1,0:T(8,128)S(1)} %bitcast.201, f32[64,4,1,128]{3,1,0,2:T(4,128)S(1)} %bitcast.182, f32[64,1,128,128]{3,2,1,0:T(8,128)S(1)} %copy-done.1, f32[64,128]{1,0:T(8,128)S(1)} %fusion.82, f32[64,128]{1,0:T(8,128)S(1)} %get-tuple-element.24, f32[64,128]{1,0:T(8,128)S(1)} %bitcast.208, ...), kind=kOutput, calls=%fused_computation.18 | convolution fusion | flops 19922944 | bytes 4489216 | tf_op jit(solution)/shard_map/vmap(rkv,rk->rv)/dot_general | solution.py:58
  101.1 0.1 broadcast_multiply_fusion.1
  101.2 12.4 %fusion.61 = f32[1,64,1,128]{3,2,1,0:T(1,128)S(1)} fusion(f32[64,128]{1,0:T(8,128)S(1)} %fusion.81, f32[64,128]{1,0:T(8,128)S(1)} %get-tuple-element.23, f32[64,128]{1,0:T(8,128)S(1)} %bitcast.202, f32[64,4,1,128]{3,1,0,2:T(4,128)S(1)} %bitcast.195, f32[64,1,128,128]{3,2,1,0:T(8,128)S(1)} %copy-done.1, f32[64,128]{1,0:T(8,128)S(1)} %fusion.82, ...), kind=kOutput, calls=%fused_computation.65 | convolution fusion | flops 22020096 | bytes 4554752 | tf_op jit(solution)/shard_map/vmap(rkv,rk->rv)/dot_general | solution.py:65
  113.5 13.4 %fusion.11 = f32[64,1,128]{2,1,0:T(1,128)S(1)} fusion(f32[64,128]{1,0:T(8,128)S(1)} %bitcast.198, f32[64,128]{1,0:T(8,128)S(1)} %fusion.81, f32[64,128]{1,0:T(8,128)S(1)} %get-tuple-element.23, f32[64,128]{1,0:T(8,128)S(1)} %bitcast.203, f32[64,4,1,128]{3,1,0,2:T(4,128)S(1)} %bitcast.183, f32[64,1,128,128]{3,2,1,0:T(8,128)S(1)} %copy-done.1, ...), kind=kOutput, calls=%fused_computation.16 | convolution fusion | flops 23068672 | bytes 4587520 | tf_op jit(solution)/shard_map/vmap(rkv,rk->rv)/dot_general | solution.py:58
  127.0 0.0 copy-start.10
  127.0 0.0 copy-start.11
  127.0 0.0 copy-start.12
  127.0 14.7 %fusion.63 = f32[1,64,1,128]{3,2,1,0:T(1,128)S(1)} fusion(f32[64,128]{1,0:T(8,128)S(1)} %fusion.80, f32[64,128]{1,0:T(8,128)S(1)} %get-tuple-element.22, f32[64,128]{1,0:T(8,128)S(1)} %bitcast.199, f32[64,128]{1,0:T(8,128)S(1)} %fusion.81, f32[64,128]{1,0:T(8,128)S(1)} %get-tuple-element.23, f32[64,128]{1,0:T(8,128)S(1)} %bitcast.204, ...), kind=kOutput, calls=%fused_computation.67 | convolution fusion | flops 25165824 | bytes 4653056 | tf_op jit(solution)/shard_map/vmap(rkv,rk->rv)/dot_general | solution.py:65
  141.8 0.0 copy-start.5
  141.8 0.0 copy-start.6
  141.8 0.0 copy-start.7
  141.8 0.2 multiply_reduce_fusion
  142.0 0.1 rsqrt.38
  142.2 0.6 fusion.60
  142.8 1.5 convolution_convert_fusion
  144.3 0.0 reduce-scatter.2.cloned.1.call-update
  144.4 0.1 eq.29
  144.4 0.2 convert_reduce_fusion
  144.6 0.1 reduce_sum.60
  144.7 0.1 fusion.75
  144.9 72.1 %reduce-scatter.2.cloned.1.call-done = bf16[16,2304]{1,0:T(8,128)(2,1)} async-done(((bf16[256,2304]{1,0:T(8,128)(2,1)}), bf16[16,2304]{1,0:T(8,128)(2,1)}) %reduce-scatter.2.cloned.1.call-update) | async-done | bytes 73744 | tf_op jit(solution)/shard_map/reduce_scatter | solution.py:121
  217.0 1.0 fusion.70
  218.0 0.5 convolution_convert_fusion.1
  218.6 0.5 reshape.407
  219.1 28.2 %all_to_all.10 = bf16[128,2,2304]{2,1,0:T(2,128)(2,1)S(1)} all-to-all(bf16[128,2,2304]{2,1,0:T(2,128)(2,1)S(1)} %reshape.407), channel_id=1, replica_groups=mesh['erow'=8,'ecol'=16] {'erow','ecol'}, dimensions={0} | all-to-all | bytes 2359296 | tf_op jit(solution)/shard_map/all_to_all | solution.py:152
  247.3 0.5 reshape.408
  247.8 4.7 %fusion.4 = f32[256,1024]{1,0:T(8,128)} fusion(bf16[256,2304]{1,0:T(8,128)(2,1)S(1)} %reshape.408, bf16[1,2304,1024]{2,1,0:T(8,128)(2,1)} %param.37), kind=kOutput, calls=%fused_computation.4 | convolution fusion | flops 1207959552 | bytes 6946816 | tf_op jit(solution)/shard_map/dot_general | solution.py:160
  252.5 6.8 %fusion.17 = bf16[256,2304]{1,0:T(8,128)(2,1)S(1)} fusion(bf16[1,1024,2304]{2,1,0:T(8,128)(2,1)} %param.39, bf16[256,2304]{1,0:T(8,128)(2,1)S(1)} %reshape.408, bf16[1,2304,1024]{2,1,0:T(8,128)(2,1)} %param.38, f32[256,1024]{1,0:T(8,128)} %fusion.4), kind=kOutput, calls=%fused_computation.24 | convolution fusion | flops 2418081792 | bytes 12845056 | tf_op jit(solution)/shard_map/dot_general | solution.py:163
  259.3 0.0 copy-start.8
  259.3 1.3 reshape.409
  260.6 4.6 %all-to-all-start.1 = ((bf16[128,2,2304]{2,1,0:T(2,128)(2,1)}), bf16[128,2,2304]{2,1,0:T(2,128)(2,1)S(1)}, u32[]{:S(2)}, u32[]{:S(2)}) async-start(bf16[128,2,2304]{2,1,0:T(2,128)(2,1)} %reshape.409), calls=%async_computation.2 | async-start | bytes 2359296 | tf_op jit(solution)/shard_map/all_to_all | solution.py:166
  265.2 0.1 select_reduce_fusion
  265.4 12.0 %multiply_add_fusion = f32[64,1,128,128]{3,2,1,0:T(8,128)} fusion(f32[64,1,128,128]{3,2,1,0:T(8,128)} %param.21, f32[64,128]{1,0:T(8,128)S(1)} %fusion.80, f32[64,128]{1,0:T(8,128)S(1)} %get-tuple-element.22, f32[64,128]{1,0:T(8,128)S(1)} %bitcast.200, f32[64,128]{1,0:T(8,128)S(1)} %fusion.81, f32[64,128]{1,0:T(8,128)S(1)} %get-tuple-element.23, ...), kind=kLoop, calls=%fused_computation.7 | loop fusion | flops 12582912 | bytes 8781824 | tf_op jit(solution)/shard_map/vmap()/add | solution.py:64
  277.4 8.3 %all-to-all-done.1 = bf16[128,2,2304]{2,1,0:T(2,128)(2,1)S(1)} async-done(((bf16[128,2,2304]{2,1,0:T(2,128)(2,1)}), bf16[128,2,2304]{2,1,0:T(2,128)(2,1)S(1)}, u32[]{:S(2)}, u32[]{:S(2)}) %all-to-all-start.1) | async-done | bytes 1179680 | tf_op jit(solution)/shard_map/all_to_all | solution.py:166
  285.6 0.5 reshape.410
  286.1 0.6 fusion.20
  286.7 0.7 reshape.411
  (25 shorter events, 0.1 us)
Async XLA Ops:
  7.2 135.6 %copy-start = (bf16[128,2304]{1,0:T(8,128)(2,1)S(1)}, bf16[128,2304]{1,0:T(8,128)(2,1)}, u32[]{:S(2)}) copy-start(bf16[128,2304]{1,0:T(8,128)(2,1)} %param.33) | copy-start | bytes 1769476
  7.2 54.2 %copy-start.3 = (bf16[2304,128]{1,0:T(8,128)(2,1)S(1)}, bf16[2304,128]{1,0:T(8,128)(2,1)}, u32[]{:S(2)}) copy-start(bf16[2304,128]{1,0:T(8,128)(2,1)} %param.22) | copy-start | bytes 1769476
  7.2 54.8 %copy-start.4 = (bf16[2304,128]{1,0:T(8,128)(2,1)S(1)}, bf16[2304,128]{1,0:T(8,128)(2,1)}, u32[]{:S(2)}) copy-start(bf16[2304,128]{1,0:T(8,128)(2,1)} %param.23) | copy-start | bytes 1769476
  7.2 48.5 %all-gather.2.cloned.1.call-start = ((), (), s32[]{:S(2)}) async-start(), calls=%async_computation.3 | async-start | bytes 1253376 | tf_op jit(solution)/shard_map/all_gather | solution.py:93
  7.9 209.1 %reduce-scatter.2.cloned.1.call-start = ((), (), s32[]{:S(2)}) async-start(), calls=%async_computation.4 | async-start | bytes 1253376 | tf_op jit(solution)/shard_map/reduce_scatter | solution.py:121
  61.3 2.2 copy-start.1
  61.4 6.0 %copy-start.2 = (bf16[64,4,2304]{2,1,0:T(4,128)(2,1)S(1)}, bf16[64,4,2304]{2,1,0:T(4,128)(2,1)}, u32[]{:S(2)}) copy-start(bf16[64,4,2304]{2,1,0:T(4,128)(2,1)} %all-gather.2.cloned.1.call-done) | copy-start | bytes 3538948
  61.4 6.0 %copy-start.9 = (bf16[2304,128]{1,0:T(8,128)(2,1)S(1)}, bf16[2304,128]{1,0:T(8,128)(2,1)}, u32[]{:S(2)}) copy-start(bf16[2304,128]{1,0:T(8,128)(2,1)} %param.24) | copy-start | bytes 1769476
  127.0 15.1 %copy-start.10 = (bf16[2304,128]{1,0:T(8,128)(2,1)S(1)}, bf16[2304,128]{1,0:T(8,128)(2,1)}, u32[]{:S(2)}) copy-start(bf16[2304,128]{1,0:T(8,128)(2,1)} %param.30) | copy-start | bytes 1769476
  127.0 15.1 %copy-start.11 = (bf16[128,128]{1,0:T(8,128)(2,1)S(1)}, bf16[128,128]{1,0:T(8,128)(2,1)}, u32[]{:S(2)}) copy-start(bf16[128,128]{1,0:T(8,128)(2,1)} %param.31) | copy-start | bytes 98308
  127.0 15.1 %copy-start.12 = (f32[128]{0:T(128)S(1)}, f32[128]{0:T(128)}, u32[]{:S(2)}) copy-start(f32[128]{0:T(128)} %param.32) | copy-start | bytes 1540
  141.8 2.5 copy-start.5
  141.8 2.6 copy-start.6
  141.8 76.2 %copy-start.7 = (f32[2304]{0:T(1024)S(1)}, f32[2304]{0:T(1024)}, u32[]{:S(2)}) copy-start(f32[2304]{0:T(1024)} %param.34) | copy-start | bytes 27652
  259.3 5.9 %copy-start.8 = (f32[4,4,8]{2,1,0:T(4,128)S(1)}, f32[4,4,8]{2,1,0:T(4,128)}, u32[]{:S(2)}) copy-start(f32[4,4,8]{2,1,0:T(4,128)} %param.36) | copy-start | bytes 1540
  260.6 25.0 %all-to-all-start.1 = ((bf16[128,2,2304]{2,1,0:T(2,128)(2,1)}), bf16[128,2,2304]{2,1,0:T(2,128)(2,1)S(1)}, u32[]{:S(2)}, u32[]{:S(2)}) async-start(bf16[128,2,2304]{2,1,0:T(2,128)(2,1)} %reshape.409), calls=%async_computation.2 | async-start | bytes 2359296 | tf_op jit(solution)/shard_map/all_to_all | solution.py:166
Sparse Core Ops, SparseCore 0:
  10.2 45.4 all-gather.1
  144.4 72.5 reduce-scatter.1
where the time goes:
time: 295 us; the launch traced here: 294 us
  waiting for transfers between devices  128 us (43%)
  matrix products  96.4 us (33%)
  blocking collectives  28.2 us (10%)
  between operations  15.2 us (5%)
  other arithmetic  14.1 us (5%)
  local copies, waits for them, and re-layouts  7.41 us (3%)
  starting transfers between devices  4.71 us (2%)
    reduce_scatter x1, waiting for transfers between devices, local(): lax.psum_scatter(jnp.dot(mixed_heads, output_weight, preferred_element_ty...  72.1 us
    all_gather x1, waiting for transfers between devices, local(): gathered = lax.all_gather(hidden_in, 'ecol', axis=0, tiled=True)  47 us
    dot_general x4, matrix products, delta_head(): jnp.einsum('rkv,rk->rv', memory, queries[:, position], precision=HIGHEST)  41.3 us
    dot_general x4, matrix products, delta_head(): jnp.einsum('rkv,rk->rv', memory, key_rows[:, position], precision=HIGHEST)  36.1 us
    all_to_all x1, blocking collectives, local(): lax.all_to_all(outgoing.reshape(device_count, capacity, model_width), ('e...  28.2 us
    add x1, other arithmetic, delta_head(): memory = memory + update  12 us
    all_to_all x1, waiting for transfers between devices, local(): lax.all_to_all(produced.reshape(received.shape), ('erow', 'ecol'), split_...  8.26 us
    dot_general x1, matrix products, local(): jnp.dot(hidden, expert_down[0], preferred_element_type=jnp.float32)  6.81 us
  transfers between devices with their start and end apart: 3, of which 3 were waited for; matrix products, arithmetic and copies ran while one was open for 4% of the time, Pallas kernels for 0%

commit v1 on v0

v1 whole, which is shorter than its diff:
```python
import functools

import jax
import jax.numpy as jnp
from jax import lax
from jax.experimental import pallas as pl
from jax.experimental.pallas import tpu as pltpu
from jax.sharding import PartitionSpec as P

EPSILON = 1e-06
HIGHEST = lax.Precision.HIGHEST
F32 = jnp.float32
BF16 = jnp.bfloat16
VMEM = pl.BlockSpec(memory_space=pltpu.VMEM)


def unit_rows(vectors):
    return vectors * lax.rsqrt(jnp.sum(vectors * vectors, -1, keepdims=True) + EPSILON)


def rms_scale(vectors):
    return vectors * lax.rsqrt(jnp.mean(vectors * vectors, -1, keepdims=True) + EPSILON)


def attend_kernel(
    steps,
    tok_ref,
    wq_ref,
    wk_ref,
    wv_ref,
    wb_ref,
    dd_ref,
    gd_ref,
    du_ref,
    gl_ref,
    dl_ref,
    db_ref,
    ng_ref,
    wo_ref,
    mem_ref,
    part_ref,
    keys_ref,
    upd_ref,
    stage,
    probe,
    reply,
):
    rows, _ = tok_ref.shape
    reqs = rows // steps
    hk = wq_ref.shape[1]
    tok = tok_ref[...]

    def project(weight):
        return jnp.dot(tok, weight, preferred_element_type=F32)

    qk = project(jnp.concatenate([wq_ref[...], wk_ref[...]], axis=1))
    low = project(jnp.concatenate([dd_ref[...], gd_ref[...]], axis=1)).astype(BF16)
    vb = project(jnp.concatenate([wv_ref[...], wb_ref[...]], axis=1))
    decay_pre = jnp.dot(low[:, : dd_ref.shape[1]], du_ref[...], preferred_element_type=F32)
    decay_pre = decay_pre + db_ref[...]
    gate = jax.nn.sigmoid(
        jnp.dot(low[:, dd_ref.shape[1] :], gl_ref[...], preferred_element_type=F32)
    )
    softplus = jnp.maximum(decay_pre, 0.0) + jnp.log1p(jnp.exp(-jnp.abs(decay_pre)))
    stage[0] = unit_rows(qk[:, :hk]) * hk ** (-0.5)
    stage[1] = unit_rows(qk[:, hk:])
    stage[2] = vb[:, :hk]
    stage[3] = jax.nn.sigmoid(vb[:, hk:])
    stage[4] = jnp.exp(-jnp.exp(dl_ref[...]) * softplus)

    def at(kind, t):
        return stage[kind, pl.ds(t, reqs, stride=steps), :]

    q = [at(0, t) for t in range(steps)]
    k = [at(1, t) for t in range(steps)]
    f = [at(4, t) for t in range(steps)]
    start = []
    for t in range(steps):
        start.append(f[0] if t == 0 else start[-1] * f[t])
        probe[pl.ds(t, reqs, stride=2 * steps), :] = start[t] * k[t]
        probe[pl.ds(steps + t, reqs, stride=2 * steps), :] = start[t] * q[t]

    def one_request(r, carry):
        at_rows = pl.ds(pl.multiple_of(r * 2 * steps, 2 * steps), 2 * steps)
        reply[at_rows, :] = jnp.dot(
            probe[at_rows, :].astype(BF16), mem_ref[r].astype(BF16), preferred_element_type=F32
        )
        return carry

    lax.fori_loop(0, reqs, one_request, 0, unroll=8)

    decayed = []
    updates = []
    for t in range(steps):
        if t > 0:
            decayed = [row * f[t] for row in decayed]
        predicted = reply[pl.ds(t, reqs, stride=2 * steps), :]
        for s in range(t):
            predicted = predicted + jnp.sum(decayed[s] * k[t], -1, keepdims=True) * updates[s]
        updates.append(at(3, t) * (at(2, t) - predicted))
        decayed.append(k[t])
        head = reply[pl.ds(steps + t, reqs, stride=2 * steps), :]
        for s in range(t + 1):
            head = head + jnp.sum(decayed[s] * q[t], -1, keepdims=True) * updates[s]
        stage[0, pl.ds(t, reqs, stride=steps), :] = head
    for t in range(steps):
        keys_ref[pl.ds(t, reqs, stride=2 * steps), :] = decayed[t]
        keys_ref[pl.ds(steps + t, reqs, stride=2 * steps), :] = start[-1]
        upd_ref[pl.ds(t, reqs, stride=steps), :] = updates[t]
    mixed = (rms_scale(stage[0]) * ng_ref[...] * gate).astype(BF16)
    part_ref[...] = jnp.dot(mixed, wo_ref[...], preferred_element_type=F32).astype(BF16)


def attend(tokens, weights, memory, steps):
    rows, width = tokens.shape
    reqs, hk, _ = memory.shape
    return pl.pallas_call(
        functools.partial(attend_kernel, steps),
        out_shape=(
            jax.ShapeDtypeStruct((rows, width), BF16),
            jax.ShapeDtypeStruct((2 * rows, hk), F32),
            jax.ShapeDtypeStruct((rows, hk), F32),
        ),
        in_specs=[VMEM] * (2 + len(weights)),
        out_specs=(VMEM,) * 3,
        scratch_shapes=[
            pltpu.VMEM((5, rows, hk), F32),
            pltpu.VMEM((2 * rows, hk), F32),
            pltpu.VMEM((2 * rows, hk), F32),
        ],
        compiler_params=pltpu.CompilerParams(vmem_limit_bytes=24 * 1024 * 1024),
        cost_estimate=pl.CostEstimate(
            flops=2 * rows * width * 7 * hk + 4 * reqs * 8 * hk * hk,
            bytes_accessed=10_000_000,
            transcendentals=0,
        ),
    )(tokens, *weights, memory)


def state_kernel(steps, keys_ref, upd_ref, mem_ref, new_ref):
    count = mem_ref.shape[0]
    columns = keys_ref[...].T
    for r in range(count):
        total = mem_ref[r] * columns[:, 2 * steps * r + steps : 2 * steps * r + steps + 1]
        for s in range(steps):
            at = 2 * steps * r + s
            row = upd_ref[pl.ds(steps * r + s, 1), :]
            total = total + columns[:, at : at + 1] * row
        new_ref[r] = total


def new_memory(keys, updates, memory, steps):
    reqs, hk, _ = memory.shape
    block = 16
    return pl.pallas_call(
        functools.partial(state_kernel, steps),
        out_shape=jax.ShapeDtypeStruct(memory.shape, F32),
        grid=(reqs // block,),
        in_specs=[
            pl.BlockSpec((2 * steps * block, hk), lambda i: (i, 0)),
            pl.BlockSpec((steps * block, hk), lambda i: (i, 0)),
            pl.BlockSpec((block, hk, hk), lambda i: (i, 0, 0)),
        ],
        out_specs=pl.BlockSpec((block, hk, hk), lambda i: (i, 0, 0)),
        compiler_params=pltpu.CompilerParams(vmem_limit_bytes=16 * 1024 * 1024),
        cost_estimate=pl.CostEstimate(
            flops=9 * reqs * hk * hk, bytes_accessed=2 * reqs * hk * hk * 4, transcendentals=0
        ),
    )(keys, updates, memory)


def expert_kernel(rows_ref, gate_ref, up_ref, down_ref, out_ref, total):
    step = pl.program_id(0)
    rows = rows_ref[...]
    gate = jnp.dot(rows, gate_ref[...], preferred_element_type=F32)
    up = jnp.dot(rows, up_ref[...], preferred_element_type=F32)
    hidden = (jax.nn.silu(gate) * up).astype(BF16)
    term = jnp.dot(hidden, down_ref[...], preferred_element_type=F32)

    @pl.when(step == 0)
    def _():
        total[...] = term

    @pl.when(step > 0)
    def _():
        total[...] += term

    @pl.when(step == pl.num_programs(0) - 1)
    def _():
        out_ref[...] = total[...].astype(BF16)


def run_expert(rows, gate, up, down):
    count, width = rows.shape
    hidden = gate.shape[1]
    block = 256
    return pl.pallas_call(
        expert_kernel,
        out_shape=jax.ShapeDtypeStruct((count, width), BF16),
        grid=(hidden // block,),
        in_specs=[
            pl.BlockSpec((count, width), lambda i: (0, 0)),
            pl.BlockSpec((width, block), lambda i: (0, i)),
            pl.BlockSpec((width, block), lambda i: (0, i)),
            pl.BlockSpec((block, width), lambda i: (i, 0)),
        ],
        out_specs=pl.BlockSpec((count, width), lambda i: (0, 0)),
        scratch_shapes=[pltpu.VMEM((count, width), F32)],
        compiler_params=pltpu.CompilerParams(vmem_limit_bytes=24 * 1024 * 1024),
        cost_estimate=pl.CostEstimate(
            flops=6 * count * width * hidden,
            bytes_accessed=6 * width * hidden + 4 * count * width,
            transcendentals=count * hidden,
        ),
    )(rows, gate, up, down)


def local(
    hidden_in,
    kda_state,
    query_weight,
    key_weight,
    value_weight,
    beta_weight,
    decay_down,
    decay_up,
    decay_log,
    decay_bias,
    gate_down,
    gate_lift,
    norm_gain,
    output_weight,
    ffn_gain,
    expert_ids,
    route_weight,
    expert_gate,
    expert_up,
    expert_down,
):
    local_req, step_count, model_width = hidden_in.shape
    head_size = kda_state.shape[-1]
    grid_rows = lax.axis_size("erow")
    grid_cols = lax.axis_size("ecol")
    own_rows = local_req * step_count
    own = hidden_in.reshape(own_rows, model_width)
    gathered = lax.all_to_all(
        jnp.broadcast_to(own[None], (grid_cols, own_rows, model_width)),
        "ecol",
        split_axis=0,
        concat_axis=0,
        tiled=True,
    ).reshape(grid_cols * own_rows, model_width)
    memory = kda_state.reshape(kda_state.shape[0], head_size, head_size)
    weights = (
        query_weight,
        key_weight,
        value_weight,
        jnp.broadcast_to(beta_weight, (model_width, head_size)),
        decay_down,
        gate_down,
        decay_up,
        gate_lift,
        decay_log.reshape(1, 1),
        decay_bias.reshape(1, head_size),
        norm_gain.reshape(1, head_size),
        output_weight,
    )
    partial, keys, updates = attend(gathered, weights, memory, step_count)
    terms = lax.all_to_all(
        partial.reshape(grid_cols, own_rows, model_width),
        "ecol",
        split_axis=0,
        concat_axis=0,
        tiled=True,
    )
    new_state = new_memory(keys, updates, memory, step_count).reshape(kda_state.shape)
    attended = jnp.sum(terms.astype(F32), 0)
    residual = (own.astype(F32) + attended).astype(BF16)
    normed = (rms_scale(residual.astype(F32)) * ffn_gain).astype(BF16)
    device_count = grid_rows * grid_cols
    pick_count = expert_ids.shape[-1]
    capacity = max(2, 2 * own_rows * pick_count // device_count)
    slots_total = device_count * capacity
    flat_ids = expert_ids.reshape(-1)
    flat_weights = route_weight.reshape(-1)
    serial = jnp.arange(flat_ids.shape[0], dtype=jnp.int32)
    earlier = (flat_ids[:, None] == flat_ids[None, :]) & (serial[None, :] < serial[:, None])
    slot_of = flat_ids * capacity + jnp.sum(earlier.astype(jnp.int32), 1)
    matches = (slot_of[:, None] == jnp.arange(slots_total, dtype=jnp.int32)[None, :]).reshape(
        own_rows, pick_count, slots_total
    )
    placing = jnp.any(matches, 1).astype(BF16)
    combine = jnp.sum(jnp.where(matches, flat_weights.reshape(own_rows, pick_count, 1), 0.0), 1)
    outgoing = lax.dot_general(
        placing, normed, (((0,), (0,)), ((), ())), preferred_element_type=F32
    ).astype(BF16)
    received = lax.all_to_all(
        outgoing.reshape(device_count, capacity, model_width),
        ("erow", "ecol"),
        split_axis=0,
        concat_axis=0,
        tiled=True,
    )
    produced = run_expert(
        received.reshape(-1, model_width), expert_gate[0], expert_up[0], expert_down[0]
    )
    returned = lax.all_to_all(
        produced.reshape(received.shape), ("erow", "ecol"), split_axis=0, concat_axis=0, tiled=True
    )
    returned = returned.reshape(slots_total, model_width)
    routed = jnp.dot(combine, returned.astype(F32), precision=HIGHEST)
    mixed = (
        (residual.astype(F32) + routed).astype(BF16).reshape(local_req, step_count, model_width)
    )
    return (mixed, new_state)


def solution(mesh):
    return jax.shard_map(
        local,
        mesh=mesh,
        in_specs=(
            P(("erow", "ecol"), None, None),
            P("erow", "ecol", None, None),
            P(None, "ecol"),
            P(None, "ecol"),
            P(None, "ecol"),
            P(None, "ecol"),
            P(),
            P(None, "ecol"),
            P("ecol"),
            P("ecol"),
            P(),
            P(None, "ecol"),
            P(),
            P("ecol", None),
            P(),
            P(("erow", "ecol"), None, None),
            P(("erow", "ecol"), None, None),
            P(("erow", "ecol"), None, None),
            P(("erow", "ecol"), None, None),
            P(("erow", "ecol"), None, None),
        ),
        out_specs=(P(("erow", "ecol"), None, None), P("erow", "ecol", None, None)),
        check_vma=False,
    )
```

time: 295 us -> 136 us (0.46)
  matrix products: 96.4 us -> 1.11 us
  waiting for transfers between devices: 128 us -> 44.3 us
  Pallas kernels: 0 us -> 19.3 us
  local copies, waits for them, and re-layouts: 7.41 us -> 23.4 us
  between operations: 15.2 us -> 1.6 us
  other arithmetic: 14.1 us -> 1.49 us
  starting transfers between devices: 4.71 us -> 15.9 us
    dot_general x18 -> x1, matrix products: 95.9 us -> 0.59 us  [local(): routed = jnp.dot(combine, returned.astype(F32), precision=HIGHEST)]
    reduce_scatter x1 -> x0, waiting for transfers between devices: 72.1 us -> none  [local(): lax.psum_scatter(jnp.dot(mixed_heads, output_weight, preferred_element_ty...]
    all_gather x1 -> x0, waiting for transfers between devices: 47 us -> none  [local(): gathered = lax.all_gather(hidden_in, 'ecol', axis=0, tiled=True)]
    all_to_all x0 -> x2, waiting for transfers between devices: none -> 33.9 us  [the longest x1 17.9 us: local(): lax.all_to_all(jnp.broadcast_to(own[None], (grid_cols, own_rows, model_wi...]
    pallas_call x0 -> x3, Pallas kernels: none -> 19.3 us  [the longest x1 7.63 us: new_memory(): pl.pallas_call(functools.partial(state_kernel, steps), out_shape=jax.Shap...]
    unnamed x26 -> x56, local copies, waits for them, and re-layouts: 0.8 us -> 17.4 us
    add x1 -> x0, other arithmetic: 12 us -> none  [delta_head(): memory = memory + update]
    all_to_all x0 -> x2, starting transfers between devices: none -> 11.1 us  [the longest x1 7.26 us: local(): lax.all_to_all(jnp.broadcast_to(own[None], (grid_cols, own_rows, model_wi...]
  transfers between devices with their start and end apart: 3 -> 3, of which waited for: 3 -> 3; matrix products, arithmetic and copies ran while one was open for 4% -> 1% of each run, Pallas kernels for 0% -> 6%
where the time goes in v1:
time: 136 us; the launch traced here: 135 us
  waiting for transfers between devices  44.3 us (33%)
  blocking collectives  27.9 us (21%)
  local copies, waits for them, and re-layouts  23.4 us (17%)
  Pallas kernels  19.3 us (14%)
  starting transfers between devices  15.9 us (12%)
  between operations  1.6 us (1%)
  other arithmetic  1.49 us (1%)
    all_to_all x1, blocking collectives, local(): lax.all_to_all(outgoing.reshape(device_count, capacity, model_width), ('e...  27.9 us
    all_to_all x1, waiting for transfers between devices, local(): lax.all_to_all(jnp.broadcast_to(own[None], (grid_cols, own_rows, model_wi...  17.9 us
    unnamed x56, local copies, waits for them, and re-layouts  17.4 us
    all_to_all x1, waiting for transfers between devices, local(): lax.all_to_all(partial.reshape(grid_cols, own_rows, model_width), 'ecol',...  16 us
    all_to_all x1, waiting for transfers between devices, local(): lax.all_to_all(produced.reshape(received.shape), ('erow', 'ecol'), split_...  10.4 us
    pallas_call x1, Pallas kernels, new_memory(): pl.pallas_call(functools.partial(state_kernel, steps), out_shape=jax.Shap...  7.63 us
    all_to_all x1, starting transfers between devices, local(): lax.all_to_all(jnp.broadcast_to(own[None], (grid_cols, own_rows, model_wi...  7.26 us
    pallas_call x1, Pallas kernels, run_expert(): pl.pallas_call(expert_kernel, out_shape=jax.ShapeDtypeStruct((count, widt...  7.13 us
  transfers between devices with their start and end apart: 3, of which 3 were waited for; matrix products, arithmetic and copies ran while one was open for 1% of the time, Pallas kernels for 6%

profile of v1, /device:TPU:0, one launch (start us, length us, event | category | flops | bytes accessed | tf_op | source)
XLA Modules:
  0.0 135.0 jit_solution(4062009280542429155)
XLA Ops:
  0.6 0.9 reshape.87
  1.5 0.0 copy-start.21
  1.5 0.6 copy-done.21
  2.2 1.1 broadcast_in_dim.32
  3.3 0.0 copy-start.17
  3.3 0.0 copy-start.18
  3.3 7.3 %all-to-all-start = ((bf16[16,16,2304]{2,1,0:T(8,128)(2,1)}), bf16[16,16,2304]{2,1,0:T(8,128)(2,1)S(1)}, u32[]{:S(2)}, u32[]{:S(2)}) async-start(bf16[16,16,2304]{2,1,0:T(8,128)(2,1)} %broadcast_in_dim.32), calls=%async_computation | async-start | bytes 2359296 | tf_op jit(solution)/shard_map/all_to_all | solution.py:246
  11.2 0.7 reduce.1
  12.0 17.9 %all-to-all-done = bf16[16,16,2304]{2,1,0:T(8,128)(2,1)S(1)} async-done(((bf16[16,16,2304]{2,1,0:T(8,128)(2,1)}), bf16[16,16,2304]{2,1,0:T(8,128)(2,1)S(1)}, u32[]{:S(2)}, u32[]{:S(2)}) %all-to-all-start) | async-done | bytes 1179680 | tf_op jit(solution)/shard_map/all_to_all | solution.py:246
  29.9 0.4 broadcast_in_dim.34.wb_ref
  30.2 0.0 copy-done.5
  30.3 0.0 copy-done.6
  30.3 0.0 copy-done.7
  30.3 0.0 copy-done.8
  30.3 0.0 copy-done.17
  30.3 0.0 copy-done.18
  30.3 0.0 copy-start
  30.3 2.2 %copy-done = f32[64,1,128,128]{3,2,1,0:T(8,128)S(1)} copy-done((f32[64,1,128,128]{3,2,1,0:T(8,128)S(1)}, f32[64,1,128,128]{3,2,1,0:T(8,128)}, u32[]{:S(2)}) %copy-start) | copy-done | bytes 4194328
  32.5 1.1 copy-done.9
  33.6 1.1 copy-done.10
  34.6 0.8 copy-done.15
  35.4 0.8 copy-done.16
  36.1 4.5 %shard_map.203 = (bf16[256,2304]{1,0:T(8,128)(2,1)}, f32[512,128]{1,0:T(8,128)S(1)}, f32[256,128]{1,0:T(8,128)S(1)}) custom-call(bf16[256,2304]{1,0:T(8,128)(2,1)S(1)} %bitcast.20, bf16[2304,128]{1,0:T(8,128)(2,1)S(1)} %copy-done.5, bf16[2304,128]{1,0:T(8,128)(2,1)S(1)} %copy-done.6, bf16[2304,128]{1,0:T(8,128)(2,1)S(1)} %copy-done.7, ...), custom_call_target="tpu_custom_call" | custom-call | flops 1090519040 | bytes 10000000 | tf_op jit(solution)/shard_map/pallas_call | solution.py:117
  40.7 0.7 copy-done.11
  41.4 0.7 copy-done.13
  42.0 3.8 %all-to-all-start.1 = ((bf16[16,16,2304]{2,1,0:T(8,128)(2,1)}), bf16[16,16,2304]{2,1,0:T(8,128)(2,1)S(1)}, u32[]{:S(2)}, u32[]{:S(2)}) async-start(bf16[16,16,2304]{2,1,0:T(8,128)(2,1)} %bitcast.5), calls=%async_computation.1 | async-start | bytes 2359296 | tf_op jit(solution)/shard_map/all_to_all | solution.py:269
  45.9 0.0 copy-done.25
  45.9 0.0 copy-start.24
  45.9 0.0 copy-start.22
  45.9 0.0 copy-start.26
  45.9 0.1 eq.29
  46.0 0.2 convert_reduce_fusion.1
  46.2 0.1 reduce_sum.42
  46.3 0.1 fusion.3
  46.4 16.0 %all-to-all-done.1 = bf16[16,16,2304]{2,1,0:T(8,128)(2,1)S(1)} async-done(((bf16[16,16,2304]{2,1,0:T(8,128)(2,1)}), bf16[16,16,2304]{2,1,0:T(8,128)(2,1)S(1)}, u32[]{:S(2)}, u32[]{:S(2)}) %all-to-all-start.1) | async-done | bytes 1179680 | tf_op jit(solution)/shard_map/all_to_all | solution.py:269
  62.4 0.2 convert_reduce_fusion
  62.6 0.0 copy-start.19
  62.6 0.0 copy-done.24
  62.7 0.1 multiply_reduce_fusion
  62.8 0.1 rsqrt.12
  62.9 0.3 copy-done.19
  63.2 0.0 copy-done.22
  63.2 0.0 copy-done.26
  63.2 0.5 convolution_convert_fusion
  63.8 0.5 reshape.94
  64.3 27.9 %all_to_all.20 = bf16[128,2,2304]{2,1,0:T(2,128)(2,1)S(1)} all-to-all(bf16[128,2,2304]{2,1,0:T(2,128)(2,1)S(1)} %reshape.94), channel_id=1, replica_groups=mesh['erow'=8,'ecol'=16] {'erow','ecol'}, dimensions={0} | all-to-all | bytes 2359296 | tf_op jit(solution)/shard_map/all_to_all | solution.py:297
  92.1 0.5 reshape.95.rows_ref
  92.6 0.0 copy-start.2
  92.6 2.3 %copy-done.2 = bf16[1,2304,1024]{2,1,0:T(8,128)(2,1)S(1)} copy-done((bf16[1,2304,1024]{2,1,0:T(8,128)(2,1)S(1)}, bf16[1,2304,1024]{2,1,0:T(8,128)(2,1)}, u32[]{:S(2)}) %copy-start.2) | copy-done | bytes 4718616
  94.9 2.3 %copy-done.3 = bf16[1,2304,1024]{2,1,0:T(8,128)(2,1)S(1)} copy-done((bf16[1,2304,1024]{2,1,0:T(8,128)(2,1)S(1)}, bf16[1,2304,1024]{2,1,0:T(8,128)(2,1)}, u32[]{:S(2)}) %copy-start.3) | copy-done | bytes 4718616
  97.3 2.3 %copy-done.4 = bf16[1,1024,2304]{2,1,0:T(8,128)(2,1)S(1)} copy-done((bf16[1,1024,2304]{2,1,0:T(8,128)(2,1)S(1)}, bf16[1,1024,2304]{2,1,0:T(8,128)(2,1)}, u32[]{:S(2)}) %copy-start.4) | copy-done | bytes 4718616
  99.6 7.1 %shard_map.204 = bf16[256,2304]{1,0:T(8,128)(2,1)S(1)} custom-call(bf16[256,2304]{1,0:T(8,128)(2,1)S(1)} %reshape.95.rows_ref, bf16[2304,1024]{1,0:T(8,128)(2,1)S(1)} %bitcast.21, bf16[2304,1024]{1,0:T(8,128)(2,1)S(1)} %bitcast.22, bf16[1024,2304]{1,0:T(8,128)(2,1)S(1)} %bitcast.23), custom_call_target="tpu_custom_call" | custom-call | flops 3623878656 | bytes 16515072 | tf_op jit(solution)/shard_map/pallas_call | solution.py:197
  106.8 1.3 reshape.96
  108.1 4.8 %all-to-all-start.3 = ((bf16[128,2,2304]{2,1,0:T(2,128)(2,1)}), bf16[128,2,2304]{2,1,0:T(2,128)(2,1)S(1)}, u32[]{:S(2)}, u32[]{:S(2)}) async-start(bf16[128,2,2304]{2,1,0:T(2,128)(2,1)} %reshape.96), calls=%async_computation.3 | async-start | bytes 2359296 | tf_op jit(solution)/shard_map/all_to_all | solution.py:307
  112.8 0.0 copy-done.27
  112.8 0.1 select_reduce_fusion
  113.0 0.0 copy-done.12
  113.0 0.0 copy-start.1
  113.0 2.2 %copy-done.1 = f32[64,1,128,128]{3,2,1,0:T(8,128)S(1)} copy-done((f32[64,1,128,128]{3,2,1,0:T(8,128)S(1)}, f32[64,1,128,128]{3,2,1,0:T(8,128)}, u32[]{:S(2)}) %copy-start.1) | copy-done | bytes 4194328
  115.2 7.6 %shard_map.205 = f32[64,128,128]{2,1,0:T(8,128)} custom-call(f32[512,128]{1,0:T(8,128)S(1)} %copy-done.12, f32[256,128]{1,0:T(8,128)S(1)} %copy-done.14, f32[64,128,128]{2,1,0:T(8,128)S(1)} %bitcast.19), custom_call_target="tpu_custom_call" | custom-call | flops 9437184 | bytes 8388608 | tf_op jit(solution)/shard_map/pallas_call | solution.py:155
  122.8 10.4 %all-to-all-done.3 = bf16[128,2,2304]{2,1,0:T(2,128)(2,1)S(1)} async-done(((bf16[128,2,2304]{2,1,0:T(2,128)(2,1)}), bf16[128,2,2304]{2,1,0:T(2,128)(2,1)S(1)}, u32[]{:S(2)}, u32[]{:S(2)}) %all-to-all-start.3) | async-done | bytes 1179680 | tf_op jit(solution)/shard_map/all_to_all | solution.py:307
  133.2 0.5 reshape.97
  133.7 0.6 fusion
  134.3 0.7 reshape.98
  (25 shorter events, 0.1 us)
Async XLA Ops:
  1.5 0.6 copy-start.21
  3.3 27.0 %copy-start.5 = (bf16[2304,128]{1,0:T(8,128)(2,1)S(1)}, bf16[2304,128]{1,0:T(8,128)(2,1)}, u32[]{:S(2)}) copy-start(bf16[2304,128]{1,0:T(8,128)(2,1)} %wq_ref.1) | copy-start | bytes 1769476
  3.3 27.0 %copy-start.6 = (bf16[2304,128]{1,0:T(8,128)(2,1)S(1)}, bf16[2304,128]{1,0:T(8,128)(2,1)}, u32[]{:S(2)}) copy-start(bf16[2304,128]{1,0:T(8,128)(2,1)} %wk_ref.1) | copy-start | bytes 1769476
  3.3 27.0 %copy-start.7 = (bf16[2304,128]{1,0:T(8,128)(2,1)S(1)}, bf16[2304,128]{1,0:T(8,128)(2,1)}, u32[]{:S(2)}) copy-start(bf16[2304,128]{1,0:T(8,128)(2,1)} %wv_ref.1) | copy-start | bytes 1769476
  3.3 27.0 %copy-start.8 = (bf16[2304,128]{1,0:T(8,128)(2,1)S(1)}, bf16[2304,128]{1,0:T(8,128)(2,1)}, u32[]{:S(2)}) copy-start(bf16[2304,128]{1,0:T(8,128)(2,1)} %dd_ref.1) | copy-start | bytes 1769476
  3.3 27.0 %copy-start.17 = (f32[128]{0:T(128)S(1)}, f32[128]{0:T(128)}, u32[]{:S(2)}) copy-start(f32[128]{0:T(128)} %param.29) | copy-start | bytes 1540
  3.3 27.0 %copy-start.18 = (f32[128]{0:T(128)S(1)}, f32[128]{0:T(128)}, u32[]{:S(2)}) copy-start(f32[128]{0:T(128)} %param.32) | copy-start | bytes 1540
  3.3 26.6 %all-to-all-start = ((bf16[16,16,2304]{2,1,0:T(8,128)(2,1)}), bf16[16,16,2304]{2,1,0:T(8,128)(2,1)S(1)}, u32[]{:S(2)}, u32[]{:S(2)}) async-start(bf16[16,16,2304]{2,1,0:T(8,128)(2,1)} %broadcast_in_dim.32), calls=%async_computation | async-start | bytes 2359296 | tf_op jit(solution)/shard_map/all_to_all | solution.py:246
  30.3 2.2 %copy-start = (f32[64,1,128,128]{3,2,1,0:T(8,128)S(1)}, f32[64,1,128,128]{3,2,1,0:T(8,128)}, u32[]{:S(2)}) copy-start(f32[64,1,128,128]{3,2,1,0:T(8,128)} %param.21) | copy-start | bytes 12582916
  32.5 1.1 copy-start.9
  33.6 1.1 copy-start.10
  34.6 0.8 copy-start.15
  35.4 0.8 copy-start.16
  40.7 0.7 copy-start.11
  41.4 0.7 copy-start.13
  42.0 3.8 %copy-start.25 = (s32[4,4,8]{2,1,0:T(4,128)S(1)}, s32[4,4,8]{2,1,0:T(4,128)}, u32[]{:S(2)}) copy-start(s32[4,4,8]{2,1,0:T(4,128)} %param.35) | copy-start | bytes 1540
  42.0 20.4 %all-to-all-start.1 = ((bf16[16,16,2304]{2,1,0:T(8,128)(2,1)}), bf16[16,16,2304]{2,1,0:T(8,128)(2,1)S(1)}, u32[]{:S(2)}, u32[]{:S(2)}) async-start(bf16[16,16,2304]{2,1,0:T(8,128)(2,1)} %bitcast.5), calls=%async_computation.1 | async-start | bytes 2359296 | tf_op jit(solution)/shard_map/all_to_all | solution.py:269
  45.9 16.8 %copy-start.24 = (bf16[4,4,2304]{2,1,0:T(4,128)(2,1)S(1)}, bf16[4,4,2304]{2,1,0:T(4,128)(2,1)}, u32[]{:S(2)}) copy-start(bf16[4,4,2304]{2,1,0:T(4,128)(2,1)} %param.20) | copy-start | bytes 221188
  45.9 17.3 %copy-start.22 = (bf16[16,2304]{1,0:T(8,128)(2,1)S(1)}, bf16[16,2304]{1,0:T(8,128)(2,1)}, u32[]{:S(2)}) copy-start(bf16[16,2304]{1,0:T(8,128)(2,1)} %copy-done.21) | copy-start | bytes 221188
  45.9 17.3 %copy-start.26 = (f32[2304]{0:T(1024)S(1)}, f32[2304]{0:T(1024)}, u32[]{:S(2)}) copy-start(f32[2304]{0:T(1024)} %param.34) | copy-start | bytes 27652
  62.6 0.7 copy-start.19
  92.6 2.3 %copy-start.2 = (bf16[1,2304,1024]{2,1,0:T(8,128)(2,1)S(1)}, bf16[1,2304,1024]{2,1,0:T(8,128)(2,1)}, u32[]{:S(2)}) copy-start(bf16[1,2304,1024]{2,1,0:T(8,128)(2,1)} %param.37) | copy-start | bytes 14155780
  94.9 2.3 %copy-start.3 = (bf16[1,2304,1024]{2,1,0:T(8,128)(2,1)S(1)}, bf16[1,2304,1024]{2,1,0:T(8,128)(2,1)}, u32[]{:S(2)}) copy-start(bf16[1,2304,1024]{2,1,0:T(8,128)(2,1)} %param.38) | copy-start | bytes 14155780
  97.3 2.3 %copy-start.4 = (bf16[1,1024,2304]{2,1,0:T(8,128)(2,1)S(1)}, bf16[1,1024,2304]{2,1,0:T(8,128)(2,1)}, u32[]{:S(2)}) copy-start(bf16[1,1024,2304]{2,1,0:T(8,128)(2,1)} %param.39) | copy-start | bytes 14155780
  108.1 4.8 %copy-start.27 = (f32[4,4,8]{2,1,0:T(4,128)S(1)}, f32[4,4,8]{2,1,0:T(4,128)}, u32[]{:S(2)}) copy-start(f32[4,4,8]{2,1,0:T(4,128)} %param.36) | copy-start | bytes 1540
  108.1 4.9 %copy-start.12 = (f32[512,128]{1,0:T(8,128)S(1)}, f32[512,128]{1,0:T(8,128)}, u32[]{:S(2)}) copy-start(f32[512,128]{1,0:T(8,128)} %copy-done.11) | copy-start | bytes 786436
  108.1 4.9 %copy-start.14 = (f32[256,128]{1,0:T(8,128)S(1)}, f32[256,128]{1,0:T(8,128)}, u32[]{:S(2)}) copy-start(f32[256,128]{1,0:T(8,128)} %copy-done.13) | copy-start | bytes 393220
  108.1 25.2 %all-to-all-start.3 = ((bf16[128,2,2304]{2,1,0:T(2,128)(2,1)}), bf16[128,2,2304]{2,1,0:T(2,128)(2,1)S(1)}, u32[]{:S(2)}, u32[]{:S(2)}) async-start(bf16[128,2,2304]{2,1,0:T(2,128)(2,1)} %reshape.96), calls=%async_computation.3 | async-start | bytes 2359296 | tf_op jit(solution)/shard_map/all_to_all | solution.py:307
  113.0 2.2 %copy-start.1 = (f32[64,1,128,128]{3,2,1,0:T(8,128)S(1)}, f32[64,1,128,128]{3,2,1,0:T(8,128)}, u32[]{:S(2)}) copy-start(f32[64,1,128,128]{3,2,1,0:T(8,128)} %param.21) | copy-start | bytes 12582916
  122.8 10.9 %copy-start.20 = (f32[16,2304]{1,0:T(8,128)S(1)}, f32[16,2304]{1,0:T(8,128)}, u32[]{:S(2)}) copy-start(f32[16,2304]{1,0:T(8,128)} %copy-done.19) | copy-start | bytes 442372
  122.8 10.9 %copy-start.23 = (bf16[16,2304]{1,0:T(8,128)(2,1)S(1)}, bf16[16,2304]{1,0:T(8,128)(2,1)}, u32[]{:S(2)}) copy-start(bf16[16,2304]{1,0:T(8,128)(2,1)} %copy-done.21) | copy-start | bytes 221188

commit v2 on v1

--- a/solution.py
+++ b/solution.py
@@ -8,10 +8,14 @@
 from jax.sharding import PartitionSpec as P
 
 EPSILON = 1e-06
-HIGHEST = lax.Precision.HIGHEST
 F32 = jnp.float32
 BF16 = jnp.bfloat16
 VMEM = pl.BlockSpec(memory_space=pltpu.VMEM)
+HBM = pl.BlockSpec(memory_space=pltpu.HBM)
+
+
+def in_hbm(array):
+    return pltpu.with_memory_space_constraint(array, pltpu.HBM)
 
 
 def unit_rows(vectors):
@@ -20,6 +24,27 @@
 
 def rms_scale(vectors):
     return vectors * lax.rsqrt(jnp.mean(vectors * vectors, -1, keepdims=True) + EPSILON)
+
+
+def spread_kernel(in_ref, out_hbm, send):
+    copies = [
+        pltpu.make_async_copy(in_ref, out_hbm.at[i], send.at[i]) for i in range(out_hbm.shape[0])
+    ]
+    for copy in copies:
+        copy.start()
+    for copy in copies:
+        copy.wait()
+
+
+def spread(hidden, count):
+    return pl.pallas_call(
+        spread_kernel,
+        out_shape=pltpu.HBM((count, *hidden.shape), hidden.dtype),
+        in_specs=[VMEM],
+        out_specs=HBM,
+        scratch_shapes=[pltpu.SemaphoreType.DMA((count,))],
+        compiler_params=pltpu.CompilerParams(vmem_limit_bytes=2 * 1024 * 1024),
+    )(hidden)
 
 
 def attend_kernel(
@@ -29,33 +54,61 @@
     wk_ref,
     wv_ref,
     wb_ref,
+    dl_ref,
+    db_ref,
+    ng_ref,
+    dd_hbm,
+    gd_hbm,
+    du_hbm,
+    gl_hbm,
+    wo_hbm,
+    mem_hbm,
+    part_ref,
+    keys_hbm,
+    upd_hbm,
+    stage,
+    probe,
+    reply,
+    keys_ref,
+    upd_ref,
     dd_ref,
     gd_ref,
     du_ref,
     gl_ref,
-    dl_ref,
-    db_ref,
-    ng_ref,
     wo_ref,
     mem_ref,
-    part_ref,
-    keys_ref,
-    upd_ref,
-    stage,
-    probe,
-    reply,
+    sems,
 ):
-    rows, _ = tok_ref.shape
+    width, hk = wq_ref.shape
+    rows = stage.shape[1]
     reqs = rows // steps
-    hk = wq_ref.shape[1]
-    tok = tok_ref[...]
+    pairs = (
+        (dd_hbm, dd_ref),
+        (gd_hbm, gd_ref),
+        (du_hbm, du_ref),
+        (gl_hbm, gl_ref),
+        (mem_hbm, mem_ref),
+        (wo_hbm, wo_ref),
+    )
+    loads = [pltpu.make_async_copy(src, dst, sems.at[i]) for i, (src, dst) in enumerate(pairs)]
+    for load in loads:
+        load.start()
+    tok = tok_ref[...].reshape(rows, width)
 
     def project(weight):
         return jnp.dot(tok, weight, preferred_element_type=F32)
 
     qk = project(jnp.concatenate([wq_ref[...], wk_ref[...]], axis=1))
+    value = project(wv_ref[...])
+    beta = lax.dot_general(
+        tok,
+        jnp.broadcast_to(wb_ref[...], (hk, width)),
+        (((1,), (1,)), ((), ())),
+        preferred_element_type=F32,
+    )
+    for load in loads[:4]:
+        load.wait()
     low = project(jnp.concatenate([dd_ref[...], gd_ref[...]], axis=1)).astype(BF16)
-    vb = project(jnp.concatenate([wv_ref[...], wb_ref[...]], axis=1))
     decay_pre = jnp.dot(low[:, : dd_ref.shape[1]], du_ref[...], preferred_element_type=F32)
     decay_pre = decay_pre + db_ref[...]
     gate = jax.nn.sigmoid(
@@ -64,8 +117,8 @@
     softplus = jnp.maximum(decay_pre, 0.0) + jnp.log1p(jnp.exp(-jnp.abs(decay_pre)))
     stage[0] = unit_rows(qk[:, :hk]) * hk ** (-0.5)
     stage[1] = unit_rows(qk[:, hk:])
-    stage[2] = vb[:, :hk]
-    stage[3] = jax.nn.sigmoid(vb[:, hk:])
+    stage[2] = value
+    stage[3] = jax.nn.sigmoid(beta)
     stage[4] = jnp.exp(-jnp.exp(dl_ref[...]) * softplus)
 
     def at(kind, t):
@@ -80,10 +133,12 @@
         probe[pl.ds(t, reqs, stride=2 * steps), :] = start[t] * k[t]
         probe[pl.ds(steps + t, reqs, stride=2 * steps), :] = start[t] * q[t]
 
+    loads[4].wait()
+
     def one_request(r, carry):
         at_rows = pl.ds(pl.multiple_of(r * 2 * steps, 2 * steps), 2 * steps)
         reply[at_rows, :] = jnp.dot(
-            probe[at_rows, :].astype(BF16), mem_ref[r].astype(BF16), preferred_element_type=F32
+            probe[at_rows, :].astype(BF16), mem_ref[r], preferred_element_type=F32
         )
         return carry
 
@@ -107,34 +162,48 @@
         keys_ref[pl.ds(t, reqs, stride=2 * steps), :] = decayed[t]
         keys_ref[pl.ds(steps + t, reqs, stride=2 * steps), :] = start[-1]
         upd_ref[pl.ds(t, reqs, stride=steps), :] = updates[t]
+    stores = [
+        pltpu.make_async_copy(keys_ref, keys_hbm, sems.at[6]),
+        pltpu.make_async_copy(upd_ref, upd_hbm, sems.at[7]),
+    ]
+    for store in stores:
+        store.start()
+    loads[5].wait()
     mixed = (rms_scale(stage[0]) * ng_ref[...] * gate).astype(BF16)
     part_ref[...] = jnp.dot(mixed, wo_ref[...], preferred_element_type=F32).astype(BF16)
-
-
-def attend(tokens, weights, memory, steps):
-    rows, width = tokens.shape
+    for store in stores:
+        store.wait()
+
+
+def attend(tokens, weights, fetched, memory, steps):
     reqs, hk, _ = memory.shape
+    rows, width = reqs * steps, tokens.shape[-1]
+    fetched = [in_hbm(array) for array in (*fetched, memory)]
     return pl.pallas_call(
         functools.partial(attend_kernel, steps),
         out_shape=(
             jax.ShapeDtypeStruct((rows, width), BF16),
-            jax.ShapeDtypeStruct((2 * rows, hk), F32),
-            jax.ShapeDtypeStruct((rows, hk), F32),
-        ),
-        in_specs=[VMEM] * (2 + len(weights)),
-        out_specs=(VMEM,) * 3,
+            pltpu.HBM((2 * rows, hk), F32),
+            pltpu.HBM((rows, hk), F32),
+        ),
+        in_specs=[VMEM] * (1 + len(weights)) + [HBM] * len(fetched),
+        out_specs=(VMEM, HBM, HBM),
         scratch_shapes=[
             pltpu.VMEM((5, rows, hk), F32),
             pltpu.VMEM((2 * rows, hk), F32),
             pltpu.VMEM((2 * rows, hk), F32),
+            pltpu.VMEM((2 * rows, hk), F32),
+            pltpu.VMEM((rows, hk), F32),
+            *[pltpu.VMEM(array.shape, array.dtype) for array in fetched],
+            pltpu.SemaphoreType.DMA((len(fetched) + 2,)),
         ],
-        compiler_params=pltpu.CompilerParams(vmem_limit_bytes=24 * 1024 * 1024),
+        compiler_params=pltpu.CompilerParams(vmem_limit_bytes=32 * 1024 * 1024),
         cost_estimate=pl.CostEstimate(
             flops=2 * rows * width * 7 * hk + 4 * reqs * 8 * hk * hk,
             bytes_accessed=10_000_000,
             transcendentals=0,
         ),
-    )(tokens, *weights, memory)
+    )(tokens, *weights, *fetched)
 
 
 def state_kernel(steps, keys_ref, upd_ref, mem_ref, new_ref):
@@ -166,46 +235,55 @@
         cost_estimate=pl.CostEstimate(
             flops=9 * reqs * hk * hk, bytes_accessed=2 * reqs * hk * hk * 4, transcendentals=0
         ),
-    )(keys, updates, memory)
-
-
-def expert_kernel(rows_ref, gate_ref, up_ref, down_ref, out_ref, total):
-    step = pl.program_id(0)
-    rows = rows_ref[...]
+    )(in_hbm(keys), in_hbm(updates), in_hbm(memory))
+
+
+def join_kernel(terms_ref, own_ref, gain_ref, place_ref, residual_ref, out_ref):
+    total = own_ref[...].reshape(residual_ref.shape).astype(F32)
+    attended = terms_ref[0].astype(F32)
+    for i in range(1, terms_ref.shape[0]):
+        attended = attended + terms_ref[i].astype(F32)
+    residual = (total + attended).astype(BF16)
+    residual_ref[...] = residual
+    normed = (rms_scale(residual.astype(F32)) * gain_ref[...]).astype(BF16)
+    sent = jnp.dot(place_ref[...], normed, preferred_element_type=F32).astype(BF16)
+    out_ref[...] = sent.reshape(out_ref.shape)
+
+
+def join(terms, own, gain, placing, shape):
+    _, rows, width = terms.shape
+    return pl.pallas_call(
+        join_kernel,
+        out_shape=(
+            jax.ShapeDtypeStruct((rows, width), BF16),
+            jax.ShapeDtypeStruct(shape, BF16),
+        ),
+        in_specs=[VMEM] * 4,
+        out_specs=(VMEM, VMEM),
+        compiler_params=pltpu.CompilerParams(vmem_limit_bytes=8 * 1024 * 1024),
+        cost_estimate=pl.CostEstimate(
+            flops=40_000_000_000, bytes_accessed=40_000_000, transcendentals=0
+        ),
+    )(terms, own, gain, placing)
+
+
+def expert_kernel(rows_ref, gate_ref, up_ref, down_ref, out_ref):
+    rows = rows_ref[...].reshape(-1, rows_ref.shape[-1])
     gate = jnp.dot(rows, gate_ref[...], preferred_element_type=F32)
     up = jnp.dot(rows, up_ref[...], preferred_element_type=F32)
     hidden = (jax.nn.silu(gate) * up).astype(BF16)
-    term = jnp.dot(hidden, down_ref[...], preferred_element_type=F32)
-
-    @pl.when(step == 0)
-    def _():
-        total[...] = term
-
-    @pl.when(step > 0)
-    def _():
-        total[...] += term
-
-    @pl.when(step == pl.num_programs(0) - 1)
-    def _():
-        out_ref[...] = total[...].astype(BF16)
+    out = jnp.dot(hidden, down_ref[...], preferred_element_type=F32).astype(BF16)
+    out_ref[...] = out.reshape(out_ref.shape)
 
 
 def run_expert(rows, gate, up, down):
-    count, width = rows.shape
-    hidden = gate.shape[1]
-    block = 256
+    width, hidden = gate.shape
+    count = rows.size // width
     return pl.pallas_call(
         expert_kernel,
-        out_shape=jax.ShapeDtypeStruct((count, width), BF16),
-        grid=(hidden // block,),
-        in_specs=[
-            pl.BlockSpec((count, width), lambda i: (0, 0)),
-            pl.BlockSpec((width, block), lambda i: (0, i)),
-            pl.BlockSpec((width, block), lambda i: (0, i)),
-            pl.BlockSpec((block, width), lambda i: (i, 0)),
-        ],
-        out_specs=pl.BlockSpec((count, width), lambda i: (0, 0)),
-        scratch_shapes=[pltpu.VMEM((count, width), F32)],
+        out_shape=jax.ShapeDtypeStruct(rows.shape, BF16),
+        in_specs=[VMEM] * 4,
+        out_specs=VMEM,
         compiler_params=pltpu.CompilerParams(vmem_limit_bytes=24 * 1024 * 1024),
         cost_estimate=pl.CostEstimate(
             flops=6 * count * width * hidden,
@@ -213,6 +291,30 @@
             transcendentals=count * hidden,
         ),
     )(rows, gate, up, down)
+
+
+def combine_kernel(rows_ref, residual_ref, weight_ref, out_ref):
+    rows = rows_ref[...].reshape(-1, rows_ref.shape[-1])
+    weight = weight_ref[...]
+    high = weight.astype(BF16)
+    rest = weight - high.astype(F32)
+    middle = rest.astype(BF16)
+    low = (rest - middle.astype(F32)).astype(BF16)
+    count = weight.shape[0]
+    three = jnp.dot(jnp.concatenate([high, middle, low], 0), rows, preferred_element_type=F32)
+    routed = three[:count] + (three[count : 2 * count] + three[2 * count :])
+    mixed = (residual_ref[...].astype(F32) + routed).astype(BF16)
+    out_ref[...] = mixed.reshape(out_ref.shape)
+
+
+def combine_rows(rows, residual, weight, shape):
+    return pl.pallas_call(
+        combine_kernel,
+        out_shape=jax.ShapeDtypeStruct(shape, BF16),
+        in_specs=[VMEM] * 3,
+        out_specs=VMEM,
+        compiler_params=pltpu.CompilerParams(vmem_limit_bytes=8 * 1024 * 1024),
+    )(rows, residual, weight)
 
 
 def local(
@@ -242,30 +344,23 @@
     grid_rows = lax.axis_size("erow")
     grid_cols = lax.axis_size("ecol")
     own_rows = local_req * step_count
-    own = hidden_in.reshape(own_rows, model_width)
     gathered = lax.all_to_all(
-        jnp.broadcast_to(own[None], (grid_cols, own_rows, model_width)),
-        "ecol",
-        split_axis=0,
-        concat_axis=0,
-        tiled=True,
-    ).reshape(grid_cols * own_rows, model_width)
+        spread(hidden_in, grid_cols), "ecol", split_axis=0, concat_axis=0, tiled=True
+    ).reshape(grid_cols * local_req, step_count, model_width)
     memory = kda_state.reshape(kda_state.shape[0], head_size, head_size)
     weights = (
         query_weight,
         key_weight,
         value_weight,
-        jnp.broadcast_to(beta_weight, (model_width, head_size)),
-        decay_down,
-        gate_down,
-        decay_up,
-        gate_lift,
+        beta_weight.reshape(1, model_width),
         decay_log.reshape(1, 1),
         decay_bias.reshape(1, head_size),
         norm_gain.reshape(1, head_size),
-        output_weight,
-    )
-    partial, keys, updates = attend(gathered, weights, memory, step_count)
+    )
+    fetched = (decay_down, gate_down, decay_up, gate_lift, output_weight)
+    partial, keys, updates = attend(
+        gathered, weights, fetched, memory.astype(BF16), step_count
+    )
     terms = lax.all_to_all(
         partial.reshape(grid_cols, own_rows, model_width),
         "ecol",
@@ -274,9 +369,6 @@
         tiled=True,
     )
     new_state = new_memory(keys, updates, memory, step_count).reshape(kda_state.shape)
-    attended = jnp.sum(terms.astype(F32), 0)
-    residual = (own.astype(F32) + attended).astype(BF16)
-    normed = (rms_scale(residual.astype(F32)) * ffn_gain).astype(BF16)
     device_count = grid_rows * grid_cols
     pick_count = expert_ids.shape[-1]
     capacity = max(2, 2 * own_rows * pick_count // device_count)
@@ -289,29 +381,27 @@
     matches = (slot_of[:, None] == jnp.arange(slots_total, dtype=jnp.int32)[None, :]).reshape(
         own_rows, pick_count, slots_total
     )
-    placing = jnp.any(matches, 1).astype(BF16)
+    placing = jnp.any(matches, 1).astype(BF16).T
     combine = jnp.sum(jnp.where(matches, flat_weights.reshape(own_rows, pick_count, 1), 0.0), 1)
-    outgoing = lax.dot_general(
-        placing, normed, (((0,), (0,)), ((), ())), preferred_element_type=F32
-    ).astype(BF16)
+    residual, outgoing = join(
+        terms,
+        hidden_in,
+        ffn_gain.reshape(1, model_width),
+        placing,
+        (device_count, capacity, model_width),
+    )
     received = lax.all_to_all(
-        outgoing.reshape(device_count, capacity, model_width),
+        outgoing,
         ("erow", "ecol"),
         split_axis=0,
         concat_axis=0,
         tiled=True,
     )
-    produced = run_expert(
-        received.reshape(-1, model_width), expert_gate[0], expert_up[0], expert_down[0]
-    )
+    produced = run_expert(received, expert_gate[0], expert_up[0], expert_down[0])
     returned = lax.all_to_all(
         produced.reshape(received.shape), ("erow", "ecol"), split_axis=0, concat_axis=0, tiled=True
     )
-    returned = returned.reshape(slots_total, model_width)
-    routed = jnp.dot(combine, returned.astype(F32), precision=HIGHEST)
-    mixed = (
-        (residual.astype(F32) + routed).astype(BF16).reshape(local_req, step_count, model_width)
-    )
+    mixed = combine_rows(returned, residual, combine, hidden_in.shape)
     return (mixed, new_state)
 
 

time: 136 us -> 117 us (0.86)
  local copies, waits for them, and re-layouts: 23.4 us -> 1.26 us
  Pallas kernels: 19.3 us -> 23.6 us
  other arithmetic: 1.49 us -> 4.45 us
  waiting for transfers between devices: 44.3 us -> 41.7 us
    unnamed x56 -> x34, local copies, waits for them, and re-layouts: 17.4 us -> 0.97 us
    reshape x6 -> x1, local copies, waits for them, and re-layouts: 4.29 us -> 0.01 us  [local(): ffn_gain.reshape(1, model_width)]
    convert_element_type x0 -> x2, other arithmetic: none -> 4.01 us  [the longest x1 4.01 us: local(): memory.astype(BF16)]
    all_to_all x1, waiting for transfers between devices: 17.9 us -> 14.6 us  [local(): lax.all_to_all(spread(hidden_in, grid_cols), 'ecol', split_axis=0, concat...]
    pallas_call x1, Pallas kernels: 4.54 us -> 6.71 us  [attend(): pl.pallas_call(functools.partial(attend_kernel, steps), out_shape=(jax.Sh...]
    broadcast_in_dim x2 -> x0, local copies, waits for them, and re-layouts: 1.45 us -> none  [the longest x1 1.09 us: local(): jnp.broadcast_to(own[None], (grid_cols, own_rows, model_width))]
    pallas_call x1 -> x4, Pallas kernels: 7.13 us -> 7.96 us  [the longest x1 5.03 us: run_expert(): pl.pallas_call(expert_kernel, out_shape=jax.ShapeDtypeStruct(rows.shape,...]
  transfers between devices with their start and end apart: 3 -> 3, of which waited for: 3 -> 3; matrix products, arithmetic and copies ran while one was open for 1% -> 4% of each run, Pallas kernels for 6% -> 8%
where the time goes in v2:
time: 117 us; the launch traced here: 116 us
  waiting for transfers between devices  41.7 us (36%)
  blocking collectives  27.9 us (24%)
  Pallas kernels  23.6 us (20%)
  starting transfers between devices  15.7 us (13%)
  other arithmetic  4.45 us (4%)
  between operations  1.58 us (1%)
  local copies, waits for them, and re-layouts  1.26 us (1%)
    all_to_all x1, blocking collectives, local(): lax.all_to_all(outgoing, ('erow', 'ecol'), split_axis=0, concat_axis=0, t...  27.9 us
    all_to_all x1, waiting for transfers between devices, local(): lax.all_to_all(partial.reshape(grid_cols, own_rows, model_width), 'ecol',...  15.9 us
    all_to_all x1, waiting for transfers between devices, local(): lax.all_to_all(spread(hidden_in, grid_cols), 'ecol', split_axis=0, concat...  14.6 us
    all_to_all x1, waiting for transfers between devices, local(): lax.all_to_all(produced.reshape(received.shape), ('erow', 'ecol'), split_...  11.3 us
    pallas_call x1, Pallas kernels, new_memory(): pl.pallas_call(functools.partial(state_kernel, steps), out_shape=jax.Shap...  8.97 us
    all_to_all x1, starting transfers between devices, local(): lax.all_to_all(spread(hidden_in, grid_cols), 'ecol', split_axis=0, concat...  7.13 us
    pallas_call x1, Pallas kernels, attend(): pl.pallas_call(functools.partial(attend_kernel, steps), out_shape=(jax.Sh...  6.71 us
    pallas_call x1, Pallas kernels, run_expert(): pl.pallas_call(expert_kernel, out_shape=jax.ShapeDtypeStruct(rows.shape,...  5.03 us
  transfers between devices with their start and end apart: 3, of which 3 were waited for; matrix products, arithmetic and copies ran while one was open for 4% of the time, Pallas kernels for 8%

profile of v2, /device:TPU:0, one launch (start us, length us, event | category | flops | bytes accessed | tf_op | source)
XLA Modules:
  0.0 116.3 jit_solution(7132701647873304404)
XLA Ops:
  0.6 0.0 copy-start.3
  0.6 0.9 copy-done.3
  1.5 1.2 %shard_map.203 = bf16[16,4,4,2304]{3,2,1,0:T(4,128)(2,1)} custom-call(bf16[4,4,2304]{2,1,0:T(4,128)(2,1)S(1)} %copy-done.3), custom_call_target="tpu_custom_call" | custom-call | tf_op jit(solution)/shard_map/pallas_call | solution.py:40
  2.7 7.1 %all-to-all-start = ((bf16[16,4,4,2304]{3,2,1,0:T(4,128)(2,1)}), bf16[16,4,4,2304]{3,2,1,0:T(4,128)(2,1)S(1)}, u32[]{:S(2)}, u32[]{:S(2)}) async-start(bf16[16,4,4,2304]{3,2,1,0:T(4,128)(2,1)} %shard_map.203), calls=%async_computation | async-start | bytes 2359296 | tf_op jit(solution)/shard_map/all_to_all | solution.py:347
  10.5 0.0 copy-start
  10.5 0.0 copy-start.1
  10.5 0.0 copy-start.2
  10.5 0.0 copy-start.5
  10.5 0.0 copy-start.6
  10.5 0.0 copy-start.7
  10.6 4.0 %bitcast_convert_fusion.mem_hbm = bf16[64,128,128]{2,1,0:T(8,128)(2,1)} fusion(f32[64,1,128,128]{3,2,1,0:T(8,128)} %param.21), kind=kLoop, calls=%fused_computation.7 | loop fusion | flops 1048576 | bytes 6291456 | tf_op jit(solution)/shard_map/convert_element_type | solution.py:362
  14.6 14.6 %all-to-all-done = bf16[16,4,4,2304]{3,2,1,0:T(4,128)(2,1)S(1)} async-done(((bf16[16,4,4,2304]{3,2,1,0:T(4,128)(2,1)}), bf16[16,4,4,2304]{3,2,1,0:T(4,128)(2,1)S(1)}, u32[]{:S(2)}, u32[]{:S(2)}) %all-to-all-start) | async-done | bytes 1179680 | tf_op jit(solution)/shard_map/all_to_all | solution.py:347
  29.1 0.0 copy-done
  29.1 0.0 copy-done.1
  29.1 0.0 copy-done.2
  29.2 0.0 copy-done.5
  29.2 0.0 copy-done.6
  29.2 0.0 copy-done.7
  29.2 6.7 %shard_map.204 = (bf16[256,2304]{1,0:T(8,128)(2,1)}, f32[512,128]{1,0:T(8,128)}, f32[256,128]{1,0:T(8,128)}) custom-call(bf16[64,4,2304]{2,1,0:T(4,128)(2,1)S(1)} %bitcast.18, bf16[2304,128]{1,0:T(8,128)(2,1)S(1)} %copy-done, bf16[2304,128]{1,0:T(8,128)(2,1)S(1)} %copy-done.1, bf16[2304,128]{1,0:T(8,128)(2,1)S(1)} %copy-done.2, ...), custom_call_target="tpu_custom_call" | custom-call | flops 1090519040 | bytes 10000000 | tf_op jit(solution)/shard_map/pallas_call | solution.py:182
  35.9 0.0 copy-start.8
  35.9 0.0 copy-start.9
  35.9 0.0 copy-start.4
  35.9 3.8 %all-to-all-start.1 = ((bf16[16,16,2304]{2,1,0:T(8,128)(2,1)}), bf16[16,16,2304]{2,1,0:T(8,128)(2,1)S(1)}, u32[]{:S(2)}, u32[]{:S(2)}) async-start(bf16[16,16,2304]{2,1,0:T(8,128)(2,1)} %bitcast.6), calls=%async_computation.1 | async-start | bytes 2359296 | tf_op jit(solution)/shard_map/all_to_all | solution.py:364
  39.8 0.0 copy-done.8
  39.8 0.1 eq.29
  39.9 0.2 convert_reduce_fusion
  40.1 0.1 reduce_sum.21
  40.2 0.1 fusion
  40.3 0.1 copy.24
  40.4 0.0 copy-done.9
  40.5 15.9 %all-to-all-done.1.terms_ref = bf16[16,16,2304]{2,1,0:T(8,128)(2,1)S(1)} async-done(((bf16[16,16,2304]{2,1,0:T(8,128)(2,1)}), bf16[16,16,2304]{2,1,0:T(8,128)(2,1)S(1)}, u32[]{:S(2)}, u32[]{:S(2)}) %all-to-all-start.1) | async-done | bytes 1179680 | tf_op jit(solution)/shard_map/all_to_all | solution.py:364
  56.3 0.0 slice-start
  56.3 0.0 slice-start.2
  56.4 0.0 slice-start.4
  56.4 0.0 copy-done.4
  56.4 0.0 slice-start.1
  56.4 0.0 slice-start.3
  56.4 0.0 slice-start.5
  56.4 0.8 shard_map.205
  57.1 27.9 %all_to_all.20.rows_ref = bf16[128,2,2304]{2,1,0:T(2,128)(2,1)S(1)} all-to-all(bf16[128,2,2304]{2,1,0:T(2,128)(2,1)S(1)} %get-tuple-element.8), channel_id=1, replica_groups=mesh['erow'=8,'ecol'=16] {'erow','ecol'}, dimensions={0} | all-to-all | bytes 2359296 | tf_op jit(solution)/shard_map/all_to_all | solution.py:393
  85.0 0.0 slice-done
  85.0 0.0 slice-done.2
  85.0 0.0 slice-done.4
  85.0 0.0 slice-done.1
  85.0 0.0 slice-done.3
  85.0 0.0 slice-done.5
  85.1 5.0 %shard_map.206 = bf16[128,2,2304]{2,1,0:T(2,128)(2,1)} custom-call(bf16[128,2,2304]{2,1,0:T(2,128)(2,1)S(1)} %all_to_all.20.rows_ref, bf16[2304,1024]{1,0:T(8,128)(2,1)S(1)} %bitcast.21, bf16[2304,1024]{1,0:T(8,128)(2,1)S(1)} %bitcast.24, bf16[1024,2304]{1,0:T(8,128)(2,1)S(1)} %bitcast.27), custom_call_target="tpu_custom_call" | custom-call | flops 3623878656 | bytes 16515072 | tf_op jit(solution)/shard_map/pallas_call | solution.py:282
  90.1 0.0 copy-start.10
  90.1 4.8 %all-to-all-start.3 = ((bf16[128,2,2304]{2,1,0:T(2,128)(2,1)}), bf16[128,2,2304]{2,1,0:T(2,128)(2,1)S(1)}, u32[]{:S(2)}, u32[]{:S(2)}) async-start(bf16[128,2,2304]{2,1,0:T(2,128)(2,1)} %shard_map.206), calls=%async_computation.3 | async-start | bytes 2359296 | tf_op jit(solution)/shard_map/all_to_all | solution.py:401
  94.9 0.0 copy-done.10
  94.9 0.1 select_reduce_fusion.weight_ref
  95.0 9.0 %shard_map.208 = f32[64,128,128]{2,1,0:T(8,128)} custom-call(f32[512,128]{1,0:T(8,128)} %get-tuple-element.10.keys_ref, f32[256,128]{1,0:T(8,128)} %get-tuple-element.11.upd_ref, f32[64,128,128]{2,1,0:T(8,128)} %bitcast.32), custom_call_target="tpu_custom_call" | custom-call | flops 9437184 | bytes 8388608 | tf_op jit(solution)/shard_map/pallas_call | solution.py:224
  104.0 11.3 %all-to-all-done.3.rows_ref = bf16[128,2,2304]{2,1,0:T(2,128)(2,1)S(1)} async-done(((bf16[128,2,2304]{2,1,0:T(2,128)(2,1)}), bf16[128,2,2304]{2,1,0:T(2,128)(2,1)S(1)}, u32[]{:S(2)}, u32[]{:S(2)}) %all-to-all-start.3) | async-done | bytes 1179680 | tf_op jit(solution)/shard_map/all_to_all | solution.py:401
  115.3 1.0 shard_map.207
  (7 shorter events, 0.0 us)
Async XLA Ops:
  0.6 0.9 copy-start.3
  2.7 26.4 %all-to-all-start = ((bf16[16,4,4,2304]{3,2,1,0:T(4,128)(2,1)}), bf16[16,4,4,2304]{3,2,1,0:T(4,128)(2,1)S(1)}, u32[]{:S(2)}, u32[]{:S(2)}) async-start(bf16[16,4,4,2304]{3,2,1,0:T(4,128)(2,1)} %shard_map.203), calls=%async_computation | async-start | bytes 2359296 | tf_op jit(solution)/shard_map/all_to_all | solution.py:347
  10.5 18.7 %copy-start = (bf16[2304,128]{1,0:T(8,128)(2,1)S(1)}, bf16[2304,128]{1,0:T(8,128)(2,1)}, u32[]{:S(2)}) copy-start(bf16[2304,128]{1,0:T(8,128)(2,1)} %wq_ref.1) | copy-start | bytes 1769476
  10.5 18.6 %copy-start.1 = (bf16[2304,128]{1,0:T(8,128)(2,1)S(1)}, bf16[2304,128]{1,0:T(8,128)(2,1)}, u32[]{:S(2)}) copy-start(bf16[2304,128]{1,0:T(8,128)(2,1)} %wk_ref.1) | copy-start | bytes 1769476
  10.5 18.6 %copy-start.2 = (bf16[2304,128]{1,0:T(8,128)(2,1)S(1)}, bf16[2304,128]{1,0:T(8,128)(2,1)}, u32[]{:S(2)}) copy-start(bf16[2304,128]{1,0:T(8,128)(2,1)} %wv_ref.1) | copy-start | bytes 1769476
  10.5 18.6 %copy-start.5 = (bf16[2304,1]{0,1:T(2,128)(2,1)S(1)}, bf16[2304,1]{0,1:T(2,128)(2,1)}, u32[]{:S(2)}) copy-start(bf16[2304,1]{0,1:T(2,128)(2,1)} %param.25) | copy-start | bytes 13828
  10.5 18.6 %copy-start.6 = (f32[128]{0:T(128)S(1)}, f32[128]{0:T(128)}, u32[]{:S(2)}) copy-start(f32[128]{0:T(128)} %param.29) | copy-start | bytes 1540
  10.5 18.6 %copy-start.7 = (f32[128]{0:T(128)S(1)}, f32[128]{0:T(128)}, u32[]{:S(2)}) copy-start(f32[128]{0:T(128)} %param.32) | copy-start | bytes 1540
  35.9 3.9 %copy-start.8 = (s32[4,4,8]{2,1,0:T(4,128)S(1)}, s32[4,4,8]{2,1,0:T(4,128)}, u32[]{:S(2)}) copy-start(s32[4,4,8]{2,1,0:T(4,128)} %param.35) | copy-start | bytes 1540
  35.9 4.5 %copy-start.9 = (f32[2304]{0:T(1024)S(1)}, f32[2304]{0:T(1024)}, u32[]{:S(2)}) copy-start(f32[2304]{0:T(1024)} %param.34) | copy-start | bytes 27652
  35.9 20.4 %copy-start.4 = (bf16[4,4,2304]{2,1,0:T(4,128)(2,1)S(1)}, bf16[4,4,2304]{2,1,0:T(4,128)(2,1)}, u32[]{:S(2)}) copy-start(bf16[4,4,2304]{2,1,0:T(4,128)(2,1)} %own_ref.1) | copy-start | bytes 221188
  35.9 20.4 %all-to-all-start.1 = ((bf16[16,16,2304]{2,1,0:T(8,128)(2,1)}), bf16[16,16,2304]{2,1,0:T(8,128)(2,1)S(1)}, u32[]{:S(2)}, u32[]{:S(2)}) async-start(bf16[16,16,2304]{2,1,0:T(8,128)(2,1)} %bitcast.6), calls=%async_computation.1 | async-start | bytes 2359296 | tf_op jit(solution)/shard_map/all_to_all | solution.py:364
  56.3 28.7 %slice-start = ((s8[4718592]{0:T(1024)(128)(4,1)}), s8[4194304]{0:T(1024)(128)(4,1)S(1)}, s32[]{:S(2)}) async-start(s8[4718592]{0:T(1024)(128)(4,1)} %bitcast.19), calls=%async_computation.4 | async-start | bytes 8388608
  56.3 28.7 %slice-start.2 = ((s8[4718592]{0:T(1024)(128)(4,1)}), s8[4194304]{0:T(1024)(128)(4,1)S(1)}, s32[]{:S(2)}) async-start(s8[4718592]{0:T(1024)(128)(4,1)} %bitcast.22), calls=%async_computation.6 | async-start | bytes 8388608
  56.4 28.7 %slice-start.4 = ((s8[4718592]{0:T(1024)(128)(4,1)}), s8[4194304]{0:T(1024)(128)(4,1)S(1)}, s32[]{:S(2)}) async-start(s8[4718592]{0:T(1024)(128)(4,1)} %bitcast.25), calls=%async_computation.8 | async-start | bytes 8388608
  56.4 28.7 %slice-start.1 = ((s8[4718592]{0:T(1024)(128)(4,1)}), s8[524288]{0:T(1024)(128)(4,1)S(1)}, s32[]{:S(2)}) async-start(s8[4718592]{0:T(1024)(128)(4,1)} %bitcast.19), calls=%async_computation.5 | async-start | bytes 1048576
  56.4 28.7 %slice-start.3 = ((s8[4718592]{0:T(1024)(128)(4,1)}), s8[524288]{0:T(1024)(128)(4,1)S(1)}, s32[]{:S(2)}) async-start(s8[4718592]{0:T(1024)(128)(4,1)} %bitcast.22), calls=%async_computation.7 | async-start | bytes 1048576
  56.4 28.7 %slice-start.5 = ((s8[4718592]{0:T(1024)(128)(4,1)}), s8[524288]{0:T(1024)(128)(4,1)S(1)}, s32[]{:S(2)}) async-start(s8[4718592]{0:T(1024)(128)(4,1)} %bitcast.25), calls=%async_computation.9 | async-start | bytes 1048576
  90.1 4.8 %copy-start.10 = (f32[4,4,8]{2,1,0:T(4,128)S(1)}, f32[4,4,8]{2,1,0:T(4,128)}, u32[]{:S(2)}) copy-start(f32[4,4,8]{2,1,0:T(4,128)} %param.36) | copy-start | bytes 1540
  90.1 25.2 %all-to-all-start.3 = ((bf16[128,2,2304]{2,1,0:T(2,128)(2,1)}), bf16[128,2,2304]{2,1,0:T(2,128)(2,1)S(1)}, u32[]{:S(2)}, u32[]{:S(2)}) async-start(bf16[128,2,2304]{2,1,0:T(2,128)(2,1)} %shard_map.206), calls=%async_computation.3 | async-start | bytes 2359296 | tf_op jit(solution)/shard_map/all_to_all | solution.py:401

commit v3 on v2

--- a/solution.py
+++ b/solution.py
@@ -1,4 +1,5 @@
 import functools
+import math
 
 import jax
 import jax.numpy as jnp
@@ -26,30 +27,80 @@
     return vectors * lax.rsqrt(jnp.mean(vectors * vectors, -1, keepdims=True) + EPSILON)
 
 
-def spread_kernel(in_ref, out_hbm, send):
-    copies = [
-        pltpu.make_async_copy(in_ref, out_hbm.at[i], send.at[i]) for i in range(out_hbm.shape[0])
-    ]
-    for copy in copies:
-        copy.start()
-    for copy in copies:
-        copy.wait()
-
-
-def spread(hidden, count):
-    return pl.pallas_call(
-        spread_kernel,
-        out_shape=pltpu.HBM((count, *hidden.shape), hidden.dtype),
+def own_kernel(in_ref, own_ref):
+    own_ref[...] = in_ref[...].reshape(own_ref.shape)
+
+
+def own_rows(hidden):
+    reqs, steps, width = hidden.shape
+    return pl.pallas_call(
+        own_kernel,
+        out_shape=jax.ShapeDtypeStruct((reqs * steps, width), BF16),
         in_specs=[VMEM],
-        out_specs=HBM,
-        scratch_shapes=[pltpu.SemaphoreType.DMA((count,))],
+        out_specs=VMEM,
         compiler_params=pltpu.CompilerParams(vmem_limit_bytes=2 * 1024 * 1024),
     )(hidden)
 
 
+def collect_kernel(own_ref, *refs):
+    *blocks, out_ref = refs
+    rows, width = own_ref.shape
+    out_ref[pl.ds(0, rows), :] = own_ref[...]
+    for i, block in enumerate(blocks):
+        out_ref[pl.ds(rows * (i + 1), rows), :] = block[...].reshape(rows, width)
+
+
+def collect(own, blocks):
+    rows, width = own.shape
+    return pl.pallas_call(
+        collect_kernel,
+        out_shape=jax.ShapeDtypeStruct(((1 + len(blocks)) * rows, width), BF16),
+        in_specs=[VMEM] * (1 + len(blocks)),
+        out_specs=VMEM,
+        compiler_params=pltpu.CompilerParams(vmem_limit_bytes=4 * 1024 * 1024),
+        cost_estimate=pl.CostEstimate(
+            flops=40_000_000_000, bytes_accessed=40_000_000, transcendentals=0
+        ),
+    )(own, *blocks)
+
+
+ORDER = (2, 3, 1)
+
+
+def gather_rows(hidden, grid_rows, grid_cols):
+    side = math.isqrt(grid_cols)
+
+    def shifted(array, first, amount):
+        pairs = []
+        for row in range(grid_rows):
+            for col in range(grid_cols):
+                high, low = col // side, col % side
+                if (row % 2 == 0) == first:
+                    low = (low + amount) % side
+                else:
+                    high = (high + amount) % side
+                pairs.append((row * grid_cols + col, row * grid_cols + high * side + low))
+        return lax.ppermute(array, ("erow", "ecol"), pairs)
+
+    near = collect(own_rows(hidden), [shifted(hidden, True, amount) for amount in ORDER])
+    return [near] + [shifted(near, False, amount) for amount in ORDER]
+
+
+def place_of(piece, block, side):
+    row, col = lax.axis_index("erow"), lax.axis_index("ecol")
+    later, earlier = (0, *ORDER)[piece], (0, *ORDER)[block]
+    even = lax.rem(row, 2) == 0
+    high = lax.div(col, side) + side - jnp.where(even, later, earlier)
+    low = lax.rem(col, side) + side - jnp.where(even, earlier, later)
+    return lax.rem(high, side) * side + lax.rem(low, side)
+
+
 def attend_kernel(
     steps,
-    tok_ref,
+    piece0_ref,
+    piece1_ref,
+    piece2_ref,
+    piece3_ref,
     wq_ref,
     wk_ref,
     wv_ref,
@@ -57,43 +108,34 @@
     dl_ref,
     db_ref,
     ng_ref,
-    dd_hbm,
-    gd_hbm,
-    du_hbm,
-    gl_hbm,
-    wo_hbm,
-    mem_hbm,
-    part_ref,
-    keys_hbm,
-    upd_hbm,
-    stage,
-    probe,
-    reply,
-    keys_ref,
-    upd_ref,
     dd_ref,
     gd_ref,
     du_ref,
     gl_ref,
     wo_ref,
     mem_ref,
+    part_ref,
+    keys_hbm,
+    upd_hbm,
+    tok_ref,
+    stage,
+    probe,
+    reply,
+    keys_ref,
+    upd_ref,
     sems,
 ):
     width, hk = wq_ref.shape
     rows = stage.shape[1]
     reqs = rows // steps
-    pairs = (
-        (dd_hbm, dd_ref),
-        (gd_hbm, gd_ref),
-        (du_hbm, du_ref),
-        (gl_hbm, gl_ref),
-        (mem_hbm, mem_ref),
-        (wo_hbm, wo_ref),
-    )
-    loads = [pltpu.make_async_copy(src, dst, sems.at[i]) for i, (src, dst) in enumerate(pairs)]
-    for load in loads:
-        load.start()
-    tok = tok_ref[...].reshape(rows, width)
+    pieces = (piece0_ref, piece1_ref, piece2_ref, piece3_ref)
+    side = len(pieces)
+    size = rows // side**2
+    for j, piece in enumerate(pieces):
+        for i in range(side):
+            start = pl.multiple_of(place_of(j, i, side) * size, size)
+            tok_ref[pl.ds(start, size), :] = piece[pl.ds(size * i, size), :]
+    tok = tok_ref[...]
 
     def project(weight):
         return jnp.dot(tok, weight, preferred_element_type=F32)
@@ -102,12 +144,10 @@
     value = project(wv_ref[...])
     beta = lax.dot_general(
         tok,
-        jnp.broadcast_to(wb_ref[...], (hk, width)),
+        jnp.broadcast_to(wb_ref[...], (8, width)),
         (((1,), (1,)), ((), ())),
         preferred_element_type=F32,
     )
-    for load in loads[:4]:
-        load.wait()
     low = project(jnp.concatenate([dd_ref[...], gd_ref[...]], axis=1)).astype(BF16)
     decay_pre = jnp.dot(low[:, : dd_ref.shape[1]], du_ref[...], preferred_element_type=F32)
     decay_pre = decay_pre + db_ref[...]
@@ -118,7 +158,7 @@
     stage[0] = unit_rows(qk[:, :hk]) * hk ** (-0.5)
     stage[1] = unit_rows(qk[:, hk:])
     stage[2] = value
-    stage[3] = jax.nn.sigmoid(beta)
+    stage[3] = jnp.broadcast_to(jax.nn.sigmoid(beta[:, :1]), (rows, hk))
     stage[4] = jnp.exp(-jnp.exp(dl_ref[...]) * softplus)
 
     def at(kind, t):
@@ -133,16 +173,14 @@
         probe[pl.ds(t, reqs, stride=2 * steps), :] = start[t] * k[t]
         probe[pl.ds(steps + t, reqs, stride=2 * steps), :] = start[t] * q[t]
 
-    loads[4].wait()
-
     def one_request(r, carry):
         at_rows = pl.ds(pl.multiple_of(r * 2 * steps, 2 * steps), 2 * steps)
         reply[at_rows, :] = jnp.dot(
-            probe[at_rows, :].astype(BF16), mem_ref[r], preferred_element_type=F32
+            probe[at_rows, :].astype(BF16), mem_ref[r].astype(BF16), preferred_element_type=F32
         )
         return carry
 
-    lax.fori_loop(0, reqs, one_request, 0, unroll=8)
+    lax.fori_loop(0, reqs, one_request, 0, unroll=64)
 
     decayed = []
     updates = []
@@ -163,22 +201,21 @@
         keys_ref[pl.ds(steps + t, reqs, stride=2 * steps), :] = start[-1]
         upd_ref[pl.ds(t, reqs, stride=steps), :] = updates[t]
     stores = [
-        pltpu.make_async_copy(keys_ref, keys_hbm, sems.at[6]),
-        pltpu.make_async_copy(upd_ref, upd_hbm, sems.at[7]),
+        pltpu.make_async_copy(keys_ref, keys_hbm, sems.at[0]),
+        pltpu.make_async_copy(upd_ref, upd_hbm, sems.at[1]),
     ]
     for store in stores:
         store.start()
-    loads[5].wait()
     mixed = (rms_scale(stage[0]) * ng_ref[...] * gate).astype(BF16)
     part_ref[...] = jnp.dot(mixed, wo_ref[...], preferred_element_type=F32).astype(BF16)
     for store in stores:
         store.wait()
 
 
-def attend(tokens, weights, fetched, memory, steps):
+def attend(pieces, weights, fetched, memory, steps):
     reqs, hk, _ = memory.shape
-    rows, width = reqs * steps, tokens.shape[-1]
-    fetched = [in_hbm(array) for array in (*fetched, memory)]
+    rows, width = reqs * steps, pieces[0].shape[-1]
+    fetched = [*fetched, memory]
     return pl.pallas_call(
         functools.partial(attend_kernel, steps),
         out_shape=(
@@ -186,24 +223,24 @@
             pltpu.HBM((2 * rows, hk), F32),
             pltpu.HBM((rows, hk), F32),
         ),
-        in_specs=[VMEM] * (1 + len(weights)) + [HBM] * len(fetched),
+        in_specs=[VMEM] * (len(pieces) + len(weights) + len(fetched)),
         out_specs=(VMEM, HBM, HBM),
         scratch_shapes=[
+            pltpu.VMEM((rows, width), BF16),
             pltpu.VMEM((5, rows, hk), F32),
             pltpu.VMEM((2 * rows, hk), F32),
             pltpu.VMEM((2 * rows, hk), F32),
             pltpu.VMEM((2 * rows, hk), F32),
             pltpu.VMEM((rows, hk), F32),
-            *[pltpu.VMEM(array.shape, array.dtype) for array in fetched],
-            pltpu.SemaphoreType.DMA((len(fetched) + 2,)),
+            pltpu.SemaphoreType.DMA((2,)),
         ],
-        compiler_params=pltpu.CompilerParams(vmem_limit_bytes=32 * 1024 * 1024),
+        compiler_params=pltpu.CompilerParams(vmem_limit_bytes=12 * 1024 * 1024),
         cost_estimate=pl.CostEstimate(
             flops=2 * rows * width * 7 * hk + 4 * reqs * 8 * hk * hk,
             bytes_accessed=10_000_000,
             transcendentals=0,
         ),
-    )(tokens, *weights, *fetched)
+    )(*pieces, *weights, *fetched)
 
 
 def state_kernel(steps, keys_ref, upd_ref, mem_ref, new_ref):
@@ -344,9 +381,7 @@
     grid_rows = lax.axis_size("erow")
     grid_cols = lax.axis_size("ecol")
     own_rows = local_req * step_count
-    gathered = lax.all_to_all(
-        spread(hidden_in, grid_cols), "ecol", split_axis=0, concat_axis=0, tiled=True
-    ).reshape(grid_cols * local_req, step_count, model_width)
+    pieces = gather_rows(hidden_in, grid_rows, grid_cols)
     memory = kda_state.reshape(kda_state.shape[0], head_size, head_size)
     weights = (
         query_weight,
@@ -359,7 +394,7 @@
     )
     fetched = (decay_down, gate_down, decay_up, gate_lift, output_weight)
     partial, keys, updates = attend(
-        gathered, weights, fetched, memory.astype(BF16), step_count
+        pieces, weights, fetched, memory, step_count
     )
     terms = lax.all_to_all(
         partial.reshape(grid_cols, own_rows, model_width),

time: 117 us -> 108 us (0.923)
  waiting for transfers between devices: 41.7 us -> 37.5 us
  other arithmetic: 4.45 us -> 0.45 us
  Pallas kernels: 23.6 us -> 20.2 us
  starting transfers between devices: 15.7 us -> 19.1 us
    all_to_all x1 -> x0, waiting for transfers between devices: 14.6 us -> none  [local(): lax.all_to_all(spread(hidden_in, grid_cols), 'ecol', split_axis=0, concat...]
    ppermute x0 -> x6, waiting for transfers between devices: none -> 10.6 us  [shifted(): return lax.ppermute(array, ('erow', 'ecol'), pairs)]
    ppermute x0 -> x6, starting transfers between devices: none -> 9.89 us  [shifted(): return lax.ppermute(array, ('erow', 'ecol'), pairs)]
    all_to_all x1 -> x0, starting transfers between devices: 7.13 us -> none  [local(): lax.all_to_all(spread(hidden_in, grid_cols), 'ecol', split_axis=0, concat...]
    convert_element_type x1 -> x0, other arithmetic: 4.01 us -> none  [local(): memory.astype(BF16)]
    pallas_call x1, Pallas kernels: 6.71 us -> 4.42 us  [attend(): pl.pallas_call(functools.partial(attend_kernel, steps), out_shape=(jax.Sh...]
  transfers between devices with their start and end apart: 3 -> 8, of which waited for: 3 -> 7; matrix products, arithmetic and copies ran while one was open for 4% -> 1% of each run, Pallas kernels for 8% -> 8%
where the time goes in v3:
time: 108 us
  waiting for transfers between devices  37.5 us (35%)
  blocking collectives  27.3 us (25%)
  Pallas kernels  20.2 us (19%)
  starting transfers between devices  19.1 us (18%)
  between operations  1.67 us (2%)
  local copies, waits for them, and re-layouts  1.34 us (1%)
    all_to_all x1, blocking collectives, local(): lax.all_to_all(outgoing, ('erow', 'ecol'), split_axis=0, concat_axis=0, t...  27.3 us
    all_to_all x1, waiting for transfers between devices, local(): lax.all_to_all(partial.reshape(grid_cols, own_rows, model_width), 'ecol',...  15.7 us
    all_to_all x1, waiting for transfers between devices, local(): lax.all_to_all(produced.reshape(received.shape), ('erow', 'ecol'), split_...  11.3 us
    ppermute x6, waiting for transfers between devices, shifted(): return lax.ppermute(array, ('erow', 'ecol'), pairs)  10.6 us
    ppermute x6, starting transfers between devices, shifted(): return lax.ppermute(array, ('erow', 'ecol'), pairs)  9.89 us
    pallas_call x1, Pallas kernels, new_memory(): pl.pallas_call(functools.partial(state_kernel, steps), out_shape=jax.Shap...  8.97 us
    pallas_call x1, Pallas kernels, run_expert(): pl.pallas_call(expert_kernel, out_shape=jax.ShapeDtypeStruct(rows.shape,...  5.01 us
    all_to_all x1, starting transfers between devices, local(): lax.all_to_all(produced.reshape(received.shape), ('erow', 'ecol'), split_...  4.76 us
  transfers between devices with their start and end apart: 8, of which 7 were waited for; matrix products, arithmetic and copies ran while one was open for 1% of the time, Pallas kernels for 8%

profile of v3, /device:TPU:0, one launch (start us, length us, event | category | flops | bytes accessed | tf_op | source)
XLA Modules:
  0.0 107.6 jit_solution(5378038111063566526)
XLA Ops:
  0.6 3.2 %collective-permute-start.1 = (bf16[4,4,2304]{2,1,0:T(4,128)(2,1)}, bf16[4,4,2304]{2,1,0:T(4,128)(2,1)S(1)}, u32[]{:S(2)}, u32[]{:S(2)}) collective-permute-start(bf16[4,4,2304]{2,1,0:T(4,128)(2,1)} %own_ref.1), channel_id=1, source_target_pairs={{0,3},{1,0},{2,1},{3,2},{4,7},{5,4},{6,5},{7,6},{8,11},{9,8},{10,9... | collective-permute-start | bytes 221192 | tf_op jit(solution)/shard_map/ppermute | solution.py:83
  3.8 0.6 collective-permute-start
  4.4 1.0 collective-permute-start.2
  5.4 0.9 copy-done.7
  6.3 0.0 copy-start.1
  6.3 0.0 copy-start.2
  6.4 0.0 copy-start.3
  6.4 0.0 copy-start.4
  6.4 0.0 copy-start.5
  6.4 0.0 copy-start.6
  6.4 0.0 copy-start.9
  6.4 0.0 copy-start.10
  6.4 0.0 copy-start.11
  6.4 0.0 copy-start.12
  6.4 0.0 copy-start.13
  6.5 0.0 collective-permute-done.1.refs_1_
  6.5 3.4 %collective-permute-done.refs_0_ = bf16[4,4,2304]{2,1,0:T(4,128)(2,1)S(1)} collective-permute-done((bf16[4,4,2304]{2,1,0:T(4,128)(2,1)}, bf16[4,4,2304]{2,1,0:T(4,128)(2,1)S(1)}, u32[]{:S(2)}, u32[]{:S(2)}) %collective-permute-start) | collective-permute-done | bytes 73760 | tf_op jit(solution)/shard_map/ppermute | solution.py:83
  9.9 0.7 collective-permute-done.2.refs_2_
  10.7 1.6 %collective-permute-start.5 = (bf16[64,2304]{1,0:T(8,128)(2,1)S(1)}, bf16[64,2304]{1,0:T(8,128)(2,1)S(1)}, u32[]{:S(2)}, u32[]{:S(2)}) collective-permute-start(bf16[64,2304]{1,0:T(8,128)(2,1)S(1)} %shard_map.204.piece0_ref), channel_id=1, source_target_pairs={{0,4},{1,5},{2,6},{3,7},{4,8},{5,9},{6,10},{7,11},{8,12},{9,13},{1... | collective-permute-start | bytes 884744 | tf_op jit(solution)/shard_map/ppermute | solution.py:83
  12.3 1.7 %collective-permute-start.4 = (bf16[64,2304]{1,0:T(8,128)(2,1)S(1)}, bf16[64,2304]{1,0:T(8,128)(2,1)S(1)}, u32[]{:S(2)}, u32[]{:S(2)}) collective-permute-start(bf16[64,2304]{1,0:T(8,128)(2,1)S(1)} %shard_map.204.piece0_ref), channel_id=1, source_target_pairs={{0,12},{1,13},{2,14},{3,15},{4,0},{5,1},{6,2},{7,3},{8,4},{9,5},{1... | collective-permute-start | bytes 884744 | tf_op jit(solution)/shard_map/ppermute | solution.py:83
  14.0 1.8 %collective-permute-start.3 = (bf16[64,2304]{1,0:T(8,128)(2,1)S(1)}, bf16[64,2304]{1,0:T(8,128)(2,1)S(1)}, u32[]{:S(2)}, u32[]{:S(2)}) collective-permute-start(bf16[64,2304]{1,0:T(8,128)(2,1)S(1)} %shard_map.204.piece0_ref), channel_id=1, source_target_pairs={{0,8},{1,9},{2,10},{3,11},{4,12},{5,13},{6,14},{7,15},{8,0},{9,1},... | collective-permute-start | bytes 884744 | tf_op jit(solution)/shard_map/ppermute | solution.py:83
  16.5 2.2 %collective-permute-done.5.piece3_ref = bf16[64,2304]{1,0:T(8,128)(2,1)S(1)} collective-permute-done((bf16[64,2304]{1,0:T(8,128)(2,1)S(1)}, bf16[64,2304]{1,0:T(8,128)(2,1)S(1)}, u32[]{:S(2)}, u32[]{:S(2)}) %collective-permute-start.5) | collective-permute-done | bytes 294944 | tf_op jit(solution)/shard_map/ppermute | solution.py:83
  18.7 2.7 %collective-permute-done.4.piece2_ref = bf16[64,2304]{1,0:T(8,128)(2,1)S(1)} collective-permute-done((bf16[64,2304]{1,0:T(8,128)(2,1)S(1)}, bf16[64,2304]{1,0:T(8,128)(2,1)S(1)}, u32[]{:S(2)}, u32[]{:S(2)}) %collective-permute-start.4) | collective-permute-done | bytes 294944 | tf_op jit(solution)/shard_map/ppermute | solution.py:83
  21.4 1.4 %collective-permute-done.3.piece1_ref = bf16[64,2304]{1,0:T(8,128)(2,1)S(1)} collective-permute-done((bf16[64,2304]{1,0:T(8,128)(2,1)S(1)}, bf16[64,2304]{1,0:T(8,128)(2,1)S(1)}, u32[]{:S(2)}, u32[]{:S(2)}) %collective-permute-start.3) | collective-permute-done | bytes 294944 | tf_op jit(solution)/shard_map/ppermute | solution.py:83
  22.8 0.0 copy-done.1
  22.8 0.0 copy-done.2
  22.8 0.0 copy-done.3
  22.8 0.0 copy-done.4
  22.9 0.0 copy-done.5
  22.9 0.0 copy-done.6
  22.9 0.0 copy-done.9
  22.9 0.0 copy-done.10
  22.9 0.0 copy-done.11
  22.9 0.0 copy-done.12
  22.9 0.0 copy-done.13
  22.9 0.0 copy-done
  22.9 4.4 %shard_map.205 = (bf16[256,2304]{1,0:T(8,128)(2,1)}, f32[512,128]{1,0:T(8,128)}, f32[256,128]{1,0:T(8,128)}) custom-call(bf16[64,2304]{1,0:T(8,128)(2,1)S(1)} %shard_map.204.piece0_ref, bf16[64,2304]{1,0:T(8,128)(2,1)S(1)} %collective-permute-done.3.piece1_ref, bf16[64,2304]{1,0:T(8,128)(2,1)S(1)} %collective-permute-done.4.piece2_ref, ...), custom_call_target="tpu_custom_call" | custom-call | flops 1090519040 | bytes 10000000 | tf_op jit(solution)/shard_map/pallas_call | solution.py:219
  27.4 0.0 copy-start.14
  27.4 0.0 copy-start.15
  27.4 0.0 copy-start.8
  27.4 4.5 %all-to-all-start = ((bf16[16,16,2304]{2,1,0:T(8,128)(2,1)}), bf16[16,16,2304]{2,1,0:T(8,128)(2,1)S(1)}, u32[]{:S(2)}, u32[]{:S(2)}) async-start(bf16[16,16,2304]{2,1,0:T(8,128)(2,1)} %bitcast.5), calls=%async_computation | async-start | bytes 2359296 | tf_op jit(solution)/shard_map/all_to_all | solution.py:399
  31.9 0.0 copy-done.14
  31.9 0.1 eq.29
  32.0 0.2 convert_reduce_fusion
  32.2 0.1 reduce_sum.21
  32.3 0.1 fusion
  32.4 0.0 copy-done.15
  32.4 0.1 copy.24
  32.5 15.7 %all-to-all-done.terms_ref = bf16[16,16,2304]{2,1,0:T(8,128)(2,1)S(1)} async-done(((bf16[16,16,2304]{2,1,0:T(8,128)(2,1)}), bf16[16,16,2304]{2,1,0:T(8,128)(2,1)S(1)}, u32[]{:S(2)}, u32[]{:S(2)}) %all-to-all-start) | async-done | bytes 1179680 | tf_op jit(solution)/shard_map/all_to_all | solution.py:399
  48.2 0.0 copy-done.8
  48.2 0.0 slice-start.1
  48.3 0.0 slice-start.3
  48.3 0.0 slice-start.5
  48.3 0.8 shard_map.206
  49.0 27.3 %all_to_all.15.rows_ref = bf16[128,2,2304]{2,1,0:T(2,128)(2,1)S(1)} all-to-all(bf16[128,2,2304]{2,1,0:T(2,128)(2,1)S(1)} %get-tuple-element.8), channel_id=1, replica_groups=mesh['erow'=8,'ecol'=16] {'erow','ecol'}, dimensions={0} | all-to-all | bytes 2359296 | tf_op jit(solution)/shard_map/all_to_all | solution.py:428
  76.4 0.0 slice-done
  76.4 0.0 slice-done.2
  76.4 0.0 slice-done.4
  76.4 5.0 %shard_map.207 = bf16[128,2,2304]{2,1,0:T(2,128)(2,1)} custom-call(bf16[128,2,2304]{2,1,0:T(2,128)(2,1)S(1)} %all_to_all.15.rows_ref, bf16[2304,1024]{1,0:T(8,128)(2,1)S(1)} %bitcast.20, bf16[2304,1024]{1,0:T(8,128)(2,1)S(1)} %bitcast.23, bf16[1024,2304]{1,0:T(8,128)(2,1)S(1)} %bitcast.26), custom_call_target="tpu_custom_call" | custom-call | flops 3623878656 | bytes 16515072 | tf_op jit(solution)/shard_map/pallas_call | solution.py:319
  81.4 4.8 %all-to-all-start.2 = ((bf16[128,2,2304]{2,1,0:T(2,128)(2,1)}), bf16[128,2,2304]{2,1,0:T(2,128)(2,1)S(1)}, u32[]{:S(2)}, u32[]{:S(2)}) async-start(bf16[128,2,2304]{2,1,0:T(2,128)(2,1)} %shard_map.207), calls=%async_computation.2 | async-start | bytes 2359296 | tf_op jit(solution)/shard_map/all_to_all | solution.py:436
  86.2 0.1 select_reduce_fusion.weight_ref
  86.3 9.0 %shard_map.209 = f32[64,128,128]{2,1,0:T(8,128)} custom-call(f32[512,128]{1,0:T(8,128)} %get-tuple-element.10.keys_ref, f32[256,128]{1,0:T(8,128)} %get-tuple-element.11.upd_ref, f32[64,128,128]{2,1,0:T(8,128)} %bitcast.16), custom_call_target="tpu_custom_call" | custom-call | flops 9437184 | bytes 8388608 | tf_op jit(solution)/shard_map/pallas_call | solution.py:261
  95.3 11.3 %all-to-all-done.2.rows_ref = bf16[128,2,2304]{2,1,0:T(2,128)(2,1)S(1)} async-done(((bf16[128,2,2304]{2,1,0:T(2,128)(2,1)}), bf16[128,2,2304]{2,1,0:T(2,128)(2,1)S(1)}, u32[]{:S(2)}, u32[]{:S(2)}) %all-to-all-start.2) | async-done | bytes 1179680 | tf_op jit(solution)/shard_map/all_to_all | solution.py:436
  106.6 1.0 shard_map.208
  (19 shorter events, 0.1 us)
Async XLA Ops:
  0.6 5.8 %collective-permute-start.1 = (bf16[4,4,2304]{2,1,0:T(4,128)(2,1)}, bf16[4,4,2304]{2,1,0:T(4,128)(2,1)S(1)}, u32[]{:S(2)}, u32[]{:S(2)}) collective-permute-start(bf16[4,4,2304]{2,1,0:T(4,128)(2,1)} %own_ref.1), channel_id=1, source_target_pairs={{0,3},{1,0},{2,1},{3,2},{4,7},{5,4},{6,5},{7,6},{8,11},{9,8},{10,9... | collective-permute-start | bytes 221192 | tf_op jit(solution)/shard_map/ppermute | solution.py:83
  3.8 6.1 %collective-permute-start = (bf16[4,4,2304]{2,1,0:T(4,128)(2,1)}, bf16[4,4,2304]{2,1,0:T(4,128)(2,1)S(1)}, u32[]{:S(2)}, u32[]{:S(2)}) collective-permute-start(bf16[4,4,2304]{2,1,0:T(4,128)(2,1)} %own_ref.1), channel_id=1, source_target_pairs={{0,2},{1,3},{2,0},{3,1},{4,6},{5,7},{6,4},{7,5},{8,10},{9,11},{10,... | collective-permute-start | bytes 221192 | tf_op jit(solution)/shard_map/ppermute | solution.py:83
  4.4 6.2 %collective-permute-start.2 = (bf16[4,4,2304]{2,1,0:T(4,128)(2,1)}, bf16[4,4,2304]{2,1,0:T(4,128)(2,1)S(1)}, u32[]{:S(2)}, u32[]{:S(2)}) collective-permute-start(bf16[4,4,2304]{2,1,0:T(4,128)(2,1)} %own_ref.1), channel_id=1, source_target_pairs={{0,1},{1,2},{2,3},{3,0},{4,5},{5,6},{6,7},{7,4},{8,9},{9,10},{10,1... | collective-permute-start | bytes 221192 | tf_op jit(solution)/shard_map/ppermute | solution.py:83
  5.4 0.9 copy-start.7
  6.3 16.5 %copy-start.1 = (bf16[2304,128]{1,0:T(8,128)(2,1)S(1)}, bf16[2304,128]{1,0:T(8,128)(2,1)}, u32[]{:S(2)}) copy-start(bf16[2304,128]{1,0:T(8,128)(2,1)} %wq_ref.1) | copy-start | bytes 1769476
  6.3 16.5 %copy-start.2 = (bf16[2304,128]{1,0:T(8,128)(2,1)S(1)}, bf16[2304,128]{1,0:T(8,128)(2,1)}, u32[]{:S(2)}) copy-start(bf16[2304,128]{1,0:T(8,128)(2,1)} %wk_ref.1) | copy-start | bytes 1769476
  6.4 16.5 %copy-start.3 = (bf16[2304,128]{1,0:T(8,128)(2,1)S(1)}, bf16[2304,128]{1,0:T(8,128)(2,1)}, u32[]{:S(2)}) copy-start(bf16[2304,128]{1,0:T(8,128)(2,1)} %wv_ref.1) | copy-start | bytes 1769476
  6.4 16.5 %copy-start.4 = (bf16[2304,128]{1,0:T(8,128)(2,1)S(1)}, bf16[2304,128]{1,0:T(8,128)(2,1)}, u32[]{:S(2)}) copy-start(bf16[2304,128]{1,0:T(8,128)(2,1)} %dd_ref.1) | copy-start | bytes 1769476
  6.4 16.5 %copy-start.5 = (bf16[2304,128]{1,0:T(8,128)(2,1)S(1)}, bf16[2304,128]{1,0:T(8,128)(2,1)}, u32[]{:S(2)}) copy-start(bf16[2304,128]{1,0:T(8,128)(2,1)} %gd_ref.1) | copy-start | bytes 1769476
  6.4 16.5 %copy-start.6 = (bf16[128,2304]{1,0:T(8,128)(2,1)S(1)}, bf16[128,2304]{1,0:T(8,128)(2,1)}, u32[]{:S(2)}) copy-start(bf16[128,2304]{1,0:T(8,128)(2,1)} %wo_ref.1) | copy-start | bytes 1769476
  6.4 16.5 %copy-start.9 = (bf16[128,128]{1,0:T(8,128)(2,1)S(1)}, bf16[128,128]{1,0:T(8,128)(2,1)}, u32[]{:S(2)}) copy-start(bf16[128,128]{1,0:T(8,128)(2,1)} %du_ref.1) | copy-start | bytes 98308
  6.4 16.5 %copy-start.10 = (bf16[128,128]{1,0:T(8,128)(2,1)S(1)}, bf16[128,128]{1,0:T(8,128)(2,1)}, u32[]{:S(2)}) copy-start(bf16[128,128]{1,0:T(8,128)(2,1)} %gl_ref.1) | copy-start | bytes 98308
  6.4 16.5 %copy-start.11 = (bf16[2304,1]{0,1:T(2,128)(2,1)S(1)}, bf16[2304,1]{0,1:T(2,128)(2,1)}, u32[]{:S(2)}) copy-start(bf16[2304,1]{0,1:T(2,128)(2,1)} %param.25) | copy-start | bytes 13828
  6.4 16.5 %copy-start.12 = (f32[128]{0:T(128)S(1)}, f32[128]{0:T(128)}, u32[]{:S(2)}) copy-start(f32[128]{0:T(128)} %param.29) | copy-start | bytes 1540
  6.4 16.5 %copy-start.13 = (f32[128]{0:T(128)S(1)}, f32[128]{0:T(128)}, u32[]{:S(2)}) copy-start(f32[128]{0:T(128)} %param.32) | copy-start | bytes 1540
  10.7 12.3 %copy-start = (f32[64,1,128,128]{3,2,1,0:T(8,128)S(1)}, f32[64,1,128,128]{3,2,1,0:T(8,128)}, u32[]{:S(2)}) copy-start(f32[64,1,128,128]{3,2,1,0:T(8,128)} %param.21) | copy-start | bytes 12582916
  10.7 8.0 %collective-permute-start.5 = (bf16[64,2304]{1,0:T(8,128)(2,1)S(1)}, bf16[64,2304]{1,0:T(8,128)(2,1)S(1)}, u32[]{:S(2)}, u32[]{:S(2)}) collective-permute-start(bf16[64,2304]{1,0:T(8,128)(2,1)S(1)} %shard_map.204.piece0_ref), channel_id=1, source_target_pairs={{0,4},{1,5},{2,6},{3,7},{4,8},{5,9},{6,10},{7,11},{8,12},{9,13},{1... | collective-permute-start | bytes 884744 | tf_op jit(solution)/shard_map/ppermute | solution.py:83
  12.3 9.2 %collective-permute-start.4 = (bf16[64,2304]{1,0:T(8,128)(2,1)S(1)}, bf16[64,2304]{1,0:T(8,128)(2,1)S(1)}, u32[]{:S(2)}, u32[]{:S(2)}) collective-permute-start(bf16[64,2304]{1,0:T(8,128)(2,1)S(1)} %shard_map.204.piece0_ref), channel_id=1, source_target_pairs={{0,12},{1,13},{2,14},{3,15},{4,0},{5,1},{6,2},{7,3},{8,4},{9,5},{1... | collective-permute-start | bytes 884744 | tf_op jit(solution)/shard_map/ppermute | solution.py:83
  14.0 8.8 %collective-permute-start.3 = (bf16[64,2304]{1,0:T(8,128)(2,1)S(1)}, bf16[64,2304]{1,0:T(8,128)(2,1)S(1)}, u32[]{:S(2)}, u32[]{:S(2)}) collective-permute-start(bf16[64,2304]{1,0:T(8,128)(2,1)S(1)} %shard_map.204.piece0_ref), channel_id=1, source_target_pairs={{0,8},{1,9},{2,10},{3,11},{4,12},{5,13},{6,14},{7,15},{8,0},{9,1},... | collective-permute-start | bytes 884744 | tf_op jit(solution)/shard_map/ppermute | solution.py:83
  27.4 4.5 %copy-start.14 = (s32[4,4,8]{2,1,0:T(4,128)S(1)}, s32[4,4,8]{2,1,0:T(4,128)}, u32[]{:S(2)}) copy-start(s32[4,4,8]{2,1,0:T(4,128)} %param.35) | copy-start | bytes 1540
  27.4 5.0 %copy-start.15 = (f32[2304]{0:T(1024)S(1)}, f32[2304]{0:T(1024)}, u32[]{:S(2)}) copy-start(f32[2304]{0:T(1024)} %param.34) | copy-start | bytes 27652
  27.4 20.8 %copy-start.8 = (bf16[4,4,2304]{2,1,0:T(4,128)(2,1)S(1)}, bf16[4,4,2304]{2,1,0:T(4,128)(2,1)}, u32[]{:S(2)}) copy-start(bf16[4,4,2304]{2,1,0:T(4,128)(2,1)} %own_ref.1) | copy-start | bytes 221188
  27.4 20.8 %all-to-all-start = ((bf16[16,16,2304]{2,1,0:T(8,128)(2,1)}), bf16[16,16,2304]{2,1,0:T(8,128)(2,1)S(1)}, u32[]{:S(2)}, u32[]{:S(2)}) async-start(bf16[16,16,2304]{2,1,0:T(8,128)(2,1)} %bitcast.5), calls=%async_computation | async-start | bytes 2359296 | tf_op jit(solution)/shard_map/all_to_all | solution.py:399
  48.2 28.1 %slice-start = ((s8[4718592]{0:T(1024)(128)(4,1)}), s8[4194304]{0:T(1024)(128)(4,1)S(1)}, s32[]{:S(2)}) async-start(s8[4718592]{0:T(1024)(128)(4,1)} %bitcast.18), calls=%async_computation.3 | async-start | bytes 8388608
  48.2 28.1 %slice-start.2 = ((s8[4718592]{0:T(1024)(128)(4,1)}), s8[4194304]{0:T(1024)(128)(4,1)S(1)}, s32[]{:S(2)}) async-start(s8[4718592]{0:T(1024)(128)(4,1)} %bitcast.21), calls=%async_computation.5 | async-start | bytes 8388608
  48.2 28.1 %slice-start.4 = ((s8[4718592]{0:T(1024)(128)(4,1)}), s8[4194304]{0:T(1024)(128)(4,1)S(1)}, s32[]{:S(2)}) async-start(s8[4718592]{0:T(1024)(128)(4,1)} %bitcast.24), calls=%async_computation.7 | async-start | bytes 8388608
  48.2 28.1 %slice-start.1 = ((s8[4718592]{0:T(1024)(128)(4,1)}), s8[524288]{0:T(1024)(128)(4,1)S(1)}, s32[]{:S(2)}) async-start(s8[4718592]{0:T(1024)(128)(4,1)} %bitcast.18), calls=%async_computation.4 | async-start | bytes 1048576
  48.3 28.1 %slice-start.3 = ((s8[4718592]{0:T(1024)(128)(4,1)}), s8[524288]{0:T(1024)(128)(4,1)S(1)}, s32[]{:S(2)}) async-start(s8[4718592]{0:T(1024)(128)(4,1)} %bitcast.21), calls=%async_computation.6 | async-start | bytes 1048576
  48.3 28.1 %slice-start.5 = ((s8[4718592]{0:T(1024)(128)(4,1)}), s8[524288]{0:T(1024)(128)(4,1)S(1)}, s32[]{:S(2)}) async-start(s8[4718592]{0:T(1024)(128)(4,1)} %bitcast.24), calls=%async_computation.8 | async-start | bytes 1048576
  81.4 4.8 %copy-start.16 = (f32[4,4,8]{2,1,0:T(4,128)S(1)}, f32[4,4,8]{2,1,0:T(4,128)}, u32[]{:S(2)}) copy-start(f32[4,4,8]{2,1,0:T(4,128)} %param.36) | copy-start | bytes 1540
  81.4 25.2 %all-to-all-start.2 = ((bf16[128,2,2304]{2,1,0:T(2,128)(2,1)}), bf16[128,2,2304]{2,1,0:T(2,128)(2,1)S(1)}, u32[]{:S(2)}, u32[]{:S(2)}) async-start(bf16[128,2,2304]{2,1,0:T(2,128)(2,1)} %shard_map.207), calls=%async_computation.2 | async-start | bytes 2359296 | tf_op jit(solution)/shard_map/all_to_all | solution.py:436

commit v4 on v3

v4 whole, which is shorter than its diff:
```python
import functools
import math

import jax
import jax.numpy as jnp
from jax import lax
from jax.experimental import pallas as pl
from jax.experimental.pallas import tpu as pltpu
from jax.sharding import PartitionSpec as P

EPSILON = 1e-06
F32 = jnp.float32
BF16 = jnp.bfloat16
VMEM = pl.BlockSpec(memory_space=pltpu.VMEM)
HBM = pl.BlockSpec(memory_space=pltpu.HBM)


def in_hbm(array):
    return pltpu.with_memory_space_constraint(array, pltpu.HBM)


def unit_rows(vectors):
    return vectors * lax.rsqrt(jnp.sum(vectors * vectors, -1, keepdims=True) + EPSILON)


def rms_scale(vectors):
    return vectors * lax.rsqrt(jnp.mean(vectors * vectors, -1, keepdims=True) + EPSILON)


def own_kernel(in_ref, own_ref):
    own_ref[...] = in_ref[...].reshape(own_ref.shape)


def own_rows(hidden):
    reqs, steps, width = hidden.shape
    return pl.pallas_call(
        own_kernel,
        out_shape=jax.ShapeDtypeStruct((reqs * steps, width), BF16),
        in_specs=[VMEM],
        out_specs=VMEM,
        compiler_params=pltpu.CompilerParams(vmem_limit_bytes=2 * 1024 * 1024),
    )(hidden)


def collect_kernel(own_ref, *refs):
    *blocks, out_ref = refs
    rows, width = own_ref.shape
    out_ref[pl.ds(0, rows), :] = own_ref[...]
    for i, block in enumerate(blocks):
        out_ref[pl.ds(rows * (i + 1), rows), :] = block[...].reshape(rows, width)


def collect(own, blocks):
    rows, width = own.shape
    return pl.pallas_call(
        collect_kernel,
        out_shape=jax.ShapeDtypeStruct(((1 + len(blocks)) * rows, width), BF16),
        in_specs=[VMEM] * (1 + len(blocks)),
        out_specs=VMEM,
        compiler_params=pltpu.CompilerParams(vmem_limit_bytes=4 * 1024 * 1024),
        cost_estimate=pl.CostEstimate(
            flops=40_000_000_000, bytes_accessed=40_000_000, transcendentals=0
        ),
    )(own, *blocks)


NEAR = (2, 1, 3)
FAR = (3, 1, 2)


def shifted(array, first, amount, grid_rows, grid_cols):
    side = math.isqrt(grid_cols)
    pairs = []
    for row in range(grid_rows):
        for col in range(grid_cols):
            high, low = col // side, col % side
            if (row % 2 == 0) == first:
                low = (low + amount) % side
            else:
                high = (high + amount) % side
            pairs.append((row * grid_cols + col, row * grid_cols + high * side + low))
    return lax.ppermute(array, ("erow", "ecol"), pairs)


def place_of(piece, block, side):
    row, col = lax.axis_index("erow"), lax.axis_index("ecol")
    later, earlier = (0, *FAR)[piece], (0, *NEAR)[block]
    even = lax.rem(row, 2) == 0
    high = lax.div(col, side) + side - jnp.where(even, later, earlier)
    low = lax.rem(col, side) + side - jnp.where(even, earlier, later)
    return lax.rem(high, side) * side + lax.rem(low, side)


def attend_kernel(steps, index, side, *refs):
    (
        tok_ref,
        wq_ref,
        wk_ref,
        wv_ref,
        wb_ref,
        dl_ref,
        db_ref,
        ng_ref,
        dd_ref,
        gd_ref,
        du_ref,
        gl_ref,
        wo_ref,
        mem_ref,
    ) = refs[:14]
    (
        part_ref,
        keys_ref,
        upd_ref,
        stage,
        probe,
        reply,
    ) = refs[14:]
    width, hk = wq_ref.shape
    rows = stage.shape[1]
    reqs = rows // steps
    per_block = reqs // side
    places = [place_of(index, i, side) for i in range(side)]
    tok = tok_ref[...]

    def project(weight):
        return jnp.dot(tok, weight, preferred_element_type=F32)

    query = project(wq_ref[...])
    key = project(wk_ref[...])
    value = project(wv_ref[...])
    beta = jnp.sum(tok.astype(F32) * wb_ref[...].astype(F32), -1, keepdims=True)
    low_decay = project(dd_ref[...]).astype(BF16)
    low_gate = project(gd_ref[...]).astype(BF16)
    decay_pre = jnp.dot(low_decay, du_ref[...], preferred_element_type=F32)
    decay_pre = decay_pre + db_ref[...]
    gate = jax.nn.sigmoid(jnp.dot(low_gate, gl_ref[...], preferred_element_type=F32))
    softplus = jnp.maximum(decay_pre, 0.0) + jnp.log1p(jnp.exp(-jnp.abs(decay_pre)))
    stage[0] = unit_rows(query) * hk ** (-0.5)
    stage[1] = unit_rows(key)
    stage[2] = value
    stage[3] = jnp.broadcast_to(jax.nn.sigmoid(beta), (rows, hk))
    rate = jnp.exp(jnp.full((1, hk), dl_ref[0], F32))
    stage[4] = jnp.exp(-rate * softplus)

    def at(kind, t):
        return stage[kind, pl.ds(t, reqs, stride=steps), :]

    q = [at(0, t) for t in range(steps)]
    k = [at(1, t) for t in range(steps)]
    f = [at(4, t) for t in range(steps)]
    start = []
    for t in range(steps):
        start.append(f[0] if t == 0 else start[-1] * f[t])
        probe[pl.ds(t, reqs, stride=2 * steps), :] = start[t] * k[t]
        probe[pl.ds(steps + t, reqs, stride=2 * steps), :] = start[t] * q[t]

    for r in range(reqs):
        at_rows = pl.ds(r * 2 * steps, 2 * steps)
        memory = mem_ref[places[r // per_block] * per_block + r % per_block]
        reply[at_rows, :] = jnp.dot(
            probe[at_rows, :].astype(BF16), memory.astype(BF16), preferred_element_type=F32
        )

    decayed = []
    updates = []
    for t in range(steps):
        if t > 0:
            decayed = [row * f[t] for row in decayed]
        predicted = reply[pl.ds(t, reqs, stride=2 * steps), :]
        for s in range(t):
            predicted = predicted + jnp.sum(decayed[s] * k[t], -1, keepdims=True) * updates[s]
        updates.append(at(3, t) * (at(2, t) - predicted))
        decayed.append(k[t])
        head = reply[pl.ds(steps + t, reqs, stride=2 * steps), :]
        for s in range(t + 1):
            head = head + jnp.sum(decayed[s] * q[t], -1, keepdims=True) * updates[s]
        stage[0, pl.ds(t, reqs, stride=steps), :] = head
    for t in range(steps):
        keys_ref[pl.ds(t, reqs, stride=2 * steps), :] = decayed[t]
        keys_ref[pl.ds(steps + t, reqs, stride=2 * steps), :] = start[-1]
        upd_ref[pl.ds(t, reqs, stride=steps), :] = updates[t]
    mixed = (rms_scale(stage[0]) * ng_ref[...] * gate).astype(BF16)
    part_ref[...] = jnp.dot(mixed, wo_ref[...], preferred_element_type=F32).astype(BF16)


def attend(index, side, piece, operands, steps):
    rows, width = piece.shape
    hk = operands[-1].shape[-1]
    in_specs = [VMEM] * (1 + len(operands))
    in_specs[5] = pl.BlockSpec(memory_space=pltpu.SMEM)
    return pl.pallas_call(
        functools.partial(attend_kernel, steps, index, side),
        out_shape=(
            jax.ShapeDtypeStruct((rows, width), BF16),
            jax.ShapeDtypeStruct((2 * rows, hk), F32),
            jax.ShapeDtypeStruct((rows, hk), F32),
        ),
        in_specs=in_specs,
        out_specs=(VMEM,) * 3,
        scratch_shapes=[
            pltpu.VMEM((5, rows, hk), F32),
            pltpu.VMEM((2 * rows, hk), F32),
            pltpu.VMEM((2 * rows, hk), F32),
        ],
        compiler_params=pltpu.CompilerParams(vmem_limit_bytes=8 * 1024 * 1024),
        cost_estimate=pl.CostEstimate(
            flops=1_500_000_000, bytes_accessed=2_000_000, transcendentals=0
        ),
    )(piece, *operands)


def middle_kernel(here_ref, *refs):
    count = (len(refs) - 1) // 2
    total = here_ref[...].astype(F32)
    for ref in refs[:count]:
        total = total + ref[...].astype(F32)
    rows = refs[count].shape[0]
    refs[count][...] = total[:rows]
    for i, ref in enumerate(refs[count + 1 :]):
        ref[...] = total[rows * (i + 1) : rows * (i + 2)].astype(BF16)


def middle(here, terms):
    width = here.shape[1]
    rows = here.shape[0] // (1 + len(terms))
    return pl.pallas_call(
        middle_kernel,
        out_shape=(jax.ShapeDtypeStruct((rows, width), F32),)
        + (jax.ShapeDtypeStruct((rows, width), BF16),) * len(terms),
        in_specs=[VMEM] * (1 + len(terms)),
        out_specs=(VMEM,) * (1 + len(terms)),
        compiler_params=pltpu.CompilerParams(vmem_limit_bytes=4 * 1024 * 1024),
    )(here, *terms)


def state_kernel(steps, side, *refs):
    keys, upds = refs[:side], refs[side : 2 * side]
    mem_hbm, new_hbm, old, new, load_sem, store_sem = refs[2 * side :]
    slots, size = old.shape[:2]
    total = side**2

    def at(b):
        start = place_of(b // side, b % side, side) * size
        return pl.ds(start, size)

    def load(b):
        return pltpu.make_async_copy(mem_hbm.at[at(b)], old.at[b % slots], load_sem.at[b % slots])

    def store(b):
        return pltpu.make_async_copy(new.at[b % slots], new_hbm.at[at(b)], store_sem.at[b % slots])

    for b in range(slots - 1):
        load(b).start()
    for b in range(total):
        load(b).wait()
        if b + slots - 1 < total:
            load(b + slots - 1).start()
        if b >= slots:
            store(b - slots).wait()
        piece, block = b // side, b % side
        height = 2 * steps * size
        columns = keys[piece][pl.ds(height * block, height), :].T
        for r in range(size):
            first = 2 * steps * r
            memory = old[b % slots, r] * columns[:, first + steps : first + steps + 1]
            for s in range(steps):
                row = upds[piece][pl.ds(steps * (size * block + r) + s, 1), :]
                memory = memory + columns[:, first + s : first + s + 1] * row
            new[b % slots, r] = memory
        store(b).start()
    for b in range(total - slots, total):
        store(b).wait()


def new_memory(keys, updates, memory, steps):
    reqs, hk, _ = memory.shape
    side = len(keys)
    size, slots = reqs // side**2, 4
    return pl.pallas_call(
        functools.partial(state_kernel, steps, side),
        out_shape=pltpu.HBM(memory.shape, F32),
        in_specs=[VMEM] * (2 * side) + [HBM],
        out_specs=HBM,
        scratch_shapes=[
            pltpu.VMEM((slots, size, hk, hk), F32),
            pltpu.VMEM((slots, size, hk, hk), F32),
            pltpu.SemaphoreType.DMA((slots,)),
            pltpu.SemaphoreType.DMA((slots,)),
        ],
        compiler_params=pltpu.CompilerParams(vmem_limit_bytes=8 * 1024 * 1024),
        cost_estimate=pl.CostEstimate(
            flops=9 * reqs * hk * hk, bytes_accessed=2 * reqs * hk * hk * 4, transcendentals=0
        ),
    )(*keys, *updates, in_hbm(memory))


def route_kernel(capacity, ids_ref, weights_ref, place_ref, combine_ref):
    rows, slots = combine_ref.shape
    picks = ids_ref.shape[-1]
    ids = ids_ref[...].reshape(rows, picks)
    weights = weights_ref[...].reshape(rows, picks)
    slot = lax.broadcasted_iota(jnp.int32, (rows, slots), 1)
    named = jnp.zeros((rows, slots), F32)
    weight = jnp.zeros((rows, slots), F32)
    for j in range(picks):
        hit = ids[:, j : j + 1] == slot // capacity
        named = jnp.where(hit, 1.0, named)
        weight = jnp.where(hit, weights[:, j : j + 1], weight)
    row = lax.broadcasted_iota(jnp.int32, (rows, rows), 0)
    earlier = (lax.broadcasted_iota(jnp.int32, (rows, rows), 1) < row).astype(BF16)
    number = jnp.dot(earlier, named.astype(BF16), preferred_element_type=F32)
    mine = (named > 0.0) & (number == (slot % capacity).astype(F32))
    place_ref[...] = jnp.where(mine, 1.0, 0.0).astype(BF16)
    combine_ref[...] = jnp.where(mine, weight, 0.0)


def route(ids, weights, capacity, slots):
    rows = ids.shape[0] * ids.shape[1]
    return pl.pallas_call(
        functools.partial(route_kernel, capacity),
        out_shape=(
            jax.ShapeDtypeStruct((rows, slots), BF16),
            jax.ShapeDtypeStruct((rows, slots), F32),
        ),
        in_specs=[VMEM] * 2,
        out_specs=(VMEM,) * 2,
        compiler_params=pltpu.CompilerParams(vmem_limit_bytes=2 * 1024 * 1024),
    )(ids, weights)


def join_kernel(own_ref, gain_ref, place_ref, *refs):
    *terms, residual_ref, out_ref = refs
    attended = terms[0][...]
    for ref in terms[1:]:
        attended = attended + ref[...].astype(F32)
    residual = (own_ref[...].astype(F32) + attended).astype(BF16)
    residual_ref[...] = residual
    gain = gain_ref[...].reshape(1, -1)
    normed = (rms_scale(residual.astype(F32)) * gain).astype(BF16)
    sent = lax.dot_general(
        place_ref[...], normed, (((0,), (0,)), ((), ())), preferred_element_type=F32
    ).astype(BF16)
    out_ref[...] = sent.reshape(out_ref.shape)


def join(terms, own, gain, placing, shape):
    rows, width = own.shape
    return pl.pallas_call(
        join_kernel,
        out_shape=(
            jax.ShapeDtypeStruct((rows, width), BF16),
            jax.ShapeDtypeStruct(shape, BF16),
        ),
        in_specs=[VMEM] * (3 + len(terms)),
        out_specs=(VMEM, VMEM),
        compiler_params=pltpu.CompilerParams(vmem_limit_bytes=8 * 1024 * 1024),
        cost_estimate=pl.CostEstimate(
            flops=40_000_000_000, bytes_accessed=40_000_000, transcendentals=0
        ),
    )(own, gain, placing, *terms)


def expert_kernel(rows_ref, gate_ref, up_ref, down_ref, out_ref):
    rows = rows_ref[...].reshape(-1, rows_ref.shape[-1])
    gate = jnp.dot(rows, gate_ref[...], preferred_element_type=F32)
    up = jnp.dot(rows, up_ref[...], preferred_element_type=F32)
    hidden = (jax.nn.silu(gate) * up).astype(BF16)
    out = jnp.dot(hidden, down_ref[...], preferred_element_type=F32).astype(BF16)
    out_ref[...] = out.reshape(out_ref.shape)


def run_expert(rows, gate, up, down):
    width, hidden = gate.shape
    count = rows.size // width
    return pl.pallas_call(
        expert_kernel,
        out_shape=jax.ShapeDtypeStruct(rows.shape, BF16),
        in_specs=[VMEM] * 4,
        out_specs=VMEM,
        compiler_params=pltpu.CompilerParams(vmem_limit_bytes=24 * 1024 * 1024),
        cost_estimate=pl.CostEstimate(
            flops=6 * count * width * hidden,
            bytes_accessed=6 * width * hidden + 4 * count * width,
            transcendentals=count * hidden,
        ),
    )(rows, gate, up, down)


def combine_kernel(rows_ref, residual_ref, weight_ref, out_ref):
    rows = rows_ref[...].reshape(-1, rows_ref.shape[-1])
    weight = weight_ref[...]
    high = weight.astype(BF16)
    rest = weight - high.astype(F32)
    middle = rest.astype(BF16)
    low = (rest - middle.astype(F32)).astype(BF16)
    count = weight.shape[0]
    three = jnp.dot(jnp.concatenate([high, middle, low], 0), rows, preferred_element_type=F32)
    routed = three[:count] + (three[count : 2 * count] + three[2 * count :])
    mixed = (residual_ref[...].astype(F32) + routed).astype(BF16)
    out_ref[...] = mixed.reshape(out_ref.shape)


def combine_rows(rows, residual, weight, shape):
    return pl.pallas_call(
        combine_kernel,
        out_shape=jax.ShapeDtypeStruct(shape, BF16),
        in_specs=[VMEM] * 3,
        out_specs=VMEM,
        compiler_params=pltpu.CompilerParams(vmem_limit_bytes=8 * 1024 * 1024),
    )(rows, residual, weight)


def local(
    hidden_in,
    kda_state,
    query_weight,
    key_weight,
    value_weight,
    beta_weight,
    decay_down,
    decay_up,
    decay_log,
    decay_bias,
    gate_down,
    gate_lift,
    norm_gain,
    output_weight,
    ffn_gain,
    expert_ids,
    route_weight,
    expert_gate,
    expert_up,
    expert_down,
):
    local_req, step_count, model_width = hidden_in.shape
    head_size = kda_state.shape[-1]
    grid_rows = lax.axis_size("erow")
    grid_cols = lax.axis_size("ecol")
    side = math.isqrt(grid_cols)
    own = own_rows(hidden_in)

    def move(array, first, amount):
        return shifted(array, first, amount, grid_rows, grid_cols)

    near = collect(own, [move(hidden_in, True, amount) for amount in NEAR])
    pieces = [near] + [move(near, False, amount) for amount in FAR]
    memory = kda_state.reshape(kda_state.shape[0], head_size, head_size)
    operands = (
        query_weight,
        key_weight,
        value_weight,
        beta_weight.reshape(1, model_width),
        decay_log,
        decay_bias.reshape(1, head_size),
        norm_gain.reshape(1, head_size),
        decay_down,
        gate_down,
        decay_up,
        gate_lift,
        output_weight,
        memory,
    )
    parts, keys, updates = zip(
        *(
            attend(index, side, piece, operands, step_count)
            for index, piece in enumerate(pieces)
        )
    )
    returned = [move(part, False, -amount) for part, amount in zip(parts[1:], FAR)]
    here, *others = middle(parts[0], returned)
    terms = [here] + [move(other, True, -amount) for other, amount in zip(others, NEAR)]
    new_state = new_memory(keys, updates, memory, step_count).reshape(kda_state.shape)
    device_count = grid_rows * grid_cols
    row_total, pick_count = local_req * step_count, expert_ids.shape[-1]
    capacity = max(2, 2 * row_total * pick_count // device_count)
    slots_total = device_count * capacity
    placing, combine = route(expert_ids, route_weight, capacity, slots_total)
    residual, outgoing = join(
        terms, own, ffn_gain, placing, (device_count, capacity, model_width)
    )
    received = lax.all_to_all(
        outgoing, ("erow", "ecol"), split_axis=0, concat_axis=0, tiled=True
    )
    produced = run_expert(received, expert_gate[0], expert_up[0], expert_down[0])
    returned = lax.all_to_all(
        produced, ("erow", "ecol"), split_axis=0, concat_axis=0, tiled=True
    )
    mixed = combine_rows(returned, residual, combine, hidden_in.shape)
    return (mixed, new_state)


def solution(mesh):
    return jax.shard_map(
        local,
        mesh=mesh,
        in_specs=(
            P(("erow", "ecol"), None, None),
            P("erow", "ecol", None, None),
            P(None, "ecol"),
            P(None, "ecol"),
            P(None, "ecol"),
            P(None, "ecol"),
            P(),
            P(None, "ecol"),
            P("ecol"),
            P("ecol"),
            P(),
            P(None, "ecol"),
            P(),
            P("ecol", None),
            P(),
            P(("erow", "ecol"), None, None),
            P(("erow", "ecol"), None, None),
            P(("erow", "ecol"), None, None),
            P(("erow", "ecol"), None, None),
            P(("erow", "ecol"), None, None),
        ),
        out_specs=(P(("erow", "ecol"), None, None), P("erow", "ecol", None, None)),
        check_vma=False,
    )
```

time: 108 us -> 103 us (0.954)
  waiting for transfers between devices: 37.5 us -> 26.4 us
  starting transfers between devices: 19.1 us -> 23.9 us
  Pallas kernels: 20.2 us -> 22.5 us
    all_to_all x2 -> x1, waiting for transfers between devices: 27 us -> 9.87 us  [local(): lax.all_to_all(produced, ('erow', 'ecol'), split_axis=0, concat_axis=0, t...]
    ppermute x6 -> x12, starting transfers between devices: 9.89 us -> 19.2 us  [shifted(): return lax.ppermute(array, ('erow', 'ecol'), pairs)]
    ppermute x6 -> x12, waiting for transfers between devices: 10.6 us -> 16.5 us  [shifted(): return lax.ppermute(array, ('erow', 'ecol'), pairs)]
    all_to_all x2 -> x1, starting transfers between devices: 9.22 us -> 4.63 us  [local(): lax.all_to_all(produced, ('erow', 'ecol'), split_axis=0, concat_axis=0, t...]
    pallas_call x2 -> x7, Pallas kernels: 13.4 us -> 15.8 us  [the longest x1 10.5 us: new_memory(): pl.pallas_call(functools.partial(state_kernel, steps, side), out_shape=pl...]
  transfers between devices with their start and end apart: 8 -> 13, of which waited for: 7 -> 8; matrix products, arithmetic and copies ran while one was open for 1% -> 0% of each run, Pallas kernels for 8% -> 15%
where the time goes in v4:
time: 103 us; the launch traced here: 102 us
  blocking collectives  26.9 us (26%)
  waiting for transfers between devices  26.4 us (26%)
  starting transfers between devices  23.9 us (23%)
  Pallas kernels  22.5 us (22%)
  between operations  1.64 us (2%)
  local copies, waits for them, and re-layouts  1.03 us (1%)
    all_to_all x1, blocking collectives, local(): lax.all_to_all(outgoing, ('erow', 'ecol'), split_axis=0, concat_axis=0, t...  26.9 us
    ppermute x12, starting transfers between devices, shifted(): return lax.ppermute(array, ('erow', 'ecol'), pairs)  19.2 us
    ppermute x12, waiting for transfers between devices, shifted(): return lax.ppermute(array, ('erow', 'ecol'), pairs)  16.5 us
    pallas_call x1, Pallas kernels, new_memory(): pl.pallas_call(functools.partial(state_kernel, steps, side), out_shape=pl...  10.5 us
    all_to_all x1, waiting for transfers between devices, local(): lax.all_to_all(produced, ('erow', 'ecol'), split_axis=0, concat_axis=0, t...  9.87 us
    pallas_call x1, Pallas kernels, run_expert(): pl.pallas_call(expert_kernel, out_shape=jax.ShapeDtypeStruct(rows.shape,...  5.04 us
    pallas_call x4, Pallas kernels, attend(): pl.pallas_call(functools.partial(attend_kernel, steps, index, side), out_...  4.93 us
    all_to_all x1, starting transfers between devices, local(): lax.all_to_all(produced, ('erow', 'ecol'), split_axis=0, concat_axis=0, t...  4.63 us
  transfers between devices with their start and end apart: 13, of which 8 were waited for; matrix products, arithmetic and copies ran while one was open for 0% of the time, Pallas kernels for 15%

profile of v4, /device:TPU:0, one launch (start us, length us, event | category | flops | bytes accessed | tf_op | source)
XLA Modules:
  0.0 102.3 jit_solution(5080747082357451799)
XLA Ops:
  0.6 3.4 %collective-permute-start = (bf16[4,4,2304]{2,1,0:T(4,128)(2,1)}, bf16[4,4,2304]{2,1,0:T(4,128)(2,1)S(1)}, u32[]{:S(2)}, u32[]{:S(2)}) collective-permute-start(bf16[4,4,2304]{2,1,0:T(4,128)(2,1)} %in_ref.1), channel_id=1, source_target_pairs={{0,2},{1,3},{2,0},{3,1},{4,6},{5,7},{6,4},{7,5},{8,10},{9,11},{10,... | collective-permute-start | bytes 221192 | tf_op jit(solution)/shard_map/ppermute | solution.py:82
  4.0 1.1 %collective-permute-start.2 = (bf16[4,4,2304]{2,1,0:T(4,128)(2,1)}, bf16[4,4,2304]{2,1,0:T(4,128)(2,1)S(1)}, u32[]{:S(2)}, u32[]{:S(2)}) collective-permute-start(bf16[4,4,2304]{2,1,0:T(4,128)(2,1)} %in_ref.1), channel_id=1, source_target_pairs={{0,3},{1,0},{2,1},{3,2},{4,7},{5,4},{6,5},{7,6},{8,11},{9,8},{10,9... | collective-permute-start | bytes 221192 | tf_op jit(solution)/shard_map/ppermute | solution.py:82
  5.0 1.0 collective-permute-start.1
  6.0 0.9 copy-done.10
  6.9 0.0 copy-start
  7.0 0.0 copy-start.1
  7.0 0.0 copy-start.2
  7.0 0.0 copy-start.3
  7.0 0.0 copy-start.4
  7.0 0.0 copy-start.5
  7.0 0.0 copy-start.6
  7.0 0.0 copy-start.7
  7.0 0.0 copy-start.8
  7.1 0.0 copy-start.9
  7.1 0.0 copy-start.11
  7.1 0.0 copy-start.12
  7.1 0.0 collective-permute-done.refs_0_
  7.1 1.4 %collective-permute-done.2.refs_2_ = bf16[4,4,2304]{2,1,0:T(4,128)(2,1)S(1)} collective-permute-done((bf16[4,4,2304]{2,1,0:T(4,128)(2,1)}, bf16[4,4,2304]{2,1,0:T(4,128)(2,1)S(1)}, u32[]{:S(2)}, u32[]{:S(2)}) %collective-permute-start.2) | collective-permute-done | bytes 73760 | tf_op jit(solution)/shard_map/ppermute | solution.py:82
  8.6 2.3 %collective-permute-done.1.refs_1_ = bf16[4,4,2304]{2,1,0:T(4,128)(2,1)S(1)} collective-permute-done((bf16[4,4,2304]{2,1,0:T(4,128)(2,1)}, bf16[4,4,2304]{2,1,0:T(4,128)(2,1)S(1)}, u32[]{:S(2)}, u32[]{:S(2)}) %collective-permute-start.1) | collective-permute-done | bytes 73760 | tf_op jit(solution)/shard_map/ppermute | solution.py:82
  10.8 3.1 %collective-permute-start.7 = (bf16[64,2304]{1,0:T(8,128)(2,1)S(1)}, bf16[64,2304]{1,0:T(8,128)(2,1)S(1)}, u32[]{:S(2)}, u32[]{:S(2)}) collective-permute-start(bf16[64,2304]{1,0:T(8,128)(2,1)S(1)} %shard_map.205.refs_0_), channel_id=1, source_target_pairs={{0,8},{1,9},{2,10},{3,11},{4,12},{5,13},{6,14},{7,15},{8,0},{9,1},... | collective-permute-start | bytes 884744 | tf_op jit(solution)/shard_map/ppermute | solution.py:82
  14.0 0.6 collective-permute-start.5
  14.5 2.6 %collective-permute-start.3 = (bf16[64,2304]{1,0:T(8,128)(2,1)S(1)}, bf16[64,2304]{1,0:T(8,128)(2,1)S(1)}, u32[]{:S(2)}, u32[]{:S(2)}) collective-permute-start(bf16[64,2304]{1,0:T(8,128)(2,1)S(1)} %shard_map.205.refs_0_), channel_id=1, source_target_pairs={{0,12},{1,13},{2,14},{3,15},{4,0},{5,1},{6,2},{7,3},{8,4},{9,5},{1... | collective-permute-start | bytes 884744 | tf_op jit(solution)/shard_map/ppermute | solution.py:82
  17.8 1.4 %collective-permute-done.7.refs_0_ = bf16[64,2304]{1,0:T(8,128)(2,1)S(1)} collective-permute-done((bf16[64,2304]{1,0:T(8,128)(2,1)S(1)}, bf16[64,2304]{1,0:T(8,128)(2,1)S(1)}, u32[]{:S(2)}, u32[]{:S(2)}) %collective-permute-start.7) | collective-permute-done | bytes 294944 | tf_op jit(solution)/shard_map/ppermute | solution.py:82
  19.2 0.0 copy-done
  19.2 0.0 copy-done.1
  19.2 0.0 copy-done.2
  19.2 0.0 copy-done.3
  19.2 0.0 copy-done.4
  19.2 0.0 copy-done.5
  19.2 0.0 copy-done.6
  19.3 0.0 copy-done.7
  19.3 1.2 %shard_map.209 = (bf16[64,2304]{1,0:T(8,128)(2,1)S(1)}, f32[128,128]{1,0:T(8,128)S(1)}, f32[64,128]{1,0:T(8,128)S(1)}) custom-call(bf16[64,2304]{1,0:T(8,128)(2,1)S(1)} %collective-permute-done.7.refs_0_, bf16[2304,128]{1,0:T(8,128)(2,1)S(1)} %copy-done.1, bf16[2304,128]{1,0:T(8,128)(2,1)S(1)} %copy-done.2, bf16[2304,128]{1,0:T(8,128)(2,1)S(1)} %copy-done.3, ...), custom_call_target="tpu_custom_call" | custom-call | flops 1500000000 | bytes 2000000 | tf_op jit(solution)/shard_map/pallas_call | solution.py:192
  20.5 3.2 %collective-permute-start.8 = (bf16[64,2304]{1,0:T(8,128)(2,1)S(1)}, bf16[64,2304]{1,0:T(8,128)(2,1)S(1)}, u32[]{:S(2)}, u32[]{:S(2)}) collective-permute-start(bf16[64,2304]{1,0:T(8,128)(2,1)S(1)} %get-tuple-element.26), channel_id=1, source_target_pairs={{0,8},{1,9},{2,10},{3,11},{4,12},{5,13},{6,14},{7,15},{8,0},{9,1},... | collective-permute-start | bytes 884744 | tf_op jit(solution)/shard_map/ppermute | solution.py:82
  23.7 0.0 collective-permute-done.5.refs_0_
  23.7 1.2 %shard_map.208 = (bf16[64,2304]{1,0:T(8,128)(2,1)S(1)}, f32[128,128]{1,0:T(8,128)S(1)}, f32[64,128]{1,0:T(8,128)S(1)}) custom-call(bf16[64,2304]{1,0:T(8,128)(2,1)S(1)} %collective-permute-done.5.refs_0_, bf16[2304,128]{1,0:T(8,128)(2,1)S(1)} %copy-done.1, bf16[2304,128]{1,0:T(8,128)(2,1)S(1)} %copy-done.2, bf16[2304,128]{1,0:T(8,128)(2,1)S(1)} %copy-done.3, ...), custom_call_target="tpu_custom_call" | custom-call | flops 1500000000 | bytes 2000000 | tf_op jit(solution)/shard_map/pallas_call | solution.py:192
  25.0 1.2 %collective-permute-start.6 = (bf16[64,2304]{1,0:T(8,128)(2,1)S(1)}, bf16[64,2304]{1,0:T(8,128)(2,1)S(1)}, u32[]{:S(2)}, u32[]{:S(2)}) collective-permute-start(bf16[64,2304]{1,0:T(8,128)(2,1)S(1)} %get-tuple-element.25), channel_id=1, source_target_pairs={{0,12},{1,13},{2,14},{3,15},{4,0},{5,1},{6,2},{7,3},{8,4},{9,5},{1... | collective-permute-start | bytes 884744 | tf_op jit(solution)/shard_map/ppermute | solution.py:82
  26.2 0.0 collective-permute-done.3.refs_0_
  26.2 1.2 %shard_map.207 = (bf16[64,2304]{1,0:T(8,128)(2,1)S(1)}, f32[128,128]{1,0:T(8,128)S(1)}, f32[64,128]{1,0:T(8,128)S(1)}) custom-call(bf16[64,2304]{1,0:T(8,128)(2,1)S(1)} %collective-permute-done.3.refs_0_, bf16[2304,128]{1,0:T(8,128)(2,1)S(1)} %copy-done.1, bf16[2304,128]{1,0:T(8,128)(2,1)S(1)} %copy-done.2, bf16[2304,128]{1,0:T(8,128)(2,1)S(1)} %copy-done.3, ...), custom_call_target="tpu_custom_call" | custom-call | flops 1500000000 | bytes 2000000 | tf_op jit(solution)/shard_map/pallas_call | solution.py:192
  27.4 0.0 copy-start.13
  27.4 0.0 copy-start.14
  27.4 0.0 copy-start.15
  27.4 1.0 collective-permute-start.4
  28.4 1.2 %shard_map.206 = (bf16[64,2304]{1,0:T(8,128)(2,1)S(1)}, f32[128,128]{1,0:T(8,128)S(1)}, f32[64,128]{1,0:T(8,128)S(1)}) custom-call(bf16[64,2304]{1,0:T(8,128)(2,1)S(1)} %shard_map.205.refs_0_, bf16[2304,128]{1,0:T(8,128)(2,1)S(1)} %copy-done.1, bf16[2304,128]{1,0:T(8,128)(2,1)S(1)} %copy-done.2, bf16[2304,128]{1,0:T(8,128)(2,1)S(1)} %copy-done.3, ...), custom_call_target="tpu_custom_call" | custom-call | flops 1500000000 | bytes 2000000 | tf_op jit(solution)/shard_map/pallas_call | solution.py:192
  29.6 0.0 collective-permute-done.8.refs_2_
  29.7 2.4 %collective-permute-done.6.refs_1_ = bf16[64,2304]{1,0:T(8,128)(2,1)S(1)} collective-permute-done((bf16[64,2304]{1,0:T(8,128)(2,1)S(1)}, bf16[64,2304]{1,0:T(8,128)(2,1)S(1)}, u32[]{:S(2)}, u32[]{:S(2)}) %collective-permute-start.6) | collective-permute-done | bytes 294944 | tf_op jit(solution)/shard_map/ppermute | solution.py:82
  32.1 4.2 %collective-permute-done.4.refs_0_ = bf16[64,2304]{1,0:T(8,128)(2,1)S(1)} collective-permute-done((bf16[64,2304]{1,0:T(8,128)(2,1)S(1)}, bf16[64,2304]{1,0:T(8,128)(2,1)S(1)}, u32[]{:S(2)}, u32[]{:S(2)}) %collective-permute-start.4) | collective-permute-done | bytes 294944 | tf_op jit(solution)/shard_map/ppermute | solution.py:82
  36.2 0.1 shard_map.210
  36.4 0.1 collective-permute-start.9
  36.5 1.6 %collective-permute-start.10 = (bf16[16,2304]{1,0:T(8,128)(2,1)S(1)}, bf16[16,2304]{1,0:T(8,128)(2,1)S(1)}, u32[]{:S(2)}, u32[]{:S(2)}) collective-permute-start(bf16[16,2304]{1,0:T(8,128)(2,1)S(1)} %get-tuple-element.29), channel_id=1, source_target_pairs={{0,3},{1,0},{2,1},{3,2},{4,7},{5,4},{6,5},{7,6},{8,11},{9,8},{10,9... | collective-permute-start | bytes 221192 | tf_op jit(solution)/shard_map/ppermute | solution.py:82
  38.1 0.5 collective-permute-start.11
  38.6 0.0 copy-done.14
  38.6 0.2 shard_map.204
  38.8 3.5 %collective-permute-done.9.refs_1_ = bf16[16,2304]{1,0:T(8,128)(2,1)S(1)} collective-permute-done((bf16[16,2304]{1,0:T(8,128)(2,1)S(1)}, bf16[16,2304]{1,0:T(8,128)(2,1)S(1)}, u32[]{:S(2)}, u32[]{:S(2)}) %collective-permute-start.9) | collective-permute-done | bytes 73760 | tf_op jit(solution)/shard_map/ppermute | solution.py:82
  42.3 0.0 collective-permute-done.10.refs_2_
  42.3 1.4 %collective-permute-done.11.refs_3_ = bf16[16,2304]{1,0:T(8,128)(2,1)S(1)} collective-permute-done((bf16[16,2304]{1,0:T(8,128)(2,1)S(1)}, bf16[16,2304]{1,0:T(8,128)(2,1)S(1)}, u32[]{:S(2)}, u32[]{:S(2)}) %collective-permute-start.11) | collective-permute-done | bytes 73760 | tf_op jit(solution)/shard_map/ppermute | solution.py:82
  43.7 0.6 shard_map.211
  44.3 26.9 %all_to_all.10.rows_ref = bf16[128,2,2304]{2,1,0:T(2,128)(2,1)S(1)} all-to-all(bf16[128,2,2304]{2,1,0:T(2,128)(2,1)S(1)} %get-tuple-element.31), channel_id=1, replica_groups=mesh['erow'=8,'ecol'=16] {'erow','ecol'}, dimensions={0} | all-to-all | bytes 2359296 | tf_op jit(solution)/shard_map/all_to_all | solution.py:482
  71.2 0.0 slice-done
  71.2 0.0 slice-done.4
  71.3 5.0 %shard_map.212 = bf16[128,2,2304]{2,1,0:T(2,128)(2,1)} custom-call(bf16[128,2,2304]{2,1,0:T(2,128)(2,1)S(1)} %all_to_all.10.rows_ref, bf16[2304,1024]{1,0:T(8,128)(2,1)S(1)} %bitcast.17, bf16[2304,1024]{1,0:T(8,128)(2,1)S(1)} %bitcast.20, bf16[1024,2304]{1,0:T(8,128)(2,1)S(1)} %bitcast.23), custom_call_target="tpu_custom_call" | custom-call | flops 3623878656 | bytes 16515072 | tf_op jit(solution)/shard_map/pallas_call | solution.py:376
  76.3 4.6 %all-to-all-start.1 = ((bf16[128,2,2304]{2,1,0:T(2,128)(2,1)}), bf16[128,2,2304]{2,1,0:T(2,128)(2,1)S(1)}, u32[]{:S(2)}, u32[]{:S(2)}) async-start(bf16[128,2,2304]{2,1,0:T(2,128)(2,1)} %shard_map.212), calls=%async_computation.1 | async-start | bytes 2359296 | tf_op jit(solution)/shard_map/all_to_all | solution.py:486
  80.9 10.5 %shard_map.214 = f32[64,128,128]{2,1,0:T(8,128)} custom-call(f32[128,128]{1,0:T(8,128)S(1)} %get-tuple-element.34.refs_0_, f32[128,128]{1,0:T(8,128)S(1)} %get-tuple-element.35.refs_1_, f32[128,128]{1,0:T(8,128)S(1)} %get-tuple-element.36.refs_2_, f32[128,128]{1,0:T(8,128)S(1)} %get-tuple-element.37.refs_3_, f32[64,128]{1,0:T(8,128)S(1)} %get-tuple-element.38.refs_4_, ...), custom_call_target="tpu_custom_call" | custom-call | flops 9437184 | bytes 8388608 | tf_op jit(solution)/shard_map/pallas_call | solution.py:280
  91.5 9.9 %all-to-all-done.1.rows_ref = bf16[128,2,2304]{2,1,0:T(2,128)(2,1)S(1)} async-done(((bf16[128,2,2304]{2,1,0:T(2,128)(2,1)}), bf16[128,2,2304]{2,1,0:T(2,128)(2,1)S(1)}, u32[]{:S(2)}, u32[]{:S(2)}) %all-to-all-start.1) | async-done | bytes 1179680 | tf_op jit(solution)/shard_map/all_to_all | solution.py:486
  101.3 1.0 shard_map.213
  (22 shorter events, 0.1 us)
Async XLA Ops:
  0.6 6.5 %collective-permute-start = (bf16[4,4,2304]{2,1,0:T(4,128)(2,1)}, bf16[4,4,2304]{2,1,0:T(4,128)(2,1)S(1)}, u32[]{:S(2)}, u32[]{:S(2)}) collective-permute-start(bf16[4,4,2304]{2,1,0:T(4,128)(2,1)} %in_ref.1), channel_id=1, source_target_pairs={{0,2},{1,3},{2,0},{3,1},{4,6},{5,7},{6,4},{7,5},{8,10},{9,11},{10,... | collective-permute-start | bytes 221192 | tf_op jit(solution)/shard_map/ppermute | solution.py:82
  4.0 4.6 %collective-permute-start.2 = (bf16[4,4,2304]{2,1,0:T(4,128)(2,1)}, bf16[4,4,2304]{2,1,0:T(4,128)(2,1)S(1)}, u32[]{:S(2)}, u32[]{:S(2)}) collective-permute-start(bf16[4,4,2304]{2,1,0:T(4,128)(2,1)} %in_ref.1), channel_id=1, source_target_pairs={{0,3},{1,0},{2,1},{3,2},{4,7},{5,4},{6,5},{7,6},{8,11},{9,8},{10,9... | collective-permute-start | bytes 221192 | tf_op jit(solution)/shard_map/ppermute | solution.py:82
  5.0 5.8 %collective-permute-start.1 = (bf16[4,4,2304]{2,1,0:T(4,128)(2,1)}, bf16[4,4,2304]{2,1,0:T(4,128)(2,1)S(1)}, u32[]{:S(2)}, u32[]{:S(2)}) collective-permute-start(bf16[4,4,2304]{2,1,0:T(4,128)(2,1)} %in_ref.1), channel_id=1, source_target_pairs={{0,1},{1,2},{2,3},{3,0},{4,5},{5,6},{6,7},{7,4},{8,9},{9,10},{10,1... | collective-permute-start | bytes 221192 | tf_op jit(solution)/shard_map/ppermute | solution.py:82
  6.0 0.9 copy-start.10
  6.9 12.3 %copy-start = (f32[64,1,128,128]{3,2,1,0:T(8,128)S(1)}, f32[64,1,128,128]{3,2,1,0:T(8,128)}, u32[]{:S(2)}) copy-start(f32[64,1,128,128]{3,2,1,0:T(8,128)} %param.21) | copy-start | bytes 12582916
  7.0 12.3 %copy-start.1 = (bf16[2304,128]{1,0:T(8,128)(2,1)S(1)}, bf16[2304,128]{1,0:T(8,128)(2,1)}, u32[]{:S(2)}) copy-start(bf16[2304,128]{1,0:T(8,128)(2,1)} %refs_1_.7) | copy-start | bytes 1769476
  7.0 12.2 %copy-start.2 = (bf16[2304,128]{1,0:T(8,128)(2,1)S(1)}, bf16[2304,128]{1,0:T(8,128)(2,1)}, u32[]{:S(2)}) copy-start(bf16[2304,128]{1,0:T(8,128)(2,1)} %refs_2_.7) | copy-start | bytes 1769476
  7.0 12.2 %copy-start.3 = (bf16[2304,128]{1,0:T(8,128)(2,1)S(1)}, bf16[2304,128]{1,0:T(8,128)(2,1)}, u32[]{:S(2)}) copy-start(bf16[2304,128]{1,0:T(8,128)(2,1)} %refs_3_.7) | copy-start | bytes 1769476
  7.0 12.2 %copy-start.4 = (bf16[2304,128]{1,0:T(8,128)(2,1)S(1)}, bf16[2304,128]{1,0:T(8,128)(2,1)}, u32[]{:S(2)}) copy-start(bf16[2304,128]{1,0:T(8,128)(2,1)} %refs_8_.7) | copy-start | bytes 1769476
  7.0 12.2 %copy-start.5 = (bf16[2304,128]{1,0:T(8,128)(2,1)S(1)}, bf16[2304,128]{1,0:T(8,128)(2,1)}, u32[]{:S(2)}) copy-start(bf16[2304,128]{1,0:T(8,128)(2,1)} %refs_9_.7) | copy-start | bytes 1769476
  7.0 12.2 %copy-start.6 = (bf16[128,2304]{1,0:T(8,128)(2,1)S(1)}, bf16[128,2304]{1,0:T(8,128)(2,1)}, u32[]{:S(2)}) copy-start(bf16[128,2304]{1,0:T(8,128)(2,1)} %refs_12_.7) | copy-start | bytes 1769476
  7.0 12.2 %copy-start.7 = (bf16[128,128]{1,0:T(8,128)(2,1)S(1)}, bf16[128,128]{1,0:T(8,128)(2,1)}, u32[]{:S(2)}) copy-start(bf16[128,128]{1,0:T(8,128)(2,1)} %refs_10_.7) | copy-start | bytes 98308
  7.0 12.2 %copy-start.8 = (bf16[128,128]{1,0:T(8,128)(2,1)S(1)}, bf16[128,128]{1,0:T(8,128)(2,1)}, u32[]{:S(2)}) copy-start(bf16[128,128]{1,0:T(8,128)(2,1)} %refs_11_.7) | copy-start | bytes 98308
  7.1 12.2 %copy-start.9 = (bf16[2304,1]{0,1:T(2,128)(2,1)S(1)}, bf16[2304,1]{0,1:T(2,128)(2,1)}, u32[]{:S(2)}) copy-start(bf16[2304,1]{0,1:T(2,128)(2,1)} %param.25) | copy-start | bytes 13828
  7.1 12.2 %copy-start.11 = (f32[128]{0:T(128)S(1)}, f32[128]{0:T(128)}, u32[]{:S(2)}) copy-start(f32[128]{0:T(128)} %param.29) | copy-start | bytes 1540
  7.1 12.2 %copy-start.12 = (f32[128]{0:T(128)S(1)}, f32[128]{0:T(128)}, u32[]{:S(2)}) copy-start(f32[128]{0:T(128)} %param.32) | copy-start | bytes 1540
  10.8 8.4 %collective-permute-start.7 = (bf16[64,2304]{1,0:T(8,128)(2,1)S(1)}, bf16[64,2304]{1,0:T(8,128)(2,1)S(1)}, u32[]{:S(2)}, u32[]{:S(2)}) collective-permute-start(bf16[64,2304]{1,0:T(8,128)(2,1)S(1)} %shard_map.205.refs_0_), channel_id=1, source_target_pairs={{0,8},{1,9},{2,10},{3,11},{4,12},{5,13},{6,14},{7,15},{8,0},{9,1},... | collective-permute-start | bytes 884744 | tf_op jit(solution)/shard_map/ppermute | solution.py:82
  14.0 9.8 %collective-permute-start.5 = (bf16[64,2304]{1,0:T(8,128)(2,1)S(1)}, bf16[64,2304]{1,0:T(8,128)(2,1)S(1)}, u32[]{:S(2)}, u32[]{:S(2)}) collective-permute-start(bf16[64,2304]{1,0:T(8,128)(2,1)S(1)} %shard_map.205.refs_0_), channel_id=1, source_target_pairs={{0,4},{1,5},{2,6},{3,7},{4,8},{5,9},{6,10},{7,11},{8,12},{9,13},{1... | collective-permute-start | bytes 884744 | tf_op jit(solution)/shard_map/ppermute | solution.py:82
  14.5 11.6 %collective-permute-start.3 = (bf16[64,2304]{1,0:T(8,128)(2,1)S(1)}, bf16[64,2304]{1,0:T(8,128)(2,1)S(1)}, u32[]{:S(2)}, u32[]{:S(2)}) collective-permute-start(bf16[64,2304]{1,0:T(8,128)(2,1)S(1)} %shard_map.205.refs_0_), channel_id=1, source_target_pairs={{0,12},{1,13},{2,14},{3,15},{4,0},{5,1},{6,2},{7,3},{8,4},{9,5},{1... | collective-permute-start | bytes 884744 | tf_op jit(solution)/shard_map/ppermute | solution.py:82
  20.5 9.1 %collective-permute-start.8 = (bf16[64,2304]{1,0:T(8,128)(2,1)S(1)}, bf16[64,2304]{1,0:T(8,128)(2,1)S(1)}, u32[]{:S(2)}, u32[]{:S(2)}) collective-permute-start(bf16[64,2304]{1,0:T(8,128)(2,1)S(1)} %get-tuple-element.26), channel_id=1, source_target_pairs={{0,8},{1,9},{2,10},{3,11},{4,12},{5,13},{6,14},{7,15},{8,0},{9,1},... | collective-permute-start | bytes 884744 | tf_op jit(solution)/shard_map/ppermute | solution.py:82
  25.0 7.1 %collective-permute-start.6 = (bf16[64,2304]{1,0:T(8,128)(2,1)S(1)}, bf16[64,2304]{1,0:T(8,128)(2,1)S(1)}, u32[]{:S(2)}, u32[]{:S(2)}) collective-permute-start(bf16[64,2304]{1,0:T(8,128)(2,1)S(1)} %get-tuple-element.25), channel_id=1, source_target_pairs={{0,12},{1,13},{2,14},{3,15},{4,0},{5,1},{6,2},{7,3},{8,4},{9,5},{1... | collective-permute-start | bytes 884744 | tf_op jit(solution)/shard_map/ppermute | solution.py:82
  27.4 11.2 %copy-start.13 = (s32[4,4,8]{2,1,0:T(4,128)S(1)}, s32[4,4,8]{2,1,0:T(4,128)}, u32[]{:S(2)}) copy-start(s32[4,4,8]{2,1,0:T(4,128)} %ids_ref.1) | copy-start | bytes 1540
  27.4 11.2 %copy-start.14 = (f32[4,4,8]{2,1,0:T(4,128)S(1)}, f32[4,4,8]{2,1,0:T(4,128)}, u32[]{:S(2)}) copy-start(f32[4,4,8]{2,1,0:T(4,128)} %weights_ref.1) | copy-start | bytes 1540
  27.4 16.2 %copy-start.15 = (f32[2304]{0:T(1024)S(1)}, f32[2304]{0:T(1024)}, u32[]{:S(2)}) copy-start(f32[2304]{0:T(1024)} %gain_ref.1) | copy-start | bytes 27652
  27.4 8.8 %collective-permute-start.4 = (bf16[64,2304]{1,0:T(8,128)(2,1)S(1)}, bf16[64,2304]{1,0:T(8,128)(2,1)S(1)}, u32[]{:S(2)}, u32[]{:S(2)}) collective-permute-start(bf16[64,2304]{1,0:T(8,128)(2,1)S(1)} %get-tuple-element.24), channel_id=1, source_target_pairs={{0,4},{1,5},{2,6},{3,7},{4,8},{5,9},{6,10},{7,11},{8,12},{9,13},{1... | collective-permute-start | bytes 884744 | tf_op jit(solution)/shard_map/ppermute | solution.py:82
  28.4 42.8 %slice-start = ((s8[4718592]{0:T(1024)(128)(4,1)}), s8[4194304]{0:T(1024)(128)(4,1)S(1)}, s32[]{:S(2)}) async-start(s8[4718592]{0:T(1024)(128)(4,1)} %bitcast.15), calls=%async_computation.2 | async-start | bytes 8388608
  28.4 42.8 %slice-start.2 = ((s8[4718592]{0:T(1024)(128)(4,1)}), s8[4194304]{0:T(1024)(128)(4,1)S(1)}, s32[]{:S(2)}) async-start(s8[4718592]{0:T(1024)(128)(4,1)} %bitcast.18), calls=%async_computation.4 | async-start | bytes 8388608
  28.4 42.8 %slice-start.4 = ((s8[4718592]{0:T(1024)(128)(4,1)}), s8[4194304]{0:T(1024)(128)(4,1)S(1)}, s32[]{:S(2)}) async-start(s8[4718592]{0:T(1024)(128)(4,1)} %bitcast.21), calls=%async_computation.6 | async-start | bytes 8388608
  36.4 5.9 %collective-permute-start.9 = (bf16[16,2304]{1,0:T(8,128)(2,1)S(1)}, bf16[16,2304]{1,0:T(8,128)(2,1)S(1)}, u32[]{:S(2)}, u32[]{:S(2)}) collective-permute-start(bf16[16,2304]{1,0:T(8,128)(2,1)S(1)} %get-tuple-element.28), channel_id=1, source_target_pairs={{0,2},{1,3},{2,0},{3,1},{4,6},{5,7},{6,4},{7,5},{8,10},{9,11},{10,... | collective-permute-start | bytes 221192 | tf_op jit(solution)/shard_map/ppermute | solution.py:82
  36.5 5.8 %collective-permute-start.10 = (bf16[16,2304]{1,0:T(8,128)(2,1)S(1)}, bf16[16,2304]{1,0:T(8,128)(2,1)S(1)}, u32[]{:S(2)}, u32[]{:S(2)}) collective-permute-start(bf16[16,2304]{1,0:T(8,128)(2,1)S(1)} %get-tuple-element.29), channel_id=1, source_target_pairs={{0,3},{1,0},{2,1},{3,2},{4,7},{5,4},{6,5},{7,6},{8,11},{9,8},{10,9... | collective-permute-start | bytes 221192 | tf_op jit(solution)/shard_map/ppermute | solution.py:82
  38.1 5.6 %collective-permute-start.11 = (bf16[16,2304]{1,0:T(8,128)(2,1)S(1)}, bf16[16,2304]{1,0:T(8,128)(2,1)S(1)}, u32[]{:S(2)}, u32[]{:S(2)}) collective-permute-start(bf16[16,2304]{1,0:T(8,128)(2,1)S(1)} %get-tuple-element.30), channel_id=1, source_target_pairs={{0,1},{1,2},{2,3},{3,0},{4,5},{5,6},{6,7},{7,4},{8,9},{9,10},{10,1... | collective-permute-start | bytes 221192 | tf_op jit(solution)/shard_map/ppermute | solution.py:82
  43.7 27.5 %slice-start.1 = ((s8[4718592]{0:T(1024)(128)(4,1)}), s8[524288]{0:T(1024)(128)(4,1)S(1)}, s32[]{:S(2)}) async-start(s8[4718592]{0:T(1024)(128)(4,1)} %bitcast.15), calls=%async_computation.3 | async-start | bytes 1048576
  43.7 27.5 %slice-start.3 = ((s8[4718592]{0:T(1024)(128)(4,1)}), s8[524288]{0:T(1024)(128)(4,1)S(1)}, s32[]{:S(2)}) async-start(s8[4718592]{0:T(1024)(128)(4,1)} %bitcast.18), calls=%async_computation.5 | async-start | bytes 1048576
  43.7 27.5 %slice-start.5 = ((s8[4718592]{0:T(1024)(128)(4,1)}), s8[524288]{0:T(1024)(128)(4,1)S(1)}, s32[]{:S(2)}) async-start(s8[4718592]{0:T(1024)(128)(4,1)} %bitcast.21), calls=%async_computation.7 | async-start | bytes 1048576
  76.3 25.0 %all-to-all-start.1 = ((bf16[128,2,2304]{2,1,0:T(2,128)(2,1)}), bf16[128,2,2304]{2,1,0:T(2,128)(2,1)S(1)}, u32[]{:S(2)}, u32[]{:S(2)}) async-start(bf16[128,2,2304]{2,1,0:T(2,128)(2,1)} %shard_map.212), calls=%async_computation.1 | async-start | bytes 2359296 | tf_op jit(solution)/shard_map/all_to_all | solution.py:486

commit v5 on v4

--- a/solution.py
+++ b/solution.py
@@ -179,7 +179,8 @@
     for t in range(steps):
         keys_ref[pl.ds(t, reqs, stride=2 * steps), :] = decayed[t]
         keys_ref[pl.ds(steps + t, reqs, stride=2 * steps), :] = start[-1]
-        upd_ref[pl.ds(t, reqs, stride=steps), :] = updates[t]
+        upd_ref[pl.ds(t, reqs, stride=2 * steps), :] = updates[t]
+        upd_ref[pl.ds(steps + t, reqs, stride=2 * steps), :] = jnp.zeros_like(updates[t])
     mixed = (rms_scale(stage[0]) * ng_ref[...] * gate).astype(BF16)
     part_ref[...] = jnp.dot(mixed, wo_ref[...], preferred_element_type=F32).astype(BF16)
 
@@ -194,7 +195,7 @@
         out_shape=(
             jax.ShapeDtypeStruct((rows, width), BF16),
             jax.ShapeDtypeStruct((2 * rows, hk), F32),
-            jax.ShapeDtypeStruct((rows, hk), F32),
+            jax.ShapeDtypeStruct((2 * rows, hk), F32),
         ),
         in_specs=in_specs,
         out_specs=(VMEM,) * 3,
@@ -236,63 +237,52 @@
 
 def state_kernel(steps, side, *refs):
     keys, upds = refs[:side], refs[side : 2 * side]
-    mem_hbm, new_hbm, old, new, load_sem, store_sem = refs[2 * side :]
-    slots, size = old.shape[:2]
-    total = side**2
-
-    def at(b):
-        start = place_of(b // side, b % side, side) * size
-        return pl.ds(start, size)
-
-    def load(b):
-        return pltpu.make_async_copy(mem_hbm.at[at(b)], old.at[b % slots], load_sem.at[b % slots])
-
-    def store(b):
-        return pltpu.make_async_copy(new.at[b % slots], new_hbm.at[at(b)], store_sem.at[b % slots])
-
-    for b in range(slots - 1):
-        load(b).start()
-    for b in range(total):
-        load(b).wait()
-        if b + slots - 1 < total:
-            load(b + slots - 1).start()
-        if b >= slots:
-            store(b - slots).wait()
+    mem_ref, new_hbm, new, store_sem = refs[2 * side :]
+    size, hk = mem_ref.shape[0] // side**2, mem_ref.shape[-1]
+    shape = (2 * steps * size, hk * size)
+    own = lax.broadcasted_iota(jnp.int32, shape, 0) // (2 * steps) == (
+        lax.broadcasted_iota(jnp.int32, shape, 1) // hk
+    )
+    stores = []
+    for b in range(side**2):
         piece, block = b // side, b % side
-        height = 2 * steps * size
-        columns = keys[piece][pl.ds(height * block, height), :].T
+        height = 2 * steps
+        rows = pl.ds(height * size * block, height * size)
+        columns = keys[piece][rows, :].T
+        change = jnp.dot(
+            columns.astype(BF16),
+            jnp.where(own, jnp.concatenate([upds[piece][rows, :]] * size, 1), 0.0).astype(BF16),
+            preferred_element_type=F32,
+        )
+        start = place_of(piece, block, side) * size
         for r in range(size):
-            first = 2 * steps * r
-            memory = old[b % slots, r] * columns[:, first + steps : first + steps + 1]
-            for s in range(steps):
-                row = upds[piece][pl.ds(steps * (size * block + r) + s, 1), :]
-                memory = memory + columns[:, first + s : first + s + 1] * row
-            new[b % slots, r] = memory
-        store(b).start()
-    for b in range(total - slots, total):
-        store(b).wait()
+            decay = columns[:, height * r + steps : height * r + steps + 1]
+            new[b, r] = mem_ref[start + r] * decay + change[:, hk * r : hk * (r + 1)]
+        stores.append(
+            pltpu.make_async_copy(new.at[b], new_hbm.at[pl.ds(start, size)], store_sem.at[b])
+        )
+        stores[-1].start()
+    for store in stores:
+        store.wait()
 
 
 def new_memory(keys, updates, memory, steps):
     reqs, hk, _ = memory.shape
     side = len(keys)
-    size, slots = reqs // side**2, 4
     return pl.pallas_call(
         functools.partial(state_kernel, steps, side),
         out_shape=pltpu.HBM(memory.shape, F32),
-        in_specs=[VMEM] * (2 * side) + [HBM],
+        in_specs=[VMEM] * (2 * side + 1),
         out_specs=HBM,
         scratch_shapes=[
-            pltpu.VMEM((slots, size, hk, hk), F32),
-            pltpu.VMEM((slots, size, hk, hk), F32),
-            pltpu.SemaphoreType.DMA((slots,)),
-            pltpu.SemaphoreType.DMA((slots,)),
+            pltpu.VMEM((side**2, reqs // side**2, hk, hk), F32),
+            pltpu.SemaphoreType.DMA((side**2,)),
         ],
-        compiler_params=pltpu.CompilerParams(vmem_limit_bytes=8 * 1024 * 1024),
+        compiler_params=pltpu.CompilerParams(vmem_limit_bytes=16 * 1024 * 1024),
         cost_estimate=pl.CostEstimate(
             flops=9 * reqs * hk * hk, bytes_accessed=2 * reqs * hk * hk * 4, transcendentals=0
         ),
-    )(*keys, *updates, in_hbm(memory))
+    )(*keys, *updates, memory)
 
 
 def route_kernel(capacity, ids_ref, weights_ref, place_ref, combine_ref):
@@ -461,16 +451,13 @@
         output_weight,
         memory,
     )
-    parts, keys, updates = zip(
-        *(
-            attend(index, side, piece, operands, step_count)
-            for index, piece in enumerate(pieces)
-        )
-    )
+    done = [attend(index, side, piece, operands, step_count) for index, piece in enumerate(pieces)]
+    parts, keys, updates = zip(*done)
     returned = [move(part, False, -amount) for part, amount in zip(parts[1:], FAR)]
-    here, *others = middle(parts[0], returned)
+    new_state = new_memory(keys, updates, memory, step_count)
+    new_state, first = lax.optimization_barrier((new_state, parts[0]))
+    here, *others = middle(first, returned)
     terms = [here] + [move(other, True, -amount) for other, amount in zip(others, NEAR)]
-    new_state = new_memory(keys, updates, memory, step_count).reshape(kda_state.shape)
     device_count = grid_rows * grid_cols
     row_total, pick_count = local_req * step_count, expert_ids.shape[-1]
     capacity = max(2, 2 * row_total * pick_count // device_count)
@@ -487,7 +474,7 @@
         produced, ("erow", "ecol"), split_axis=0, concat_axis=0, tiled=True
     )
     mixed = combine_rows(returned, residual, combine, hidden_in.shape)
-    return (mixed, new_state)
+    return (mixed, new_state.reshape(kda_state.shape))
 
 
 def solution(mesh):

time: 103 us -> 101 us (0.981)
  blocking collectives: 26.9 us -> 51.3 us
  waiting for transfers between devices: 26.4 us -> 12.8 us
  Pallas kernels: 22.5 us -> 14.6 us
  starting transfers between devices: 23.9 us -> 19.2 us
    all_to_all x0 -> x1, blocking collectives: none -> 24.4 us  [local(): lax.all_to_all(produced, ('erow', 'ecol'), split_axis=0, concat_axis=0, t...]
    all_to_all x1 -> x0, waiting for transfers between devices: 9.87 us -> none  [local(): lax.all_to_all(produced, ('erow', 'ecol'), split_axis=0, concat_axis=0, t...]
    pallas_call x1, Pallas kernels: 10.5 us -> 3.63 us  [new_memory(): pl.pallas_call(functools.partial(state_kernel, steps, side), out_shape=pl...]
    all_to_all x1 -> x0, starting transfers between devices: 4.63 us -> none  [local(): lax.all_to_all(produced, ('erow', 'ecol'), split_axis=0, concat_axis=0, t...]
    ppermute x12, waiting for transfers between devices: 16.5 us -> 12.8 us  [shifted(): return lax.ppermute(array, ('erow', 'ecol'), pairs)]
    pallas_call x1, Pallas kernels: 5.04 us -> 4 us  [run_expert(): pl.pallas_call(expert_kernel, out_shape=jax.ShapeDtypeStruct(rows.shape,...]
  transfers between devices with their start and end apart: 13 -> 12, of which waited for: 8 -> 6; matrix products, arithmetic and copies ran while one was open for 0% -> 0% of each run, Pallas kernels for 15% -> 9%
where the time goes in v5:
time: 101 us
  blocking collectives  51.3 us (51%)
  starting transfers between devices  19.2 us (19%)
  Pallas kernels  14.6 us (14%)
  waiting for transfers between devices  12.8 us (13%)
  between operations  1.65 us (2%)
  local copies, waits for them, and re-layouts  1.04 us (1%)
    all_to_all x1, blocking collectives, local(): lax.all_to_all(outgoing, ('erow', 'ecol'), split_axis=0, concat_axis=0, t...  26.9 us
    all_to_all x1, blocking collectives, local(): lax.all_to_all(produced, ('erow', 'ecol'), split_axis=0, concat_axis=0, t...  24.4 us
    ppermute x12, starting transfers between devices, shifted(): return lax.ppermute(array, ('erow', 'ecol'), pairs)  19.2 us
    ppermute x12, waiting for transfers between devices, shifted(): return lax.ppermute(array, ('erow', 'ecol'), pairs)  12.8 us
    pallas_call x4, Pallas kernels, attend(): pl.pallas_call(functools.partial(attend_kernel, steps, index, side), out_...  4.93 us
    pallas_call x1, Pallas kernels, run_expert(): pl.pallas_call(expert_kernel, out_shape=jax.ShapeDtypeStruct(rows.shape,...  4 us
    pallas_call x1, Pallas kernels, new_memory(): pl.pallas_call(functools.partial(state_kernel, steps, side), out_shape=pl...  3.63 us
  transfers between devices with their start and end apart: 12, of which 6 were waited for; matrix products, arithmetic and copies ran while one was open for 0% of the time, Pallas kernels for 9%

profile of v5, /device:TPU:0, one launch (start us, length us, event | category | flops | bytes accessed | tf_op | source)
XLA Modules:
  0.0 100.6 jit_solution(15177877403780731204)
XLA Ops:
  0.6 3.4 %collective-permute-start = (bf16[4,4,2304]{2,1,0:T(4,128)(2,1)}, bf16[4,4,2304]{2,1,0:T(4,128)(2,1)S(1)}, u32[]{:S(2)}, u32[]{:S(2)}) collective-permute-start(bf16[4,4,2304]{2,1,0:T(4,128)(2,1)} %in_ref.1), channel_id=1, source_target_pairs={{0,2},{1,3},{2,0},{3,1},{4,6},{5,7},{6,4},{7,5},{8,10},{9,11},{10,... | collective-permute-start | bytes 221192 | tf_op jit(solution)/shard_map/ppermute | solution.py:82
  4.0 1.1 %collective-permute-start.2 = (bf16[4,4,2304]{2,1,0:T(4,128)(2,1)}, bf16[4,4,2304]{2,1,0:T(4,128)(2,1)S(1)}, u32[]{:S(2)}, u32[]{:S(2)}) collective-permute-start(bf16[4,4,2304]{2,1,0:T(4,128)(2,1)} %in_ref.1), channel_id=1, source_target_pairs={{0,3},{1,0},{2,1},{3,2},{4,7},{5,4},{6,5},{7,6},{8,11},{9,8},{10,9... | collective-permute-start | bytes 221192 | tf_op jit(solution)/shard_map/ppermute | solution.py:82
  5.0 1.0 collective-permute-start.1
  6.0 0.9 copy-done.10
  6.9 0.0 copy-start
  7.0 0.0 copy-start.1
  7.0 0.0 copy-start.2
  7.0 0.0 copy-start.3
  7.0 0.0 copy-start.4
  7.0 0.0 copy-start.5
  7.0 0.0 copy-start.6
  7.0 0.0 copy-start.7
  7.0 0.0 copy-start.8
  7.1 0.0 copy-start.9
  7.1 0.0 copy-start.11
  7.1 0.0 copy-start.12
  7.1 0.0 collective-permute-done.refs_0_
  7.1 1.4 %collective-permute-done.2.refs_2_ = bf16[4,4,2304]{2,1,0:T(4,128)(2,1)S(1)} collective-permute-done((bf16[4,4,2304]{2,1,0:T(4,128)(2,1)}, bf16[4,4,2304]{2,1,0:T(4,128)(2,1)S(1)}, u32[]{:S(2)}, u32[]{:S(2)}) %collective-permute-start.2) | collective-permute-done | bytes 73760 | tf_op jit(solution)/shard_map/ppermute | solution.py:82
  8.6 2.3 %collective-permute-done.1.refs_1_ = bf16[4,4,2304]{2,1,0:T(4,128)(2,1)S(1)} collective-permute-done((bf16[4,4,2304]{2,1,0:T(4,128)(2,1)}, bf16[4,4,2304]{2,1,0:T(4,128)(2,1)S(1)}, u32[]{:S(2)}, u32[]{:S(2)}) %collective-permute-start.1) | collective-permute-done | bytes 73760 | tf_op jit(solution)/shard_map/ppermute | solution.py:82
  10.8 3.1 %collective-permute-start.5 = (bf16[64,2304]{1,0:T(8,128)(2,1)S(1)}, bf16[64,2304]{1,0:T(8,128)(2,1)S(1)}, u32[]{:S(2)}, u32[]{:S(2)}) collective-permute-start(bf16[64,2304]{1,0:T(8,128)(2,1)S(1)} %shard_map.205.refs_0_), channel_id=1, source_target_pairs={{0,8},{1,9},{2,10},{3,11},{4,12},{5,13},{6,14},{7,15},{8,0},{9,1},... | collective-permute-start | bytes 884744 | tf_op jit(solution)/shard_map/ppermute | solution.py:82
  14.0 0.6 collective-permute-start.4
  14.5 2.6 %collective-permute-start.3 = (bf16[64,2304]{1,0:T(8,128)(2,1)S(1)}, bf16[64,2304]{1,0:T(8,128)(2,1)S(1)}, u32[]{:S(2)}, u32[]{:S(2)}) collective-permute-start(bf16[64,2304]{1,0:T(8,128)(2,1)S(1)} %shard_map.205.refs_0_), channel_id=1, source_target_pairs={{0,12},{1,13},{2,14},{3,15},{4,0},{5,1},{6,2},{7,3},{8,4},{9,5},{1... | collective-permute-start | bytes 884744 | tf_op jit(solution)/shard_map/ppermute | solution.py:82
  17.8 1.4 %collective-permute-done.5.refs_0_ = bf16[64,2304]{1,0:T(8,128)(2,1)S(1)} collective-permute-done((bf16[64,2304]{1,0:T(8,128)(2,1)S(1)}, bf16[64,2304]{1,0:T(8,128)(2,1)S(1)}, u32[]{:S(2)}, u32[]{:S(2)}) %collective-permute-start.5) | collective-permute-done | bytes 294944 | tf_op jit(solution)/shard_map/ppermute | solution.py:82
  19.2 0.0 copy-done
  19.2 0.0 copy-done.1
  19.2 0.0 copy-done.2
  19.2 0.0 copy-done.3
  19.2 0.0 copy-done.4
  19.2 0.0 copy-done.5
  19.2 0.0 copy-done.6
  19.3 0.0 copy-done.7
  19.3 1.2 %shard_map.209 = (bf16[64,2304]{1,0:T(8,128)(2,1)S(1)}, f32[128,128]{1,0:T(8,128)S(1)}, f32[128,128]{1,0:T(8,128)S(1)}) custom-call(bf16[64,2304]{1,0:T(8,128)(2,1)S(1)} %collective-permute-done.5.refs_0_, bf16[2304,128]{1,0:T(8,128)(2,1)S(1)} %copy-done.1, bf16[2304,128]{1,0:T(8,128)(2,1)S(1)} %copy-done.2, bf16[2304,128]{1,0:T(8,128)(2,1)S(1)} %copy-done.3, ...), custom_call_target="tpu_custom_call" | custom-call | flops 1500000000 | bytes 2000000 | tf_op jit(solution)/shard_map/pallas_call | solution.py:193
  20.5 3.2 %collective-permute-start.8 = (bf16[64,2304]{1,0:T(8,128)(2,1)S(1)}, bf16[64,2304]{1,0:T(8,128)(2,1)S(1)}, u32[]{:S(2)}, u32[]{:S(2)}) collective-permute-start(bf16[64,2304]{1,0:T(8,128)(2,1)S(1)} %get-tuple-element.37), channel_id=1, source_target_pairs={{0,8},{1,9},{2,10},{3,11},{4,12},{5,13},{6,14},{7,15},{8,0},{9,1},... | collective-permute-start | bytes 884744 | tf_op jit(solution)/shard_map/ppermute | solution.py:82
  23.7 0.0 collective-permute-done.4.refs_0_
  23.7 1.2 %shard_map.208 = (bf16[64,2304]{1,0:T(8,128)(2,1)S(1)}, f32[128,128]{1,0:T(8,128)S(1)}, f32[128,128]{1,0:T(8,128)S(1)}) custom-call(bf16[64,2304]{1,0:T(8,128)(2,1)S(1)} %collective-permute-done.4.refs_0_, bf16[2304,128]{1,0:T(8,128)(2,1)S(1)} %copy-done.1, bf16[2304,128]{1,0:T(8,128)(2,1)S(1)} %copy-done.2, bf16[2304,128]{1,0:T(8,128)(2,1)S(1)} %copy-done.3, ...), custom_call_target="tpu_custom_call" | custom-call | flops 1500000000 | bytes 2000000 | tf_op jit(solution)/shard_map/pallas_call | solution.py:193
  25.0 1.2 %collective-permute-start.7 = (bf16[64,2304]{1,0:T(8,128)(2,1)S(1)}, bf16[64,2304]{1,0:T(8,128)(2,1)S(1)}, u32[]{:S(2)}, u32[]{:S(2)}) collective-permute-start(bf16[64,2304]{1,0:T(8,128)(2,1)S(1)} %get-tuple-element.36), channel_id=1, source_target_pairs={{0,12},{1,13},{2,14},{3,15},{4,0},{5,1},{6,2},{7,3},{8,4},{9,5},{1... | collective-permute-start | bytes 884744 | tf_op jit(solution)/shard_map/ppermute | solution.py:82
  26.2 0.0 collective-permute-done.3.refs_0_
  26.2 1.2 %shard_map.207 = (bf16[64,2304]{1,0:T(8,128)(2,1)S(1)}, f32[128,128]{1,0:T(8,128)S(1)}, f32[128,128]{1,0:T(8,128)S(1)}) custom-call(bf16[64,2304]{1,0:T(8,128)(2,1)S(1)} %collective-permute-done.3.refs_0_, bf16[2304,128]{1,0:T(8,128)(2,1)S(1)} %copy-done.1, bf16[2304,128]{1,0:T(8,128)(2,1)S(1)} %copy-done.2, bf16[2304,128]{1,0:T(8,128)(2,1)S(1)} %copy-done.3, ...), custom_call_target="tpu_custom_call" | custom-call | flops 1500000000 | bytes 2000000 | tf_op jit(solution)/shard_map/pallas_call | solution.py:193
  27.4 1.0 collective-permute-start.6
  28.4 1.2 %shard_map.206 = (bf16[64,2304]{1,0:T(8,128)(2,1)S(1)}, f32[128,128]{1,0:T(8,128)S(1)}, f32[128,128]{1,0:T(8,128)S(1)}) custom-call(bf16[64,2304]{1,0:T(8,128)(2,1)S(1)} %shard_map.205.refs_0_, bf16[2304,128]{1,0:T(8,128)(2,1)S(1)} %copy-done.1, bf16[2304,128]{1,0:T(8,128)(2,1)S(1)} %copy-done.2, bf16[2304,128]{1,0:T(8,128)(2,1)S(1)} %copy-done.3, ...), custom_call_target="tpu_custom_call" | custom-call | flops 1500000000 | bytes 2000000 | tf_op jit(solution)/shard_map/pallas_call | solution.py:193
  29.6 0.0 slice-start
  29.6 0.0 slice-start.2
  29.6 0.0 slice-start.4
  29.6 3.6 %shard_map.210 = f32[64,128,128]{2,1,0:T(8,128)} custom-call(f32[128,128]{1,0:T(8,128)S(1)} %get-tuple-element.25.refs_0_, f32[128,128]{1,0:T(8,128)S(1)} %get-tuple-element.26.refs_1_, f32[128,128]{1,0:T(8,128)S(1)} %get-tuple-element.27.refs_2_, f32[128,128]{1,0:T(8,128)S(1)} %get-tuple-element.28.refs_3_, f32[128,128]{1,0:T(8,128)S(1)} %get-tuple-element.29.refs_4_, ...), custom_call_target="tpu_custom_call" | custom-call | flops 9437184 | bytes 8388608 | tf_op jit(solution)/shard_map/pallas_call | solution.py:272
  33.3 0.0 collective-permute-done.8.refs_2_
  33.3 0.0 collective-permute-done.7.refs_1_
  33.3 2.9 %collective-permute-done.6.refs_0_ = bf16[64,2304]{1,0:T(8,128)(2,1)S(1)} collective-permute-done((bf16[64,2304]{1,0:T(8,128)(2,1)S(1)}, bf16[64,2304]{1,0:T(8,128)(2,1)S(1)}, u32[]{:S(2)}, u32[]{:S(2)}) %collective-permute-start.6) | collective-permute-done | bytes 294944 | tf_op jit(solution)/shard_map/ppermute | solution.py:82
  36.2 0.1 shard_map.211
  36.3 0.1 collective-permute-start.9
  36.4 1.6 %collective-permute-start.10 = (bf16[16,2304]{1,0:T(8,128)(2,1)S(1)}, bf16[16,2304]{1,0:T(8,128)(2,1)S(1)}, u32[]{:S(2)}, u32[]{:S(2)}) collective-permute-start(bf16[16,2304]{1,0:T(8,128)(2,1)S(1)} %get-tuple-element.40), channel_id=1, source_target_pairs={{0,3},{1,0},{2,1},{3,2},{4,7},{5,4},{6,5},{7,6},{8,11},{9,8},{10,9... | collective-permute-start | bytes 221192 | tf_op jit(solution)/shard_map/ppermute | solution.py:82
  38.1 0.5 collective-permute-start.11
  38.5 0.2 shard_map.204
  38.8 3.5 %collective-permute-done.9.refs_1_ = bf16[16,2304]{1,0:T(8,128)(2,1)S(1)} collective-permute-done((bf16[16,2304]{1,0:T(8,128)(2,1)S(1)}, bf16[16,2304]{1,0:T(8,128)(2,1)S(1)}, u32[]{:S(2)}, u32[]{:S(2)}) %collective-permute-start.9) | collective-permute-done | bytes 73760 | tf_op jit(solution)/shard_map/ppermute | solution.py:82
  42.3 0.0 collective-permute-done.10.refs_2_
  42.3 1.4 %collective-permute-done.11.refs_3_ = bf16[16,2304]{1,0:T(8,128)(2,1)S(1)} collective-permute-done((bf16[16,2304]{1,0:T(8,128)(2,1)S(1)}, bf16[16,2304]{1,0:T(8,128)(2,1)S(1)}, u32[]{:S(2)}, u32[]{:S(2)}) %collective-permute-start.11) | collective-permute-done | bytes 73760 | tf_op jit(solution)/shard_map/ppermute | solution.py:82
  43.6 0.0 copy-done.15
  43.7 0.6 shard_map.212
  44.3 26.9 %all_to_all.10.rows_ref = bf16[128,2,2304]{2,1,0:T(2,128)(2,1)S(1)} all-to-all(bf16[128,2,2304]{2,1,0:T(2,128)(2,1)S(1)} %get-tuple-element.42), channel_id=1, replica_groups=mesh['erow'=8,'ecol'=16] {'erow','ecol'}, dimensions={0} | all-to-all | bytes 2359296 | tf_op jit(solution)/shard_map/all_to_all | solution.py:469
  71.2 0.0 slice-done.1
  71.2 0.0 slice-done.3
  71.2 0.0 slice-done.5
  71.2 4.0 %shard_map.213 = bf16[128,2,2304]{2,1,0:T(2,128)(2,1)S(1)} custom-call(bf16[128,2,2304]{2,1,0:T(2,128)(2,1)S(1)} %all_to_all.10.rows_ref, bf16[2304,1024]{1,0:T(8,128)(2,1)S(1)} %bitcast.17, bf16[2304,1024]{1,0:T(8,128)(2,1)S(1)} %bitcast.20, bf16[1024,2304]{1,0:T(8,128)(2,1)S(1)} %bitcast.23), custom_call_target="tpu_custom_call" | custom-call | flops 3623878656 | bytes 16515072 | tf_op jit(solution)/shard_map/pallas_call | solution.py:366
  75.2 24.4 %all_to_all.11.rows_ref = bf16[128,2,2304]{2,1,0:T(2,128)(2,1)S(1)} all-to-all(bf16[128,2,2304]{2,1,0:T(2,128)(2,1)S(1)} %shard_map.213), channel_id=1, replica_groups=mesh['erow'=8,'ecol'=16] {'erow','ecol'}, dimensions={0} | all-to-all | bytes 2359296 | tf_op jit(solution)/shard_map/all_to_all | solution.py:473
  99.6 1.0 shard_map.214
  (21 shorter events, 0.1 us)
Async XLA Ops:
  0.6 6.5 %collective-permute-start = (bf16[4,4,2304]{2,1,0:T(4,128)(2,1)}, bf16[4,4,2304]{2,1,0:T(4,128)(2,1)S(1)}, u32[]{:S(2)}, u32[]{:S(2)}) collective-permute-start(bf16[4,4,2304]{2,1,0:T(4,128)(2,1)} %in_ref.1), channel_id=1, source_target_pairs={{0,2},{1,3},{2,0},{3,1},{4,6},{5,7},{6,4},{7,5},{8,10},{9,11},{10,... | collective-permute-start | bytes 221192 | tf_op jit(solution)/shard_map/ppermute | solution.py:82
  4.0 4.6 %collective-permute-start.2 = (bf16[4,4,2304]{2,1,0:T(4,128)(2,1)}, bf16[4,4,2304]{2,1,0:T(4,128)(2,1)S(1)}, u32[]{:S(2)}, u32[]{:S(2)}) collective-permute-start(bf16[4,4,2304]{2,1,0:T(4,128)(2,1)} %in_ref.1), channel_id=1, source_target_pairs={{0,3},{1,0},{2,1},{3,2},{4,7},{5,4},{6,5},{7,6},{8,11},{9,8},{10,9... | collective-permute-start | bytes 221192 | tf_op jit(solution)/shard_map/ppermute | solution.py:82
  5.0 5.8 %collective-permute-start.1 = (bf16[4,4,2304]{2,1,0:T(4,128)(2,1)}, bf16[4,4,2304]{2,1,0:T(4,128)(2,1)S(1)}, u32[]{:S(2)}, u32[]{:S(2)}) collective-permute-start(bf16[4,4,2304]{2,1,0:T(4,128)(2,1)} %in_ref.1), channel_id=1, source_target_pairs={{0,1},{1,2},{2,3},{3,0},{4,5},{5,6},{6,7},{7,4},{8,9},{9,10},{10,1... | collective-permute-start | bytes 221192 | tf_op jit(solution)/shard_map/ppermute | solution.py:82
  6.0 0.9 copy-start.10
  6.9 12.3 %copy-start = (f32[64,1,128,128]{3,2,1,0:T(8,128)S(1)}, f32[64,1,128,128]{3,2,1,0:T(8,128)}, u32[]{:S(2)}) copy-start(f32[64,1,128,128]{3,2,1,0:T(8,128)} %param.21) | copy-start | bytes 12582916
  7.0 12.3 %copy-start.1 = (bf16[2304,128]{1,0:T(8,128)(2,1)S(1)}, bf16[2304,128]{1,0:T(8,128)(2,1)}, u32[]{:S(2)}) copy-start(bf16[2304,128]{1,0:T(8,128)(2,1)} %refs_1_.7) | copy-start | bytes 1769476
  7.0 12.2 %copy-start.2 = (bf16[2304,128]{1,0:T(8,128)(2,1)S(1)}, bf16[2304,128]{1,0:T(8,128)(2,1)}, u32[]{:S(2)}) copy-start(bf16[2304,128]{1,0:T(8,128)(2,1)} %refs_2_.7) | copy-start | bytes 1769476
  7.0 12.2 %copy-start.3 = (bf16[2304,128]{1,0:T(8,128)(2,1)S(1)}, bf16[2304,128]{1,0:T(8,128)(2,1)}, u32[]{:S(2)}) copy-start(bf16[2304,128]{1,0:T(8,128)(2,1)} %refs_3_.7) | copy-start | bytes 1769476
  7.0 12.2 %copy-start.4 = (bf16[2304,128]{1,0:T(8,128)(2,1)S(1)}, bf16[2304,128]{1,0:T(8,128)(2,1)}, u32[]{:S(2)}) copy-start(bf16[2304,128]{1,0:T(8,128)(2,1)} %refs_8_.7) | copy-start | bytes 1769476
  7.0 12.2 %copy-start.5 = (bf16[2304,128]{1,0:T(8,128)(2,1)S(1)}, bf16[2304,128]{1,0:T(8,128)(2,1)}, u32[]{:S(2)}) copy-start(bf16[2304,128]{1,0:T(8,128)(2,1)} %refs_9_.7) | copy-start | bytes 1769476
  7.0 12.2 %copy-start.6 = (bf16[128,2304]{1,0:T(8,128)(2,1)S(1)}, bf16[128,2304]{1,0:T(8,128)(2,1)}, u32[]{:S(2)}) copy-start(bf16[128,2304]{1,0:T(8,128)(2,1)} %refs_12_.7) | copy-start | bytes 1769476
  7.0 12.2 %copy-start.7 = (bf16[128,128]{1,0:T(8,128)(2,1)S(1)}, bf16[128,128]{1,0:T(8,128)(2,1)}, u32[]{:S(2)}) copy-start(bf16[128,128]{1,0:T(8,128)(2,1)} %refs_10_.7) | copy-start | bytes 98308
  7.0 12.2 %copy-start.8 = (bf16[128,128]{1,0:T(8,128)(2,1)S(1)}, bf16[128,128]{1,0:T(8,128)(2,1)}, u32[]{:S(2)}) copy-start(bf16[128,128]{1,0:T(8,128)(2,1)} %refs_11_.7) | copy-start | bytes 98308
  7.1 12.2 %copy-start.9 = (bf16[2304,1]{0,1:T(2,128)(2,1)S(1)}, bf16[2304,1]{0,1:T(2,128)(2,1)}, u32[]{:S(2)}) copy-start(bf16[2304,1]{0,1:T(2,128)(2,1)} %param.25) | copy-start | bytes 13828
  7.1 12.2 %copy-start.11 = (f32[128]{0:T(128)S(1)}, f32[128]{0:T(128)}, u32[]{:S(2)}) copy-start(f32[128]{0:T(128)} %param.29) | copy-start | bytes 1540
  7.1 12.2 %copy-start.12 = (f32[128]{0:T(128)S(1)}, f32[128]{0:T(128)}, u32[]{:S(2)}) copy-start(f32[128]{0:T(128)} %param.32) | copy-start | bytes 1540
  10.8 8.4 %collective-permute-start.5 = (bf16[64,2304]{1,0:T(8,128)(2,1)S(1)}, bf16[64,2304]{1,0:T(8,128)(2,1)S(1)}, u32[]{:S(2)}, u32[]{:S(2)}) collective-permute-start(bf16[64,2304]{1,0:T(8,128)(2,1)S(1)} %shard_map.205.refs_0_), channel_id=1, source_target_pairs={{0,8},{1,9},{2,10},{3,11},{4,12},{5,13},{6,14},{7,15},{8,0},{9,1},... | collective-permute-start | bytes 884744 | tf_op jit(solution)/shard_map/ppermute | solution.py:82
  14.0 9.8 %collective-permute-start.4 = (bf16[64,2304]{1,0:T(8,128)(2,1)S(1)}, bf16[64,2304]{1,0:T(8,128)(2,1)S(1)}, u32[]{:S(2)}, u32[]{:S(2)}) collective-permute-start(bf16[64,2304]{1,0:T(8,128)(2,1)S(1)} %shard_map.205.refs_0_), channel_id=1, source_target_pairs={{0,4},{1,5},{2,6},{3,7},{4,8},{5,9},{6,10},{7,11},{8,12},{9,13},{1... | collective-permute-start | bytes 884744 | tf_op jit(solution)/shard_map/ppermute | solution.py:82
  14.5 11.6 %collective-permute-start.3 = (bf16[64,2304]{1,0:T(8,128)(2,1)S(1)}, bf16[64,2304]{1,0:T(8,128)(2,1)S(1)}, u32[]{:S(2)}, u32[]{:S(2)}) collective-permute-start(bf16[64,2304]{1,0:T(8,128)(2,1)S(1)} %shard_map.205.refs_0_), channel_id=1, source_target_pairs={{0,12},{1,13},{2,14},{3,15},{4,0},{5,1},{6,2},{7,3},{8,4},{9,5},{1... | collective-permute-start | bytes 884744 | tf_op jit(solution)/shard_map/ppermute | solution.py:82
  20.5 12.7 %collective-permute-start.8 = (bf16[64,2304]{1,0:T(8,128)(2,1)S(1)}, bf16[64,2304]{1,0:T(8,128)(2,1)S(1)}, u32[]{:S(2)}, u32[]{:S(2)}) collective-permute-start(bf16[64,2304]{1,0:T(8,128)(2,1)S(1)} %get-tuple-element.37), channel_id=1, source_target_pairs={{0,8},{1,9},{2,10},{3,11},{4,12},{5,13},{6,14},{7,15},{8,0},{9,1},... | collective-permute-start | bytes 884744 | tf_op jit(solution)/shard_map/ppermute | solution.py:82
  25.0 8.3 %collective-permute-start.7 = (bf16[64,2304]{1,0:T(8,128)(2,1)S(1)}, bf16[64,2304]{1,0:T(8,128)(2,1)S(1)}, u32[]{:S(2)}, u32[]{:S(2)}) collective-permute-start(bf16[64,2304]{1,0:T(8,128)(2,1)S(1)} %get-tuple-element.36), channel_id=1, source_target_pairs={{0,12},{1,13},{2,14},{3,15},{4,0},{5,1},{6,2},{7,3},{8,4},{9,5},{1... | collective-permute-start | bytes 884744 | tf_op jit(solution)/shard_map/ppermute | solution.py:82
  27.4 8.8 %collective-permute-start.6 = (bf16[64,2304]{1,0:T(8,128)(2,1)S(1)}, bf16[64,2304]{1,0:T(8,128)(2,1)S(1)}, u32[]{:S(2)}, u32[]{:S(2)}) collective-permute-start(bf16[64,2304]{1,0:T(8,128)(2,1)S(1)} %get-tuple-element.35), channel_id=1, source_target_pairs={{0,4},{1,5},{2,6},{3,7},{4,8},{5,9},{6,10},{7,11},{8,12},{9,13},{1... | collective-permute-start | bytes 884744 | tf_op jit(solution)/shard_map/ppermute | solution.py:82
  28.4 10.2 %copy-start.13 = (s32[4,4,8]{2,1,0:T(4,128)S(1)}, s32[4,4,8]{2,1,0:T(4,128)}, u32[]{:S(2)}) copy-start(s32[4,4,8]{2,1,0:T(4,128)} %ids_ref.1) | copy-start | bytes 1540
  28.4 10.2 %copy-start.14 = (f32[4,4,8]{2,1,0:T(4,128)S(1)}, f32[4,4,8]{2,1,0:T(4,128)}, u32[]{:S(2)}) copy-start(f32[4,4,8]{2,1,0:T(4,128)} %weights_ref.1) | copy-start | bytes 1540
  28.4 15.3 %copy-start.15 = (f32[2304]{0:T(1024)S(1)}, f32[2304]{0:T(1024)}, u32[]{:S(2)}) copy-start(f32[2304]{0:T(1024)} %gain_ref.1) | copy-start | bytes 27652
  29.6 41.5 %slice-start = ((s8[4718592]{0:T(1024)(128)(4,1)}), s8[4194304]{0:T(1024)(128)(4,1)S(1)}, s32[]{:S(2)}) async-start(s8[4718592]{0:T(1024)(128)(4,1)} %bitcast.15), calls=%async_computation.2 | async-start | bytes 8388608
  29.6 41.5 %slice-start.2 = ((s8[4718592]{0:T(1024)(128)(4,1)}), s8[4194304]{0:T(1024)(128)(4,1)S(1)}, s32[]{:S(2)}) async-start(s8[4718592]{0:T(1024)(128)(4,1)} %bitcast.18), calls=%async_computation.4 | async-start | bytes 8388608
  29.6 41.5 %slice-start.4 = ((s8[4718592]{0:T(1024)(128)(4,1)}), s8[4194304]{0:T(1024)(128)(4,1)S(1)}, s32[]{:S(2)}) async-start(s8[4718592]{0:T(1024)(128)(4,1)} %bitcast.21), calls=%async_computation.6 | async-start | bytes 8388608
  36.3 5.9 %collective-permute-start.9 = (bf16[16,2304]{1,0:T(8,128)(2,1)S(1)}, bf16[16,2304]{1,0:T(8,128)(2,1)S(1)}, u32[]{:S(2)}, u32[]{:S(2)}) collective-permute-start(bf16[16,2304]{1,0:T(8,128)(2,1)S(1)} %get-tuple-element.39), channel_id=1, source_target_pairs={{0,2},{1,3},{2,0},{3,1},{4,6},{5,7},{6,4},{7,5},{8,10},{9,11},{10,... | collective-permute-start | bytes 221192 | tf_op jit(solution)/shard_map/ppermute | solution.py:82
  36.4 5.8 %collective-permute-start.10 = (bf16[16,2304]{1,0:T(8,128)(2,1)S(1)}, bf16[16,2304]{1,0:T(8,128)(2,1)S(1)}, u32[]{:S(2)}, u32[]{:S(2)}) collective-permute-start(bf16[16,2304]{1,0:T(8,128)(2,1)S(1)} %get-tuple-element.40), channel_id=1, source_target_pairs={{0,3},{1,0},{2,1},{3,2},{4,7},{5,4},{6,5},{7,6},{8,11},{9,8},{10,9... | collective-permute-start | bytes 221192 | tf_op jit(solution)/shard_map/ppermute | solution.py:82
  38.1 5.6 %collective-permute-start.11 = (bf16[16,2304]{1,0:T(8,128)(2,1)S(1)}, bf16[16,2304]{1,0:T(8,128)(2,1)S(1)}, u32[]{:S(2)}, u32[]{:S(2)}) collective-permute-start(bf16[16,2304]{1,0:T(8,128)(2,1)S(1)} %get-tuple-element.41), channel_id=1, source_target_pairs={{0,1},{1,2},{2,3},{3,0},{4,5},{5,6},{6,7},{7,4},{8,9},{9,10},{10,1... | collective-permute-start | bytes 221192 | tf_op jit(solution)/shard_map/ppermute | solution.py:82
  43.6 27.5 %slice-start.1 = ((s8[4718592]{0:T(1024)(128)(4,1)}), s8[524288]{0:T(1024)(128)(4,1)S(1)}, s32[]{:S(2)}) async-start(s8[4718592]{0:T(1024)(128)(4,1)} %bitcast.15), calls=%async_computation.3 | async-start | bytes 1048576
  43.6 27.5 %slice-start.3 = ((s8[4718592]{0:T(1024)(128)(4,1)}), s8[524288]{0:T(1024)(128)(4,1)S(1)}, s32[]{:S(2)}) async-start(s8[4718592]{0:T(1024)(128)(4,1)} %bitcast.18), calls=%async_computation.5 | async-start | bytes 1048576
  43.6 27.5 %slice-start.5 = ((s8[4718592]{0:T(1024)(128)(4,1)}), s8[524288]{0:T(1024)(128)(4,1)S(1)}, s32[]{:S(2)}) async-start(s8[4718592]{0:T(1024)(128)(4,1)} %bitcast.21), calls=%async_computation.7 | async-start | bytes 1048576

commit v6 on v5

--- a/solution.py
+++ b/solution.py
@@ -64,7 +64,7 @@
     )(own, *blocks)
 
 
-NEAR = (2, 1, 3)
+NEAR = (1, 2, 3)
 FAR = (3, 1, 2)
 
 

time: 101 us -> 101 us (level)
  waiting for transfers between devices: 12.8 us -> 11.1 us
  starting transfers between devices: 19.2 us -> 20.7 us
    ppermute x12, waiting for transfers between devices: 12.8 us -> 11.1 us  [shifted(): return lax.ppermute(array, ('erow', 'ecol'), pairs)]
    ppermute x12, starting transfers between devices: 19.2 us -> 20.7 us  [shifted(): return lax.ppermute(array, ('erow', 'ecol'), pairs)]
where the time goes in v6:
time: 101 us; the launch traced here: 100 us
  blocking collectives  51.3 us (51%)
  starting transfers between devices  20.7 us (20%)
  Pallas kernels  14.6 us (14%)
  waiting for transfers between devices  11.1 us (11%)
  between operations  1.65 us (2%)
  local copies, waits for them, and re-layouts  1.04 us (1%)
    all_to_all x1, blocking collectives, local(): lax.all_to_all(outgoing, ('erow', 'ecol'), split_axis=0, concat_axis=0, t...  26.9 us
    all_to_all x1, blocking collectives, local(): lax.all_to_all(produced, ('erow', 'ecol'), split_axis=0, concat_axis=0, t...  24.4 us
    ppermute x12, starting transfers between devices, shifted(): return lax.ppermute(array, ('erow', 'ecol'), pairs)  20.7 us
    ppermute x12, waiting for transfers between devices, shifted(): return lax.ppermute(array, ('erow', 'ecol'), pairs)  11.1 us
    pallas_call x4, Pallas kernels, attend(): pl.pallas_call(functools.partial(attend_kernel, steps, index, side), out_...  4.93 us
    pallas_call x1, Pallas kernels, run_expert(): pl.pallas_call(expert_kernel, out_shape=jax.ShapeDtypeStruct(rows.shape,...  3.99 us
    pallas_call x1, Pallas kernels, new_memory(): pl.pallas_call(functools.partial(state_kernel, steps, side), out_shape=pl...  3.64 us
  transfers between devices with their start and end apart: 12, of which 6 were waited for; matrix products, arithmetic and copies ran while one was open for 0% of the time, Pallas kernels for 9%

profile of v6, /device:TPU:0, one launch (start us, length us, event | category | flops | bytes accessed | tf_op | source)
XLA Modules:
  0.0 100.3 jit_solution(3995415304149404661)
XLA Ops:
  0.6 1.7 %collective-permute-start = (bf16[4,4,2304]{2,1,0:T(4,128)(2,1)}, bf16[4,4,2304]{2,1,0:T(4,128)(2,1)S(1)}, u32[]{:S(2)}, u32[]{:S(2)}) collective-permute-start(bf16[4,4,2304]{2,1,0:T(4,128)(2,1)} %in_ref.1), channel_id=1, source_target_pairs={{0,1},{1,2},{2,3},{3,0},{4,5},{5,6},{6,7},{7,4},{8,9},{9,10},{10,1... | collective-permute-start | bytes 221192 | tf_op jit(solution)/shard_map/ppermute | solution.py:82
  2.4 1.6 %collective-permute-start.2 = (bf16[4,4,2304]{2,1,0:T(4,128)(2,1)}, bf16[4,4,2304]{2,1,0:T(4,128)(2,1)S(1)}, u32[]{:S(2)}, u32[]{:S(2)}) collective-permute-start(bf16[4,4,2304]{2,1,0:T(4,128)(2,1)} %in_ref.1), channel_id=1, source_target_pairs={{0,3},{1,0},{2,1},{3,2},{4,7},{5,4},{6,5},{7,6},{8,11},{9,8},{10,9... | collective-permute-start | bytes 221192 | tf_op jit(solution)/shard_map/ppermute | solution.py:82
  3.9 2.1 %collective-permute-start.1 = (bf16[4,4,2304]{2,1,0:T(4,128)(2,1)}, bf16[4,4,2304]{2,1,0:T(4,128)(2,1)S(1)}, u32[]{:S(2)}, u32[]{:S(2)}) collective-permute-start(bf16[4,4,2304]{2,1,0:T(4,128)(2,1)} %in_ref.1), channel_id=1, source_target_pairs={{0,2},{1,3},{2,0},{3,1},{4,6},{5,7},{6,4},{7,5},{8,10},{9,11},{10,... | collective-permute-start | bytes 221192 | tf_op jit(solution)/shard_map/ppermute | solution.py:82
  6.0 0.9 copy-done.10
  6.9 0.0 copy-start
  6.9 0.0 copy-start.1
  7.0 0.0 copy-start.2
  7.0 0.0 copy-start.3
  7.0 0.0 copy-start.4
  7.0 0.0 copy-start.5
  7.0 0.0 copy-start.6
  7.0 0.0 copy-start.7
  7.0 0.0 copy-start.8
  7.0 0.0 copy-start.9
  7.1 0.0 copy-start.11
  7.1 0.0 copy-start.12
  7.1 0.0 collective-permute-done.refs_0_
  7.1 0.0 collective-permute-done.2.refs_2_
  7.1 2.9 %collective-permute-done.1.refs_1_ = bf16[4,4,2304]{2,1,0:T(4,128)(2,1)S(1)} collective-permute-done((bf16[4,4,2304]{2,1,0:T(4,128)(2,1)}, bf16[4,4,2304]{2,1,0:T(4,128)(2,1)S(1)}, u32[]{:S(2)}, u32[]{:S(2)}) %collective-permute-start.1) | collective-permute-done | bytes 73760 | tf_op jit(solution)/shard_map/ppermute | solution.py:82
  10.0 3.2 %collective-permute-start.5 = (bf16[64,2304]{1,0:T(8,128)(2,1)S(1)}, bf16[64,2304]{1,0:T(8,128)(2,1)S(1)}, u32[]{:S(2)}, u32[]{:S(2)}) collective-permute-start(bf16[64,2304]{1,0:T(8,128)(2,1)S(1)} %shard_map.205.refs_0_), channel_id=1, source_target_pairs={{0,8},{1,9},{2,10},{3,11},{4,12},{5,13},{6,14},{7,15},{8,0},{9,1},... | collective-permute-start | bytes 884744 | tf_op jit(solution)/shard_map/ppermute | solution.py:82
  13.2 0.6 collective-permute-start.4
  13.8 2.6 %collective-permute-start.3 = (bf16[64,2304]{1,0:T(8,128)(2,1)S(1)}, bf16[64,2304]{1,0:T(8,128)(2,1)S(1)}, u32[]{:S(2)}, u32[]{:S(2)}) collective-permute-start(bf16[64,2304]{1,0:T(8,128)(2,1)S(1)} %shard_map.205.refs_0_), channel_id=1, source_target_pairs={{0,12},{1,13},{2,14},{3,15},{4,0},{5,1},{6,2},{7,3},{8,4},{9,5},{1... | collective-permute-start | bytes 884744 | tf_op jit(solution)/shard_map/ppermute | solution.py:82
  17.1 1.3 %collective-permute-done.5.refs_0_ = bf16[64,2304]{1,0:T(8,128)(2,1)S(1)} collective-permute-done((bf16[64,2304]{1,0:T(8,128)(2,1)S(1)}, bf16[64,2304]{1,0:T(8,128)(2,1)S(1)}, u32[]{:S(2)}, u32[]{:S(2)}) %collective-permute-start.5) | collective-permute-done | bytes 294944 | tf_op jit(solution)/shard_map/ppermute | solution.py:82
  18.4 0.0 copy-done
  18.4 0.0 copy-done.1
  18.4 0.0 copy-done.2
  18.4 0.0 copy-done.3
  18.4 0.0 copy-done.4
  18.4 0.0 copy-done.5
  18.4 0.0 copy-done.6
  18.5 1.2 %shard_map.209 = (bf16[64,2304]{1,0:T(8,128)(2,1)S(1)}, f32[128,128]{1,0:T(8,128)S(1)}, f32[128,128]{1,0:T(8,128)S(1)}) custom-call(bf16[64,2304]{1,0:T(8,128)(2,1)S(1)} %collective-permute-done.5.refs_0_, bf16[2304,128]{1,0:T(8,128)(2,1)S(1)} %copy-done.1, bf16[2304,128]{1,0:T(8,128)(2,1)S(1)} %copy-done.2, bf16[2304,128]{1,0:T(8,128)(2,1)S(1)} %copy-done.3, ...), custom_call_target="tpu_custom_call" | custom-call | flops 1500000000 | bytes 2000000 | tf_op jit(solution)/shard_map/pallas_call | solution.py:193
  19.7 3.3 %collective-permute-start.8 = (bf16[64,2304]{1,0:T(8,128)(2,1)S(1)}, bf16[64,2304]{1,0:T(8,128)(2,1)S(1)}, u32[]{:S(2)}, u32[]{:S(2)}) collective-permute-start(bf16[64,2304]{1,0:T(8,128)(2,1)S(1)} %get-tuple-element.37), channel_id=1, source_target_pairs={{0,8},{1,9},{2,10},{3,11},{4,12},{5,13},{6,14},{7,15},{8,0},{9,1},... | collective-permute-start | bytes 884744 | tf_op jit(solution)/shard_map/ppermute | solution.py:82
  23.0 0.0 collective-permute-done.4.refs_0_
  23.0 1.2 %shard_map.208 = (bf16[64,2304]{1,0:T(8,128)(2,1)S(1)}, f32[128,128]{1,0:T(8,128)S(1)}, f32[128,128]{1,0:T(8,128)S(1)}) custom-call(bf16[64,2304]{1,0:T(8,128)(2,1)S(1)} %collective-permute-done.4.refs_0_, bf16[2304,128]{1,0:T(8,128)(2,1)S(1)} %copy-done.1, bf16[2304,128]{1,0:T(8,128)(2,1)S(1)} %copy-done.2, bf16[2304,128]{1,0:T(8,128)(2,1)S(1)} %copy-done.3, ...), custom_call_target="tpu_custom_call" | custom-call | flops 1500000000 | bytes 2000000 | tf_op jit(solution)/shard_map/pallas_call | solution.py:193
  24.2 1.2 %collective-permute-start.7 = (bf16[64,2304]{1,0:T(8,128)(2,1)S(1)}, bf16[64,2304]{1,0:T(8,128)(2,1)S(1)}, u32[]{:S(2)}, u32[]{:S(2)}) collective-permute-start(bf16[64,2304]{1,0:T(8,128)(2,1)S(1)} %get-tuple-element.36), channel_id=1, source_target_pairs={{0,12},{1,13},{2,14},{3,15},{4,0},{5,1},{6,2},{7,3},{8,4},{9,5},{1... | collective-permute-start | bytes 884744 | tf_op jit(solution)/shard_map/ppermute | solution.py:82
  25.4 0.0 collective-permute-done.3.refs_0_
  25.4 1.2 %shard_map.207 = (bf16[64,2304]{1,0:T(8,128)(2,1)S(1)}, f32[128,128]{1,0:T(8,128)S(1)}, f32[128,128]{1,0:T(8,128)S(1)}) custom-call(bf16[64,2304]{1,0:T(8,128)(2,1)S(1)} %collective-permute-done.3.refs_0_, bf16[2304,128]{1,0:T(8,128)(2,1)S(1)} %copy-done.1, bf16[2304,128]{1,0:T(8,128)(2,1)S(1)} %copy-done.2, bf16[2304,128]{1,0:T(8,128)(2,1)S(1)} %copy-done.3, ...), custom_call_target="tpu_custom_call" | custom-call | flops 1500000000 | bytes 2000000 | tf_op jit(solution)/shard_map/pallas_call | solution.py:193
  26.7 1.0 collective-permute-start.6
  27.6 1.2 %shard_map.206 = (bf16[64,2304]{1,0:T(8,128)(2,1)S(1)}, f32[128,128]{1,0:T(8,128)S(1)}, f32[128,128]{1,0:T(8,128)S(1)}) custom-call(bf16[64,2304]{1,0:T(8,128)(2,1)S(1)} %shard_map.205.refs_0_, bf16[2304,128]{1,0:T(8,128)(2,1)S(1)} %copy-done.1, bf16[2304,128]{1,0:T(8,128)(2,1)S(1)} %copy-done.2, bf16[2304,128]{1,0:T(8,128)(2,1)S(1)} %copy-done.3, ...), custom_call_target="tpu_custom_call" | custom-call | flops 1500000000 | bytes 2000000 | tf_op jit(solution)/shard_map/pallas_call | solution.py:193
  28.9 0.0 slice-start
  28.9 0.0 slice-start.2
  28.9 0.0 slice-start.4
  28.9 3.6 %shard_map.210 = f32[64,128,128]{2,1,0:T(8,128)} custom-call(f32[128,128]{1,0:T(8,128)S(1)} %get-tuple-element.25.refs_0_, f32[128,128]{1,0:T(8,128)S(1)} %get-tuple-element.26.refs_1_, f32[128,128]{1,0:T(8,128)S(1)} %get-tuple-element.27.refs_2_, f32[128,128]{1,0:T(8,128)S(1)} %get-tuple-element.28.refs_3_, f32[128,128]{1,0:T(8,128)S(1)} %get-tuple-element.29.refs_4_, ...), custom_call_target="tpu_custom_call" | custom-call | flops 9437184 | bytes 8388608 | tf_op jit(solution)/shard_map/pallas_call | solution.py:272
  32.6 0.0 collective-permute-done.8.refs_2_
  32.6 0.0 collective-permute-done.7.refs_1_
  32.6 2.1 %collective-permute-done.6.refs_0_ = bf16[64,2304]{1,0:T(8,128)(2,1)S(1)} collective-permute-done((bf16[64,2304]{1,0:T(8,128)(2,1)S(1)}, bf16[64,2304]{1,0:T(8,128)(2,1)S(1)}, u32[]{:S(2)}, u32[]{:S(2)}) %collective-permute-start.6) | collective-permute-done | bytes 294944 | tf_op jit(solution)/shard_map/ppermute | solution.py:82
  34.7 0.1 shard_map.211
  34.8 1.9 %collective-permute-start.9 = (bf16[16,2304]{1,0:T(8,128)(2,1)S(1)}, bf16[16,2304]{1,0:T(8,128)(2,1)S(1)}, u32[]{:S(2)}, u32[]{:S(2)}) collective-permute-start(bf16[16,2304]{1,0:T(8,128)(2,1)S(1)} %get-tuple-element.39), channel_id=1, source_target_pairs={{0,3},{1,0},{2,1},{3,2},{4,7},{5,4},{6,5},{7,6},{8,11},{9,8},{10,9... | collective-permute-start | bytes 221192 | tf_op jit(solution)/shard_map/ppermute | solution.py:82
  36.7 0.6 collective-permute-start.10
  37.3 1.0 collective-permute-start.11
  38.3 0.0 copy-done.14
  38.3 0.2 shard_map.204
  38.6 0.7 collective-permute-done.9.refs_1_
  39.2 3.4 %collective-permute-done.10.refs_2_ = bf16[16,2304]{1,0:T(8,128)(2,1)S(1)} collective-permute-done((bf16[16,2304]{1,0:T(8,128)(2,1)S(1)}, bf16[16,2304]{1,0:T(8,128)(2,1)S(1)}, u32[]{:S(2)}, u32[]{:S(2)}) %collective-permute-start.10) | collective-permute-done | bytes 73760 | tf_op jit(solution)/shard_map/ppermute | solution.py:82
  42.6 0.7 collective-permute-done.11.refs_3_
  43.4 0.6 shard_map.212
  44.0 26.9 %all_to_all.10.rows_ref = bf16[128,2,2304]{2,1,0:T(2,128)(2,1)S(1)} all-to-all(bf16[128,2,2304]{2,1,0:T(2,128)(2,1)S(1)} %get-tuple-element.42), channel_id=1, replica_groups=mesh['erow'=8,'ecol'=16] {'erow','ecol'}, dimensions={0} | all-to-all | bytes 2359296 | tf_op jit(solution)/shard_map/all_to_all | solution.py:469
  70.9 0.0 slice-done.4
  70.9 0.0 slice-done.1
  70.9 0.0 slice-done.3
  70.9 0.0 slice-done.5
  70.9 4.0 %shard_map.213 = bf16[128,2,2304]{2,1,0:T(2,128)(2,1)S(1)} custom-call(bf16[128,2,2304]{2,1,0:T(2,128)(2,1)S(1)} %all_to_all.10.rows_ref, bf16[2304,1024]{1,0:T(8,128)(2,1)S(1)} %bitcast.17, bf16[2304,1024]{1,0:T(8,128)(2,1)S(1)} %bitcast.20, bf16[1024,2304]{1,0:T(8,128)(2,1)S(1)} %bitcast.23), custom_call_target="tpu_custom_call" | custom-call | flops 3623878656 | bytes 16515072 | tf_op jit(solution)/shard_map/pallas_call | solution.py:366
  74.9 24.4 %all_to_all.11.rows_ref = bf16[128,2,2304]{2,1,0:T(2,128)(2,1)S(1)} all-to-all(bf16[128,2,2304]{2,1,0:T(2,128)(2,1)S(1)} %shard_map.213), channel_id=1, replica_groups=mesh['erow'=8,'ecol'=16] {'erow','ecol'}, dimensions={0} | all-to-all | bytes 2359296 | tf_op jit(solution)/shard_map/all_to_all | solution.py:473
  99.3 1.0 shard_map.214
  (21 shorter events, 0.1 us)
Async XLA Ops:
  0.6 6.5 %collective-permute-start = (bf16[4,4,2304]{2,1,0:T(4,128)(2,1)}, bf16[4,4,2304]{2,1,0:T(4,128)(2,1)S(1)}, u32[]{:S(2)}, u32[]{:S(2)}) collective-permute-start(bf16[4,4,2304]{2,1,0:T(4,128)(2,1)} %in_ref.1), channel_id=1, source_target_pairs={{0,1},{1,2},{2,3},{3,0},{4,5},{5,6},{6,7},{7,4},{8,9},{9,10},{10,1... | collective-permute-start | bytes 221192 | tf_op jit(solution)/shard_map/ppermute | solution.py:82
  2.4 4.7 %collective-permute-start.2 = (bf16[4,4,2304]{2,1,0:T(4,128)(2,1)}, bf16[4,4,2304]{2,1,0:T(4,128)(2,1)S(1)}, u32[]{:S(2)}, u32[]{:S(2)}) collective-permute-start(bf16[4,4,2304]{2,1,0:T(4,128)(2,1)} %in_ref.1), channel_id=1, source_target_pairs={{0,3},{1,0},{2,1},{3,2},{4,7},{5,4},{6,5},{7,6},{8,11},{9,8},{10,9... | collective-permute-start | bytes 221192 | tf_op jit(solution)/shard_map/ppermute | solution.py:82
  3.9 6.1 %collective-permute-start.1 = (bf16[4,4,2304]{2,1,0:T(4,128)(2,1)}, bf16[4,4,2304]{2,1,0:T(4,128)(2,1)S(1)}, u32[]{:S(2)}, u32[]{:S(2)}) collective-permute-start(bf16[4,4,2304]{2,1,0:T(4,128)(2,1)} %in_ref.1), channel_id=1, source_target_pairs={{0,2},{1,3},{2,0},{3,1},{4,6},{5,7},{6,4},{7,5},{8,10},{9,11},{10,... | collective-permute-start | bytes 221192 | tf_op jit(solution)/shard_map/ppermute | solution.py:82
  6.0 0.9 copy-start.10
  6.9 11.4 %copy-start = (f32[64,1,128,128]{3,2,1,0:T(8,128)S(1)}, f32[64,1,128,128]{3,2,1,0:T(8,128)}, u32[]{:S(2)}) copy-start(f32[64,1,128,128]{3,2,1,0:T(8,128)} %param.21) | copy-start | bytes 12582916
  6.9 11.4 %copy-start.1 = (bf16[2304,128]{1,0:T(8,128)(2,1)S(1)}, bf16[2304,128]{1,0:T(8,128)(2,1)}, u32[]{:S(2)}) copy-start(bf16[2304,128]{1,0:T(8,128)(2,1)} %refs_1_.7) | copy-start | bytes 1769476
  7.0 11.4 %copy-start.2 = (bf16[2304,128]{1,0:T(8,128)(2,1)S(1)}, bf16[2304,128]{1,0:T(8,128)(2,1)}, u32[]{:S(2)}) copy-start(bf16[2304,128]{1,0:T(8,128)(2,1)} %refs_2_.7) | copy-start | bytes 1769476
  7.0 11.4 %copy-start.3 = (bf16[2304,128]{1,0:T(8,128)(2,1)S(1)}, bf16[2304,128]{1,0:T(8,128)(2,1)}, u32[]{:S(2)}) copy-start(bf16[2304,128]{1,0:T(8,128)(2,1)} %refs_3_.7) | copy-start | bytes 1769476
  7.0 11.4 %copy-start.4 = (bf16[2304,128]{1,0:T(8,128)(2,1)S(1)}, bf16[2304,128]{1,0:T(8,128)(2,1)}, u32[]{:S(2)}) copy-start(bf16[2304,128]{1,0:T(8,128)(2,1)} %refs_8_.7) | copy-start | bytes 1769476
  7.0 11.4 %copy-start.5 = (bf16[2304,128]{1,0:T(8,128)(2,1)S(1)}, bf16[2304,128]{1,0:T(8,128)(2,1)}, u32[]{:S(2)}) copy-start(bf16[2304,128]{1,0:T(8,128)(2,1)} %refs_9_.7) | copy-start | bytes 1769476
  7.0 11.4 %copy-start.6 = (bf16[128,2304]{1,0:T(8,128)(2,1)S(1)}, bf16[128,2304]{1,0:T(8,128)(2,1)}, u32[]{:S(2)}) copy-start(bf16[128,2304]{1,0:T(8,128)(2,1)} %refs_12_.7) | copy-start | bytes 1769476
  7.0 11.4 %copy-start.7 = (bf16[128,128]{1,0:T(8,128)(2,1)S(1)}, bf16[128,128]{1,0:T(8,128)(2,1)}, u32[]{:S(2)}) copy-start(bf16[128,128]{1,0:T(8,128)(2,1)} %refs_10_.7) | copy-start | bytes 98308
  7.0 11.4 %copy-start.8 = (bf16[128,128]{1,0:T(8,128)(2,1)S(1)}, bf16[128,128]{1,0:T(8,128)(2,1)}, u32[]{:S(2)}) copy-start(bf16[128,128]{1,0:T(8,128)(2,1)} %refs_11_.7) | copy-start | bytes 98308
  7.0 11.4 %copy-start.9 = (bf16[2304,1]{0,1:T(2,128)(2,1)S(1)}, bf16[2304,1]{0,1:T(2,128)(2,1)}, u32[]{:S(2)}) copy-start(bf16[2304,1]{0,1:T(2,128)(2,1)} %param.25) | copy-start | bytes 13828
  7.1 11.4 %copy-start.11 = (f32[128]{0:T(128)S(1)}, f32[128]{0:T(128)}, u32[]{:S(2)}) copy-start(f32[128]{0:T(128)} %param.29) | copy-start | bytes 1540
  7.1 11.4 %copy-start.12 = (f32[128]{0:T(128)S(1)}, f32[128]{0:T(128)}, u32[]{:S(2)}) copy-start(f32[128]{0:T(128)} %param.32) | copy-start | bytes 1540
  10.0 8.3 %collective-permute-start.5 = (bf16[64,2304]{1,0:T(8,128)(2,1)S(1)}, bf16[64,2304]{1,0:T(8,128)(2,1)S(1)}, u32[]{:S(2)}, u32[]{:S(2)}) collective-permute-start(bf16[64,2304]{1,0:T(8,128)(2,1)S(1)} %shard_map.205.refs_0_), channel_id=1, source_target_pairs={{0,8},{1,9},{2,10},{3,11},{4,12},{5,13},{6,14},{7,15},{8,0},{9,1},... | collective-permute-start | bytes 884744 | tf_op jit(solution)/shard_map/ppermute | solution.py:82
  13.2 9.8 %collective-permute-start.4 = (bf16[64,2304]{1,0:T(8,128)(2,1)S(1)}, bf16[64,2304]{1,0:T(8,128)(2,1)S(1)}, u32[]{:S(2)}, u32[]{:S(2)}) collective-permute-start(bf16[64,2304]{1,0:T(8,128)(2,1)S(1)} %shard_map.205.refs_0_), channel_id=1, source_target_pairs={{0,4},{1,5},{2,6},{3,7},{4,8},{5,9},{6,10},{7,11},{8,12},{9,13},{1... | collective-permute-start | bytes 884744 | tf_op jit(solution)/shard_map/ppermute | solution.py:82
  13.8 11.6 %collective-permute-start.3 = (bf16[64,2304]{1,0:T(8,128)(2,1)S(1)}, bf16[64,2304]{1,0:T(8,128)(2,1)S(1)}, u32[]{:S(2)}, u32[]{:S(2)}) collective-permute-start(bf16[64,2304]{1,0:T(8,128)(2,1)S(1)} %shard_map.205.refs_0_), channel_id=1, source_target_pairs={{0,12},{1,13},{2,14},{3,15},{4,0},{5,1},{6,2},{7,3},{8,4},{9,5},{1... | collective-permute-start | bytes 884744 | tf_op jit(solution)/shard_map/ppermute | solution.py:82
  19.7 12.8 %collective-permute-start.8 = (bf16[64,2304]{1,0:T(8,128)(2,1)S(1)}, bf16[64,2304]{1,0:T(8,128)(2,1)S(1)}, u32[]{:S(2)}, u32[]{:S(2)}) collective-permute-start(bf16[64,2304]{1,0:T(8,128)(2,1)S(1)} %get-tuple-element.37), channel_id=1, source_target_pairs={{0,8},{1,9},{2,10},{3,11},{4,12},{5,13},{6,14},{7,15},{8,0},{9,1},... | collective-permute-start | bytes 884744 | tf_op jit(solution)/shard_map/ppermute | solution.py:82
  24.2 8.4 %collective-permute-start.7 = (bf16[64,2304]{1,0:T(8,128)(2,1)S(1)}, bf16[64,2304]{1,0:T(8,128)(2,1)S(1)}, u32[]{:S(2)}, u32[]{:S(2)}) collective-permute-start(bf16[64,2304]{1,0:T(8,128)(2,1)S(1)} %get-tuple-element.36), channel_id=1, source_target_pairs={{0,12},{1,13},{2,14},{3,15},{4,0},{5,1},{6,2},{7,3},{8,4},{9,5},{1... | collective-permute-start | bytes 884744 | tf_op jit(solution)/shard_map/ppermute | solution.py:82
  26.7 8.0 %collective-permute-start.6 = (bf16[64,2304]{1,0:T(8,128)(2,1)S(1)}, bf16[64,2304]{1,0:T(8,128)(2,1)S(1)}, u32[]{:S(2)}, u32[]{:S(2)}) collective-permute-start(bf16[64,2304]{1,0:T(8,128)(2,1)S(1)} %get-tuple-element.35), channel_id=1, source_target_pairs={{0,4},{1,5},{2,6},{3,7},{4,8},{5,9},{6,10},{7,11},{8,12},{9,13},{1... | collective-permute-start | bytes 884744 | tf_op jit(solution)/shard_map/ppermute | solution.py:82
  27.6 10.7 %copy-start.13 = (s32[4,4,8]{2,1,0:T(4,128)S(1)}, s32[4,4,8]{2,1,0:T(4,128)}, u32[]{:S(2)}) copy-start(s32[4,4,8]{2,1,0:T(4,128)} %ids_ref.1) | copy-start | bytes 1540
  27.6 10.7 %copy-start.14 = (f32[4,4,8]{2,1,0:T(4,128)S(1)}, f32[4,4,8]{2,1,0:T(4,128)}, u32[]{:S(2)}) copy-start(f32[4,4,8]{2,1,0:T(4,128)} %weights_ref.1) | copy-start | bytes 1540
  27.6 15.7 %copy-start.15 = (f32[2304]{0:T(1024)S(1)}, f32[2304]{0:T(1024)}, u32[]{:S(2)}) copy-start(f32[2304]{0:T(1024)} %gain_ref.1) | copy-start | bytes 27652
  28.9 42.0 %slice-start = ((s8[4718592]{0:T(1024)(128)(4,1)}), s8[4194304]{0:T(1024)(128)(4,1)S(1)}, s32[]{:S(2)}) async-start(s8[4718592]{0:T(1024)(128)(4,1)} %bitcast.15), calls=%async_computation.2 | async-start | bytes 8388608
  28.9 42.0 %slice-start.2 = ((s8[4718592]{0:T(1024)(128)(4,1)}), s8[4194304]{0:T(1024)(128)(4,1)S(1)}, s32[]{:S(2)}) async-start(s8[4718592]{0:T(1024)(128)(4,1)} %bitcast.18), calls=%async_computation.4 | async-start | bytes 8388608
  28.9 42.0 %slice-start.4 = ((s8[4718592]{0:T(1024)(128)(4,1)}), s8[4194304]{0:T(1024)(128)(4,1)S(1)}, s32[]{:S(2)}) async-start(s8[4718592]{0:T(1024)(128)(4,1)} %bitcast.21), calls=%async_computation.6 | async-start | bytes 8388608
  34.8 4.4 %collective-permute-start.9 = (bf16[16,2304]{1,0:T(8,128)(2,1)S(1)}, bf16[16,2304]{1,0:T(8,128)(2,1)S(1)}, u32[]{:S(2)}, u32[]{:S(2)}) collective-permute-start(bf16[16,2304]{1,0:T(8,128)(2,1)S(1)} %get-tuple-element.39), channel_id=1, source_target_pairs={{0,3},{1,0},{2,1},{3,2},{4,7},{5,4},{6,5},{7,6},{8,11},{9,8},{10,9... | collective-permute-start | bytes 221192 | tf_op jit(solution)/shard_map/ppermute | solution.py:82
  36.7 5.9 %collective-permute-start.10 = (bf16[16,2304]{1,0:T(8,128)(2,1)S(1)}, bf16[16,2304]{1,0:T(8,128)(2,1)S(1)}, u32[]{:S(2)}, u32[]{:S(2)}) collective-permute-start(bf16[16,2304]{1,0:T(8,128)(2,1)S(1)} %get-tuple-element.40), channel_id=1, source_target_pairs={{0,2},{1,3},{2,0},{3,1},{4,6},{5,7},{6,4},{7,5},{8,10},{9,11},{10,... | collective-permute-start | bytes 221192 | tf_op jit(solution)/shard_map/ppermute | solution.py:82
  37.3 6.0 %collective-permute-start.11 = (bf16[16,2304]{1,0:T(8,128)(2,1)S(1)}, bf16[16,2304]{1,0:T(8,128)(2,1)S(1)}, u32[]{:S(2)}, u32[]{:S(2)}) collective-permute-start(bf16[16,2304]{1,0:T(8,128)(2,1)S(1)} %get-tuple-element.41), channel_id=1, source_target_pairs={{0,1},{1,2},{2,3},{3,0},{4,5},{5,6},{6,7},{7,4},{8,9},{9,10},{10,1... | collective-permute-start | bytes 221192 | tf_op jit(solution)/shard_map/ppermute | solution.py:82
  43.4 27.5 %slice-start.1 = ((s8[4718592]{0:T(1024)(128)(4,1)}), s8[524288]{0:T(1024)(128)(4,1)S(1)}, s32[]{:S(2)}) async-start(s8[4718592]{0:T(1024)(128)(4,1)} %bitcast.15), calls=%async_computation.3 | async-start | bytes 1048576
  43.4 27.5 %slice-start.3 = ((s8[4718592]{0:T(1024)(128)(4,1)}), s8[524288]{0:T(1024)(128)(4,1)S(1)}, s32[]{:S(2)}) async-start(s8[4718592]{0:T(1024)(128)(4,1)} %bitcast.18), calls=%async_computation.5 | async-start | bytes 1048576
  43.4 27.5 %slice-start.5 = ((s8[4718592]{0:T(1024)(128)(4,1)}), s8[524288]{0:T(1024)(128)(4,1)S(1)}, s32[]{:S(2)}) async-start(s8[4718592]{0:T(1024)(128)(4,1)} %bitcast.21), calls=%async_computation.7 | async-start | bytes 1048576
